TPU v7x, 32 devices: a whole 2x2x4 slice. The times are simulated.
32 devices in a mesh: groups: 2 (over x), segment: 8 (over z, y), slab: 2 (over core).
Axes of the slice: x: 2, y: 2, z: 4, core: 2. Of those that a mesh axis runs over, the one named last changes fastest.
Arguments:
- fields: float32 [8, 3, 16, 16, 16], P('groups', None, 'slab'), parts along dimension 0, may hold values from -6 to 6
- anchors: int32 [8, 3], P('groups'), parts along dimension 0, may hold values from 0 to 4095
- lift_weight: float32 [64, 6], replicated, may hold values from -2.5 to 2.5
- conv_weight: bfloat16 [8, 3, 9, 64, 192], P('segment'), may hold values from -0.03125 to 0.03125
- conv_bias: float32 [8, 3, 64], P('segment'), may hold values from -1.25 to 1.25
- proj_weight: float32 [3, 64], replicated, may hold values from -0.75 to 0.75
Outputs:
- trajectory: float32 [2, 8, 3, 16, 16, 16], P(None, 'groups', None, 'slab', None, 'segment'), parts along dimension 1
There are 2 independent parts, one for each index of `groups`. A program takes and returns all parts, laid end to end along the dimension named above; an argument that names none is the same for every part. Nothing has to cross between parts.
All inputs are finite; a program needn't handle non-finite values.
Results may differ from a plain program's by a relative error of at most 0.028.
Values may be sent and summed in bfloat16 or wider, within the bound.
No kernel may reach another device: no remote copies, remote signals or barrier semaphores. Data moves between devices by JAX's collectives and lax.ppermute only.
A program may use at most 64 MiB of HBM per device.

v0:
```python
import functools

import jax
import jax.numpy as jnp
from jax import lax
from jax.experimental import pallas as pl
from jax.experimental.pallas import tpu as pltpu
from jax.sharding import PartitionSpec as P

STEPS = 2
FIELD = 4096
LAYERS = 3
CH = 64
ROWS = 896
VMEM_BYTES = 48 * 1024 * 1024

MOVES = (
    [(4 * b + m, 4 * b + 2 + m, 4 * m + b, 4 * m + 2 + b) for b in range(2) for m in range(2)],
    [(2 * m, 2 * m + 1, m, 4 + m) for m in range(4)],
    [(4 * p + 2 * m, 4 * p + 2 * m + 1, 2 * p + m, 2 * (2 + p) + m) for p in range(2) for m in range(2)],
)
CYCLES = (
    [list(range(8))],
    [list(range(4)), list(range(4, 8))],
    [[2 * r, 2 * r + 1] for r in range(4)],
)


GROUPS = ((0,), (1,), (2,), (3,))


def neighbour(layer, tile, step):
    cycle = next(cycle for cycle in CYCLES[layer] if tile in cycle)
    return cycle[(cycle.index(tile) + step) % len(cycle)]


def low_lanes(shape):
    return lax.broadcasted_iota(jnp.int32, shape, len(shape) - 1) < CH


def nt_dot(a, b):
    return lax.dot_general(a, b, (((1,), (1,)), ((), ())), preferred_element_type=jnp.float32)


def pack_kernel(raw_ref, bias_ref, eye_ref, packed):
    eye = eye_ref[...]
    low = low_lanes((CH, 128))
    for layer in range(LAYERS):
        for ty in range(3):
            pair = jnp.concatenate([raw_ref[layer, 3 + ty], raw_ref[layer, ty]], axis=0)
            packed[layer, ty * 192 : (ty + 1) * 192, :] = nt_dot(eye, pair).astype(jnp.bfloat16)
        pair = jnp.concatenate([raw_ref[layer, 6], raw_ref[layer, 7]], axis=0)
        packed[layer, 576:768, :] = nt_dot(eye, pair).astype(jnp.bfloat16)
        pair = jnp.concatenate([raw_ref[layer, 8], raw_ref[layer, 8]], axis=0)
        twice = nt_dot(eye, pair)
        packed[layer, 768:832, :] = jnp.where(low, twice[0:64], twice[64:128]).astype(jnp.bfloat16)
        terms = [term.astype(jnp.float32) for term in split_terms(bias_ref[layer : layer + 1, :])]
        terms = jnp.concatenate(terms + [jnp.zeros((CH - 3, CH), jnp.float32)], axis=0)
        terms = jnp.concatenate([terms, terms], axis=1)
        packed[layer, 832:896, :] = jnp.where(low, twice[128:192], terms).astype(jnp.bfloat16)


def pair_forms(taps):
    before, here, behind = taps
    ends = 0.25 * (before + behind)
    here = 0.25 * here
    return 0.5 * before, ends + here, ends - here, 0.5 * behind


def cycle_forms(taps):
    before, here, behind = taps
    ends = 0.125 * (before + behind)
    near = 0.125 * here
    return near + ends, near - ends, 0.25 * here, 0.25 * (behind - before)


def expand(packed, w_ref, bias_ref, layer):
    low = low_lanes((192, 128))
    zero = jnp.zeros((192, 128), jnp.float32)
    forms = pair_forms if layer < 2 else cycle_forms
    mids = forms([packed[ty * 192 : (ty + 1) * 192, :].astype(jnp.float32) for ty in range(3)])
    both = packed[576:768, :].astype(jnp.float32)
    ends = packed[768:832, :].astype(jnp.float32)
    rest = packed[832:896, :].astype(jnp.float32)
    ends = jnp.concatenate([ends, pltpu.roll(ends, CH, 1), rest], axis=0)
    lasts = forms([both, pltpu.roll(both, CH, 1), ends])
    for index, (mid, last) in enumerate(zip(mids, lasts)):
        rolled = pltpu.roll(mid, CH, 1)
        blocks = (
            mid,
            jnp.where(low, last, rolled),
            jnp.where(low, zero, pltpu.roll(last, CH, 1)),
            jnp.where(low, rolled, zero),
        )
        blocks = [block.astype(jnp.bfloat16) for block in blocks]
        for tz in range(3):
            for a in range(4):
                if layer < 2:
                    w_ref[index, a * CH : (a + 1) * CH, tz * 128 : (tz + 1) * 128] = blocks[a][tz * CH : (tz + 1) * CH]
                else:
                    row = index * 256 + a * CH
                    for half in range(2):
                        chosen = blocks[((0, 2), (1, 3), (2, 0), (3, 1))[a][half]]
                        column = tz * 256 + half * 128
                        w_ref[row : row + CH, column : column + 128] = chosen[tz * CH : (tz + 1) * CH]
    bias = 0.5 * (rest[0:1] + rest[1:2] + rest[2:3])
    bias = jnp.where(low_lanes((1, 128)), pltpu.roll(bias, CH, 1), bias)
    bias_ref[...] = jnp.broadcast_to(bias, (8, 128))


def z_moved(values, tap, layer):
    even, odd = values[:, :8], values[:, 8:]
    if layer > 0:
        shift = -tap * 2 ** (layer - 1) % 8
        return pltpu.roll(even, shift, 1), pltpu.roll(odd, shift, 1)
    if tap > 0:
        return odd, pltpu.roll(even, 7, 1)
    return pltpu.roll(odd, 1, 1), even


def z_summed(products, width, layer):
    products = products.reshape(products.shape[0] // 16, 16, products.shape[1])
    here = products[:, :, width : 2 * width]
    before = z_moved(products[:, :, :width], -1, layer)
    behind = z_moved(products[:, :, 2 * width :], 1, layer)
    parts = [here[:, 8 * i : 8 * i + 8] + before[i] + behind[i] for i in range(2)]
    return jnp.concatenate(parts, axis=1)


def activate_into(v_ref, tile, value, layer):
    activated = value * jnp.tanh(value) + value
    if layer < 2:
        d = 2**layer
        pairs = activated.reshape(8 // d, 2, d, 16, 128)
        first, second = pairs[:, 0], pairs[:, 1]
        before = jnp.concatenate([second[-1:], second[:-1]], axis=0)
        behind = jnp.concatenate([first[1:], first[:1]], axis=0)
        mixed = (before - second, first + second, second - first, first - behind)
    else:
        cycle = activated.reshape(4, 4, 16, 128)
        even, odd = cycle[0] + cycle[2], cycle[1] + cycle[3]
        sine = cycle[3] - cycle[1]
        mixed = (even + odd, even - odd, cycle[0] - cycle[2], sine, -sine)
    for index, value in enumerate(mixed):
        v_ref[index, tile] = value.reshape(-1, 128).astype(jnp.bfloat16)


def spread(move, u, v, state_out, v_ref, layer):
    low = low_lanes((16, 16, 128))
    for at, value in (
        (move[2], jnp.where(low, u, pltpu.roll(v, CH, 2))),
        (move[3], jnp.where(low, pltpu.roll(u, CH, 2), v)),
    ):
        state_out[at] = value
        activate_into(v_ref, at, value, layer)


def convolve_pairs(v_ref, w_ref, tiles, layer):
    d = 2**layer
    low = low_lanes((128, 128))
    sums = []
    for index in range(4):
        rows = []
        for tile in tiles:
            after = v_ref[index, neighbour(layer, tile, 1)]
            before = v_ref[index, neighbour(layer, tile, -1)]
            rows.append(jnp.concatenate([v_ref[index, tile], jnp.where(low, after, before)], axis=1))
        rows = jnp.concatenate(rows, axis=0)
        sums.append(z_summed(jnp.dot(rows, w_ref[index], preferred_element_type=jnp.float32), 128, layer))
    first = sums[0] + sums[1] + sums[2]
    second = sums[1] - sums[2] - sums[3]
    results = []
    for at in range(len(tiles)):
        halves = [half[at * 8 : (at + 1) * 8].reshape(8 // d, 1, d, 16, 128) for half in (first, second)]
        results.append(jnp.concatenate(halves, axis=1).reshape(16, 16, 128))
    return results


def convolve_cycles(v_ref, w_ref, units, layer):
    def rows(*forms):
        parts = [jnp.concatenate([v_ref[form, 2 * r + m] for form in forms for m in range(2)], axis=1) for r in units]
        return jnp.concatenate(parts, axis=0)

    def summed(lhs, begin, end):
        return z_summed(jnp.dot(lhs, w_ref[begin:end, :], preferred_element_type=jnp.float32), 256, layer)

    flat = summed(rows(0), 0, 256)
    alternate = summed(rows(1), 256, 512)
    waves = summed(jnp.concatenate([rows(2, 4), rows(3, 2)], axis=0), 512, 1024)
    count = 4 * len(units)
    cosine, sine = waves[:count], waves[count:]
    even, odd = flat + alternate, flat - alternate
    cells = [value.reshape(len(units), 1, 4, 16, 256) for value in (even + cosine, odd - sine, even - cosine, odd + sine)]
    cells = jnp.concatenate(cells, axis=1).reshape(len(units), 16, 16, 256)
    return [cells[at, :, :, m * 128 : m * 128 + 128] for at in range(len(units)) for m in range(2)]


def begin_section(state, v_refs):
    for move in MOVES[0]:
        spread(move, state[0][move[0]], state[0][move[1]], state[1], v_refs[0], 0)


def run_section(state, v_refs, w_refs, bias_refs, prepare):
    s_a, *held_in = state
    begin_section(state, v_refs)
    prepare(0)
    for layer in range(LAYERS):
        held, following = held_in[layer], held_in[(layer + 1) % LAYERS]
        if layer + 1 < LAYERS:
            prepare(layer + 1)
        bias = bias_refs[layer][0:1][None]
        if layer == LAYERS - 1:
            for tile, total in enumerate(convolve_cycles(v_refs[2], w_refs[layer], range(4), layer)):
                s_a[tile] = (held[tile] + bias + total).astype(jnp.bfloat16).astype(jnp.float32)
            break
        for chosen in GROUPS:
            moves = [MOVES[layer + 1][at] for at in chosen]
            tiles = [tile for move in moves for tile in move[:2]]
            sums = convolve_pairs(v_refs[layer], w_refs[layer], tiles, layer)
            sums = [held[tile] + bias + total for tile, total in zip(tiles, sums)]
            for at, move in enumerate(moves):
                spread(move, sums[2 * at], sums[2 * at + 1], following, v_refs[layer + 1], layer + 1)


def by_parity(x):
    row = lax.broadcasted_iota(jnp.int32, (128, 128), 0)
    lane = lax.broadcasted_iota(jnp.int32, (128, 128), 1)
    place = (row & 112) | ((row & 1) << 3) | ((row >> 1) & 7)
    turned = jnp.where(place == lane, 1.0, 0.0).astype(jnp.bfloat16)
    blocks = jnp.concatenate([x[:, at * 128 : (at + 1) * 128] for at in range(16)], axis=0)
    moved = sum(jnp.dot(term, turned, preferred_element_type=jnp.float32) for term in split_terms(blocks))
    return jnp.concatenate([moved[at * 16 : (at + 1) * 16] for at in range(16)], axis=1)


def lift_into(x, lift_ref, s_a):
    high = x.astype(jnp.bfloat16).astype(jnp.float32)
    columns = jnp.concatenate([high, x - high, high], axis=0).T.astype(jnp.bfloat16)
    hidden = jnp.dot(columns, lift_ref[...], preferred_element_type=jnp.float32)
    s_a[...] = hidden.astype(jnp.bfloat16).astype(jnp.float32).reshape(8, 16, 16, 128)


def renewed_fields(x, proj_ref, s_a):
    gain = nt_dot(proj_ref[...], s_a[...].reshape(2048, 128).astype(jnp.bfloat16))
    return x + gain[:16] + gain[16:32] + gain[32:48]


def level_kernel(level, first, last, *refs):
    (ids_ref, own_0, own_1, far_0, far_1, x_ref, lift_ref, proj_ref) = refs[:8]
    (w_out, c_out, b_out, leaving, x_out, s_a, s_b, s_c, s_d, v_a, v_b, v_c) = refs[-17:-5]
    (packed, w_pair, w_cycle, b_all, sems) = refs[-5:]
    slab, line = ids_ref[0], ids_ref[1]
    x = by_parity(x_ref[...]) if first else x_ref[...]
    if first:
        lift_into(x, lift_ref, s_a)
    else:
        s_a[...] = refs[8][...].astype(jnp.float32)
    state, v_refs = (s_a, s_b, s_c, s_d), (v_a, v_b, v_c)

    def copies(turn):
        at = 2 * level + turn
        pairs = [pltpu.make_async_copy(w_pair.at[turn, i], w_out.at[at, i], sems.at[turn, i]) for i in range(2)]
        cycle = pltpu.make_async_copy(w_cycle.at[turn], c_out.at[at], sems.at[turn, 2])
        return pairs + [cycle, pltpu.make_async_copy(b_all.at[turn], b_out.at[at], sems.at[turn, 3])]

    def section(turn, unused):
        for wanted, sources in ((True, (own_0, own_1)), (False, (far_0, far_1))):
            for core, source in enumerate(sources):

                @pl.when(((turn == line) == wanted) & (slab == core))
                def take(source=source):
                    packed[...] = source[...]

        w_refs = [w_pair.at[turn, 0], w_pair.at[turn, 1], w_cycle.at[turn]]

        def prepare(layer):
            expand(packed.at[layer], w_refs[layer], b_all.at[turn, layer], layer)
            copies(turn)[layer].start()

        run_section(state, v_refs, w_refs, [b_all.at[turn, i] for i in range(LAYERS)], prepare)
        copies(turn)[LAYERS].start()
        return 0

    lax.fori_loop(0, 2, section, 0)
    leaving[...] = s_a[...].astype(jnp.bfloat16)
    x_out[...] = renewed_fields(x, proj_ref, s_a) if last else x
    for turn in range(2):
        for copy in copies(turn):
            copy.wait()


def feature_kernel(ids_ref, anchor_ref, kept_ref, got_ref, lift_ref, proj_ref, x_ref, lift_out, proj_out):
    slab, slot = ids_ref[0], ids_ref[2]
    kept, got = kept_ref[slot], got_ref[slot]
    halves = (jnp.where(slab == 0, kept, got), jnp.where(slab == 0, got, kept))
    columns = []
    for r in range(4):
        for m in range(2):
            columns.append(jnp.concatenate([halves[m][:, r], halves[m][:, 4 + r]], axis=0))
    current = jnp.concatenate([jnp.concatenate(columns, axis=1), jnp.zeros((10, 2048), jnp.float32)], axis=0)
    row = lax.broadcasted_iota(jnp.int32, (16, 2048), 0)
    column = lax.broadcasted_iota(jnp.int32, (16, 2048), 1)
    along_x = ((column >> 8) & 1) * 8 + (column >> 9) + jnp.where(row >= 9, 4, 0)
    along_x = along_x + anchor_ref[slot, 0]
    along_y = ((column >> 4) & 15) + anchor_ref[slot, 1]
    along_z = (column & 15) + anchor_ref[slot, 2]
    axis = jnp.where(row >= 9, row - 9, row - 6)
    position = jnp.where(axis == 0, along_x, jnp.where(axis == 1, along_y, along_z)) & (FIELD - 1)
    waves = jnp.sin(2.0 * jnp.pi * position.astype(jnp.float32) / FIELD)
    x_ref[...] = jnp.where(row < 6, current, jnp.where(row < 12, waves, 0.0))

    def two_halves(part):
        blank = jnp.zeros(part.shape, jnp.float32)
        return [jnp.concatenate([part, blank], axis=1), jnp.concatenate([blank, part], axis=1)]

    lift = 0.5 * lift_ref[...]
    lift = two_halves(lift[0:3]) + two_halves(lift[3:6]) + [jnp.zeros((4, 128), jnp.float32)]
    first, second, unused = [term.astype(jnp.float32) for term in split_terms(jnp.concatenate(lift, axis=0))]
    lift_out[...] = jnp.concatenate([first, first, second], axis=0).astype(jnp.bfloat16)
    proj = two_halves(2.0 * proj_ref[...]) + [jnp.zeros((10, 128), jnp.float32)]
    proj = [term.astype(jnp.float32) for term in split_terms(jnp.concatenate(proj, axis=0))]
    proj_out[...] = jnp.concatenate(proj, axis=0).astype(jnp.bfloat16)


def cells_in_rows(both, half):
    blocks = []
    for x_ref in both:
        for r in range(4):
            for upper in range(2):
                begin = pl.multiple_of(((2 * r + half) * 2 + upper) * 128, 128)
                blocks.append(x_ref[0:8, pl.ds(begin, 128)])
    row = lax.broadcasted_iota(jnp.int32, (128, 128), 0)
    lane = lax.broadcasted_iota(jnp.int32, (128, 128), 1)
    z = ((lane & 7) << 1) | ((lane >> 3) & 1)
    turned = ((row >> 3) == z) & ((row & 7) == (lane >> 4))
    turned = jnp.where(turned, 1.0, 0.0).astype(jnp.bfloat16)
    return nt_dot(turned, jnp.concatenate(blocks, axis=0).astype(jnp.bfloat16)).astype(jnp.bfloat16)


def second_kernel(ids_ref, x_ref, lift_ref, proj_ref, w_ref, c_ref, b_ref, kept, given, s_a, s_b, s_c, s_d, v_a, v_b, v_c, x_new):
    s = pl.program_id(0)

    state, v_refs = (s_a, s_b, s_c, s_d), (v_a, v_b, v_c)

    @pl.when(s == 0)
    def begin():
        lift_into(x_ref[...], lift_ref, s_a)

    w_refs = [w_ref.at[0, 0], w_ref.at[0, 1], c_ref.at[0]]
    run_section(state, v_refs, w_refs, [b_ref.at[0, i] for i in range(LAYERS)], lambda layer: None)

    @pl.when(s == pl.num_programs(0) - 1)
    def finish():
        x_new[...] = renewed_fields(x_ref[...], proj_ref, s_a)
        kept[...] = cells_in_rows((x_ref, x_new), ids_ref[0])
        given[...] = cells_in_rows((x_ref, x_new), 1 - ids_ref[0])


def split_terms(matrix):
    first = matrix.astype(jnp.bfloat16)
    rest = matrix - first.astype(jnp.float32)
    second = rest.astype(jnp.bfloat16)
    third = (rest - second.astype(jnp.float32)).astype(jnp.bfloat16)
    return first, second, third


def state_scratch():
    return (
        [pltpu.VMEM((8, 16, 16, 128), jnp.float32)] * 4
        + [pltpu.VMEM((4, 8, 128, 128), jnp.bfloat16)] * 2
        + [pltpu.VMEM((5, 8, 64, 128), jnp.bfloat16)]
    )


def shards(fields, anchors, lift_weight, conv_weight, conv_bias, proj_weight):
    segments = lax.axis_size("segment")
    slabs = lax.axis_size("slab")
    segment_id = lax.axis_index("segment")
    slab_id = lax.axis_index("slab")
    crop_count, comps, slab_rows, y_cells, z_cells = fields.shape
    lines = crop_count // slabs
    levels = segments // lines
    line = segment_id % lines
    slot = line * slabs + slab_id
    swap = [(0, 1), (1, 0)]
    vmem = pl.BlockSpec(memory_space=pltpu.VMEM)
    smem = pl.BlockSpec(memory_space=pltpu.SMEM)
    anyspace = pl.BlockSpec(memory_space=pl.ANY)
    params = pltpu.CompilerParams(vmem_limit_bytes=VMEM_BYTES)
    ids = jnp.stack([slab_id, line, slot]).astype(jnp.int32)

    def after(value, earlier):
        return lax.optimization_barrier((value, earlier))[0]

    def between_cores(value):
        return lax.ppermute(value, "slab", swap)

    packed = pl.pallas_call(
        pack_kernel,
        out_shape=jax.ShapeDtypeStruct((LAYERS, ROWS, 128), jnp.bfloat16),
        in_specs=[vmem] * 3,
        out_specs=vmem,
        compiler_params=params,
    )(conv_weight[0], conv_bias[0], jnp.eye(192, dtype=jnp.bfloat16))

    flat = after(fields, packed).reshape(crop_count, comps, slab_rows, y_cells * z_cells)
    x, lift, proj = pl.pallas_call(
        feature_kernel,
        out_shape=(
            jax.ShapeDtypeStruct((16, 2048), jnp.float32),
            jax.ShapeDtypeStruct((48, 128), jnp.bfloat16),
            jax.ShapeDtypeStruct((48, 128), jnp.bfloat16),
        ),
        in_specs=[smem, smem] + [vmem] * 4,
        out_specs=(vmem, vmem, vmem),
        compiler_params=params,
    )(ids, anchors, flat, between_cores(flat), lift_weight.T, proj_weight)

    w_shape = jax.ShapeDtypeStruct((segments, 2, 4, 256, 384), jnp.bfloat16)
    c_shape = jax.ShapeDtypeStruct((segments, 1024, 768), jnp.bfloat16)
    b_shape = jax.ShapeDtypeStruct((segments, LAYERS, 8, 128), jnp.float32)
    h_shape = jax.ShapeDtypeStruct((8, 16, 16, 128), jnp.bfloat16)
    x_shape = jax.ShapeDtypeStruct((16, 2048), jnp.float32)
    layer_flops = 2 * 4 * 1024 * 256 * 512
    def hand_on(value, level):
        pairs = [(s * slabs, (s - lines) * slabs) for s in range(lines, segments - lines * level)]
        pairs += [(0, slabs + 1), (slabs, 1)]
        return lax.ppermute(value, ("segment", "slab"), pairs)

    arrived = {0: after(hand_on(packed, 0), x)}
    swapped = {0: between_cores(arrived[0])}
    arrived[1] = hand_on(arrived[0], 1)
    kept = ()
    current = x
    for level in range(levels):
        own = (packed, packed) if level == 0 else (arrived[level - 1], swapped[level - 1])
        operands = (ids, *own, swapped[level], arrived[level], current, lift, proj, *kept)
        weights, cycles, rows, hidden, current = pl.pallas_call(
            functools.partial(level_kernel, level, level == 0, level == levels - 1),
            out_shape=(w_shape, c_shape, b_shape, h_shape, x_shape),
            in_specs=[smem] + [vmem] * 7 + ([vmem] + [anyspace] * 3 if kept else []),
            out_specs=(anyspace, anyspace, anyspace, vmem, vmem),
            scratch_shapes=state_scratch()
            + [
                pltpu.VMEM((LAYERS, ROWS, 128), jnp.bfloat16),
                pltpu.VMEM((2, 2, 4, 256, 384), jnp.bfloat16),
                pltpu.VMEM((2, 1024, 768), jnp.bfloat16),
                pltpu.VMEM((2, LAYERS, 8, 128), jnp.float32),
                pltpu.SemaphoreType.DMA((2, LAYERS + 1)),
            ],
            input_output_aliases={9: 0, 10: 1, 11: 2} if kept else {},
            compiler_params=params,
            cost_estimate=pl.CostEstimate(flops=2 * LAYERS * layer_flops, bytes_accessed=4 << 20, transcendentals=0),
        )(*operands)
        kept = (hidden, weights, cycles, rows)
        if level + 1 < levels:
            arrived[level + 1] = after(arrived[level + 1], hidden)
            swapped[level + 1] = between_cores(arrived[level + 1])
            if level + 2 < levels:
                arrived[level + 2] = hand_on(arrived[level + 1], level + 2)
    first_result = current
    kept, given = pl.pallas_call(
        second_kernel,
        grid=(segments,),
        out_shape=(jax.ShapeDtypeStruct((128, 128), jnp.bfloat16),) * 2,
        in_specs=[smem]
        + [vmem] * 3
        + [
            pl.BlockSpec((1, 2, 4, 256, 384), lambda s: (s, 0, 0, 0, 0)),
            pl.BlockSpec((1, 1024, 768), lambda s: (s, 0, 0)),
            pl.BlockSpec((1, LAYERS, 8, 128), lambda s: (s, 0, 0, 0)),
        ],
        out_specs=(vmem, vmem),
        scratch_shapes=state_scratch() + [pltpu.VMEM((16, 2048), jnp.float32)],
        compiler_params=params,
        cost_estimate=pl.CostEstimate(flops=segments * LAYERS * layer_flops, bytes_accessed=16 << 20, transcendentals=0),
    )(ids, first_result, lift, proj, weights, cycles, rows)

    share = z_cells // segments
    got = between_cores(given)
    pair = jnp.where(slab_id == 0, jnp.stack([kept, got]), jnp.stack([got, kept]))
    pair = pair.reshape(slabs, levels, lines, share * 8, 128)
    mine = lax.dynamic_index_in_dim(pair, line, 2, keepdims=False)
    got = lax.ppermute(lax.dynamic_index_in_dim(pair, 1 - line, 2, keepdims=False), "segment", swap)
    crops = jnp.where(line == 0, jnp.concatenate([mine, got]), jnp.concatenate([got, mine]))
    out = jnp.where(segment_id < lines, crops[:, 0], 0)
    for level in range(1, levels):
        pairs = [(s, level * lines + s) for s in range(lines)]
        out = out + lax.ppermute(crops[:, level], "segment", pairs)
    out = out.reshape(crop_count, share, 8, STEPS, 4, 2, 8)[..., : 2 * comps]
    out = out.reshape(crop_count, share, 8, STEPS, 4, 2, 2, comps).transpose(3, 0, 7, 6, 4, 5, 2, 1)
    return out.reshape(STEPS, crop_count, comps, slab_rows, y_cells, share).astype(jnp.float32)


def solution(mesh):
    in_specs = (
        P("groups", None, "slab", None, None),
        P("groups", None),
        P(),
        P("segment", None, None, None, None),
        P("segment", None, None),
        P(),
    )
    out_specs = P(None, "groups", None, "slab", None, "segment")
    return jax.shard_map(shards, mesh=mesh, in_specs=in_specs, out_specs=out_specs, check_vma=False)
```

profile of v0, /device:TPU:0, one launch (start us, length us, event | category | flops | bytes accessed | tf_op | source)
XLA Modules:
  0.0 121.6 jit_solution(3298211415696789023)
XLA Ops:
  0.0 0.7 copy.47
  0.7 1.2 copy-done
  1.9 0.5 shard_map.64.refs_1_.refs_2_
  2.4 4.3 %collective-permute-start = (bf16[3,896,128]{2,1,0:T(8,128)(2,1)S(1)}, bf16[3,896,128]{2,1,0:T(8,128)(2,1)S(1)}, u32[]{:S(2)}, u32[]{:S(2)}) collective-permute-start(bf16[3,896,128]{2,1,0:T(8,128)(2,1)S(1)} %shard_map.64.refs_1_.refs_2_), channel_id=1, source_target_pairs={{4,0},{6,2},{8,4},{10,6},{12,8},{14,10},{0,3},{2,1},{20,16},{22,18... | collective-permute-start | bytes 2064392 | tf_op jit(solution)/shard_map/ppermute | solution.py:427
  6.8 1.4 %reshape.24.kept_ref = f32[4,3,8,256]{3,2,1,0:T(8,128)S(1)} reshape(f32[4,3,8,16,16]{4,3,2,1,0:T(8,128)} %param.6) | data formatting | bytes 196608 | tf_op jit(solution)/shard_map/reshape | solution.py:405
  8.4 1.2 collective-permute-done.1.got_ref
  9.6 0.7 copy-done.1
  10.2 0.7 copy-done.2
  10.9 0.7 copy-done.3
  11.6 1.1 shard_map.65
  12.7 3.6 %collective-permute-done.refs_4_.refs_1_ = bf16[3,896,128]{2,1,0:T(8,128)(2,1)S(1)} collective-permute-done((bf16[3,896,128]{2,1,0:T(8,128)(2,1)S(1)}, bf16[3,896,128]{2,1,0:T(8,128)(2,1)S(1)}, u32[]{:S(2)}, u32[]{:S(2)}) %collective-permute-start) | collective-permute-done | bytes 688160 | tf_op jit(solution)/shard_map/ppermute | solution.py:427
  16.3 3.9 %collective-permute-start.2 = (bf16[3,896,128]{2,1,0:T(8,128)(2,1)S(1)}, bf16[3,896,128]{2,1,0:T(8,128)(2,1)S(1)}, u32[]{:S(2)}, u32[]{:S(2)}) collective-permute-start(bf16[3,896,128]{2,1,0:T(8,128)(2,1)S(1)} %collective-permute-done.refs_4_.refs_1_), channel_id=1, source_target_pairs={{4,0},{6,2},{8,4},{10,6},{0,3},{2,1},{20,16},{22,18},{24,20},{26,2... | collective-permute-start | bytes 2064392 | tf_op jit(solution)/shard_map/ppermute | solution.py:427
  20.3 11.0 %shard_map.66 = (bf16[8,2,4,256,384]{4,3,2,1,0:T(8,128)(2,1)}, bf16[8,1024,768]{2,1,0:T(8,128)(2,1)}, f32[8,3,8,128]{3,2,1,0:T(8,128)S(1)}, bf16[8,16,16,128]{3,2,1,0:T(8,128)(2,1)S(1)}, f32[16,2048]{1,0:T(8,128)S(1)}) custom-call(s32[3]{0:T(128)S(1)} %pad_add_fusion.ids_ref.refs_0_, bf16[3,896,128]{2,1,0:T(8,128)(2,1)S(1)} %shard_map.64.refs_1_.refs_2_, ...), custom_call_target="tpu_custom_call" | custom-call | flops 6442450944 | bytes 4194304 | tf_op jit(solution)/shard_map/pallas_call | solution.py:437
  31.4 2.3 %collective-permute-start.4 = (bf16[3,896,128]{2,1,0:T(8,128)(2,1)S(1)}, bf16[3,896,128]{2,1,0:T(8,128)(2,1)S(1)}, u32[]{:S(2)}, u32[]{:S(2)}) collective-permute-start(bf16[3,896,128]{2,1,0:T(8,128)(2,1)S(1)} %collective-permute-done.2.refs_4_.refs_1_), channel_id=1, source_target_pairs={{4,0},{6,2},{0,3},{2,1},{20,16},{22,18},{16,19},{18,17}} | collective-permute-start | bytes 2064392 | tf_op jit(solution)/shard_map/ppermute | solution.py:427
  33.7 10.5 %shard_map.67 = (bf16[8,2,4,256,384]{4,3,2,1,0:T(8,128)(2,1)}, bf16[8,1024,768]{2,1,0:T(8,128)(2,1)}, f32[8,3,8,128]{3,2,1,0:T(8,128)S(1)}, bf16[8,16,16,128]{3,2,1,0:T(8,128)(2,1)S(1)}, f32[16,2048]{1,0:T(8,128)S(1)}) custom-call(s32[3]{0:T(128)S(1)} %pad_add_fusion.ids_ref.refs_0_, ...), custom_call_target="tpu_custom_call", output_to_operand_aliasing={{0}: (9, {}), {1}: (10, {}), {2}: (11, {})} | custom-call | flops 6442450944 | bytes 4194304 | tf_op jit(solution)/shard_map/pallas_call | solution.py:437
  44.3 4.1 %collective-permute-start.7 = (bf16[3,896,128]{2,1,0:T(8,128)(2,1)S(1)}, bf16[3,896,128]{2,1,0:T(8,128)(2,1)S(1)}, u32[]{:S(2)}, u32[]{:S(2)}) collective-permute-start(bf16[3,896,128]{2,1,0:T(8,128)(2,1)S(1)} %collective-permute-done.4.refs_4_.refs_1_), channel_id=1, source_target_pairs={{0,3},{2,1},{16,19},{18,17}} | collective-permute-start | bytes 2064392 | tf_op jit(solution)/shard_map/ppermute | solution.py:427
  48.5 10.5 %shard_map.68 = (bf16[8,2,4,256,384]{4,3,2,1,0:T(8,128)(2,1)}, bf16[8,1024,768]{2,1,0:T(8,128)(2,1)}, f32[8,3,8,128]{3,2,1,0:T(8,128)S(1)}, bf16[8,16,16,128]{3,2,1,0:T(8,128)(2,1)S(1)}, f32[16,2048]{1,0:T(8,128)S(1)}) custom-call(s32[3]{0:T(128)S(1)} %pad_add_fusion.ids_ref.refs_0_, ...), custom_call_target="tpu_custom_call", output_to_operand_aliasing={{0}: (9, {}), {1}: (10, {}), {2}: (11, {})} | custom-call | flops 6442450944 | bytes 4194304 | tf_op jit(solution)/shard_map/pallas_call | solution.py:437
  59.0 2.1 %collective-permute-done.8.refs_3_ = bf16[3,896,128]{2,1,0:T(8,128)(2,1)S(1)} collective-permute-done((bf16[3,896,128]{2,1,0:T(8,128)(2,1)S(1)}, bf16[3,896,128]{2,1,0:T(8,128)(2,1)S(1)}, u32[]{:S(2)}, u32[]{:S(2)}) %collective-permute-start.8) | collective-permute-done | bytes 688160 | tf_op jit(solution)/shard_map/ppermute | solution.py:395
  61.2 11.4 %shard_map.69 = (bf16[8,2,4,256,384]{4,3,2,1,0:T(8,128)(2,1)}, bf16[8,1024,768]{2,1,0:T(8,128)(2,1)}, f32[8,3,8,128]{3,2,1,0:T(8,128)S(1)}, bf16[8,16,16,128]{3,2,1,0:T(8,128)(2,1)}, f32[16,2048]{1,0:T(8,128)S(1)}) custom-call(s32[3]{0:T(128)S(1)} %pad_add_fusion.ids_ref.refs_0_, ...), custom_call_target="tpu_custom_call", output_to_operand_aliasing={{0}: (9, {}), {1}: (10, {}), {2}: (11, {})} | custom-call | flops 6442450944 | bytes 4194304 | tf_op jit(solution)/shard_map/pallas_call | solution.py:437
  72.6 33.8 %shard_map.70 = (bf16[128,128]{1,0:T(8,128)(2,1)S(1)}, bf16[128,128]{1,0:T(8,128)(2,1)S(1)}) custom-call(s32[3]{0:T(128)S(1)} %pad_add_fusion.ids_ref.refs_0_, f32[16,2048]{1,0:T(8,128)S(1)} %get-tuple-element.57.x_ref, bf16[48,128]{1,0:T(8,128)(2,1)S(1)} %get-tuple-element.37.refs_6_.lift_ref, bf16[48,128]{1,0:T(8,128)(2,1)S(1)} %get-tuple-element.38.refs_7_.proj_ref, ...), custom_call_target="tpu_custom_call" | custom-call | flops 25769803776 | bytes 16777216 | tf_op jit(solution)/shard_map/pallas_call | solution.py:461
  106.4 0.2 collective-permute-start.9
  106.6 1.1 collective-permute-done.9
  107.7 2.0 %collective-permute-start.10 = (bf16[2,4,16,128]{3,2,1,0:T(8,128)(2,1)S(1)}, bf16[2,4,16,128]{3,2,1,0:T(8,128)(2,1)S(1)}, u32[]{:S(2)}, u32[]{:S(2)}) collective-permute-start(bf16[2,4,16,128]{3,2,1,0:T(8,128)(2,1)S(1)} %get-tuple-element.67), channel_id=1, source_target_pairs={{0,2},{2,0},{1,3},{3,1},{16,18},{18,16},{17,19},{19,17}} | collective-permute-start | bytes 98312 | tf_op jit(solution)/shard_map/ppermute | solution.py:483
  109.7 3.8 %collective-permute-done.10 = bf16[2,4,16,128]{3,2,1,0:T(8,128)(2,1)S(1)} collective-permute-done((bf16[2,4,16,128]{3,2,1,0:T(8,128)(2,1)S(1)}, bf16[2,4,16,128]{3,2,1,0:T(8,128)(2,1)S(1)}, u32[]{:S(2)}, u32[]{:S(2)}) %collective-permute-start.10) | collective-permute-done | bytes 32800 | tf_op jit(solution)/shard_map/ppermute | solution.py:483
  113.6 1.3 %collective-permute-start.11 = (bf16[4,16,128]{2,1,0:T(8,128)(2,1)S(1)}, bf16[4,16,128]{2,1,0:T(8,128)(2,1)S(1)}, u32[]{:S(2)}, u32[]{:S(2)}) collective-permute-start(bf16[4,16,128]{2,1,0:T(8,128)(2,1)S(1)} %get-tuple-element.63), channel_id=1, source_target_pairs={{0,4},{2,6},{1,5},{3,7},{16,20},{18,22},{17,21},{19,23}} | collective-permute-start | bytes 49160 | tf_op jit(solution)/shard_map/ppermute | solution.py:488
  114.9 1.3 %collective-permute-start.12 = (bf16[4,16,128]{2,1,0:T(8,128)(2,1)S(1)}, bf16[4,16,128]{2,1,0:T(8,128)(2,1)S(1)}, u32[]{:S(2)}, u32[]{:S(2)}) collective-permute-start(bf16[4,16,128]{2,1,0:T(8,128)(2,1)S(1)} %get-tuple-element.65), channel_id=1, source_target_pairs={{0,8},{2,10},{1,9},{3,11},{16,24},{18,26},{17,25},{19,27}} | collective-permute-start | bytes 49160 | tf_op jit(solution)/shard_map/ppermute | solution.py:488
  116.1 1.3 %collective-permute-start.13 = (bf16[4,16,128]{2,1,0:T(8,128)(2,1)S(1)}, bf16[4,16,128]{2,1,0:T(8,128)(2,1)S(1)}, u32[]{:S(2)}, u32[]{:S(2)}) collective-permute-start(bf16[4,16,128]{2,1,0:T(8,128)(2,1)S(1)} %get-tuple-element.64), channel_id=1, source_target_pairs={{0,12},{2,14},{1,13},{3,15},{16,28},{18,30},{17,29},{19,31}} | collective-permute-start | bytes 49160 | tf_op jit(solution)/shard_map/ppermute | solution.py:488
  117.6 1.3 %collective-permute-done.13 = bf16[4,16,128]{2,1,0:T(8,128)(2,1)S(1)} collective-permute-done((bf16[4,16,128]{2,1,0:T(8,128)(2,1)S(1)}, bf16[4,16,128]{2,1,0:T(8,128)(2,1)S(1)}, u32[]{:S(2)}, u32[]{:S(2)}) %collective-permute-start.13) | collective-permute-done | bytes 16416 | tf_op jit(solution)/shard_map/ppermute | solution.py:488
  118.9 0.3 reshape.25
  119.2 1.0 copy.43
  120.4 0.2 copy.37
  120.6 1.1 reshape.28
  (26 shorter events, 0.9 us)
Async XLA Ops:
  0.7 1.2 copy-start
  2.4 13.8 %collective-permute-start = (bf16[3,896,128]{2,1,0:T(8,128)(2,1)S(1)}, bf16[3,896,128]{2,1,0:T(8,128)(2,1)S(1)}, u32[]{:S(2)}, u32[]{:S(2)}) collective-permute-start(bf16[3,896,128]{2,1,0:T(8,128)(2,1)S(1)} %shard_map.64.refs_1_.refs_2_), channel_id=1, source_target_pairs={{4,0},{6,2},{8,4},{10,6},{12,8},{14,10},{0,3},{2,1},{20,16},{22,18... | collective-permute-start | bytes 2064392 | tf_op jit(solution)/shard_map/ppermute | solution.py:427
  8.2 1.4 %collective-permute-start.1 = (f32[4,3,8,256]{3,2,1,0:T(8,128)S(1)}, f32[4,3,8,256]{3,2,1,0:T(8,128)S(1)}, u32[]{:S(2)}, u32[]{:S(2)}) collective-permute-start(f32[4,3,8,256]{3,2,1,0:T(8,128)S(1)} %reshape.24.kept_ref), channel_id=1, source_target_pairs={{0,1},{1,0},{2,3},{3,2},{4,5},{5,4},{6,7},{7,6},{8,9},{9,8},{10,11... | collective-permute-start | bytes 294920 | tf_op jit(solution)/shard_map/ppermute | solution.py:395
  9.6 0.7 copy-start.1
  10.2 0.7 copy-start.2
  10.9 0.7 copy-start.3
  16.3 4.0 %collective-permute-start.3 = (bf16[3,896,128]{2,1,0:T(8,128)(2,1)S(1)}, bf16[3,896,128]{2,1,0:T(8,128)(2,1)S(1)}, u32[]{:S(2)}, u32[]{:S(2)}) collective-permute-start(bf16[3,896,128]{2,1,0:T(8,128)(2,1)S(1)} %collective-permute-done.refs_4_.refs_1_), channel_id=1, source_target_pairs={{0,1},{1,0},{2,3},{3,2},{4,5},{5,4},{6,7},{7,6},{8,9},{9,8},{10,11... | collective-permute-start | bytes 2064392 | tf_op jit(solution)/shard_map/ppermute | solution.py:395
  16.3 15.0 %collective-permute-start.2 = (bf16[3,896,128]{2,1,0:T(8,128)(2,1)S(1)}, bf16[3,896,128]{2,1,0:T(8,128)(2,1)S(1)}, u32[]{:S(2)}, u32[]{:S(2)}) collective-permute-start(bf16[3,896,128]{2,1,0:T(8,128)(2,1)S(1)} %collective-permute-done.refs_4_.refs_1_), channel_id=1, source_target_pairs={{4,0},{6,2},{8,4},{10,6},{0,3},{2,1},{20,16},{22,18},{24,20},{26,2... | collective-permute-start | bytes 2064392 | tf_op jit(solution)/shard_map/ppermute | solution.py:427
  31.3 2.4 %collective-permute-start.5 = (bf16[3,896,128]{2,1,0:T(8,128)(2,1)S(1)}, bf16[3,896,128]{2,1,0:T(8,128)(2,1)S(1)}, u32[]{:S(2)}, u32[]{:S(2)}) collective-permute-start(bf16[3,896,128]{2,1,0:T(8,128)(2,1)S(1)} %collective-permute-done.2.refs_4_.refs_1_), channel_id=1, source_target_pairs={{0,1},{1,0},{2,3},{3,2},{4,5},{5,4},{6,7},{7,6},{8,9},{9,8},{10,11... | collective-permute-start | bytes 2064392 | tf_op jit(solution)/shard_map/ppermute | solution.py:395
  31.4 12.8 %collective-permute-start.4 = (bf16[3,896,128]{2,1,0:T(8,128)(2,1)S(1)}, bf16[3,896,128]{2,1,0:T(8,128)(2,1)S(1)}, u32[]{:S(2)}, u32[]{:S(2)}) collective-permute-start(bf16[3,896,128]{2,1,0:T(8,128)(2,1)S(1)} %collective-permute-done.2.refs_4_.refs_1_), channel_id=1, source_target_pairs={{4,0},{6,2},{0,3},{2,1},{20,16},{22,18},{16,19},{18,17}} | collective-permute-start | bytes 2064392 | tf_op jit(solution)/shard_map/ppermute | solution.py:427
  44.2 4.2 %collective-permute-start.6 = (bf16[3,896,128]{2,1,0:T(8,128)(2,1)S(1)}, bf16[3,896,128]{2,1,0:T(8,128)(2,1)S(1)}, u32[]{:S(2)}, u32[]{:S(2)}) collective-permute-start(bf16[3,896,128]{2,1,0:T(8,128)(2,1)S(1)} %collective-permute-done.4.refs_4_.refs_1_), channel_id=1, source_target_pairs={{0,1},{1,0},{2,3},{3,2},{4,5},{5,4},{6,7},{7,6},{8,9},{9,8},{10,11... | collective-permute-start | bytes 2064392 | tf_op jit(solution)/shard_map/ppermute | solution.py:395
  44.3 14.6 %collective-permute-start.7 = (bf16[3,896,128]{2,1,0:T(8,128)(2,1)S(1)}, bf16[3,896,128]{2,1,0:T(8,128)(2,1)S(1)}, u32[]{:S(2)}, u32[]{:S(2)}) collective-permute-start(bf16[3,896,128]{2,1,0:T(8,128)(2,1)S(1)} %collective-permute-done.4.refs_4_.refs_1_), channel_id=1, source_target_pairs={{0,3},{2,1},{16,19},{18,17}} | collective-permute-start | bytes 2064392 | tf_op jit(solution)/shard_map/ppermute | solution.py:427
  59.0 2.2 %collective-permute-start.8 = (bf16[3,896,128]{2,1,0:T(8,128)(2,1)S(1)}, bf16[3,896,128]{2,1,0:T(8,128)(2,1)S(1)}, u32[]{:S(2)}, u32[]{:S(2)}) collective-permute-start(bf16[3,896,128]{2,1,0:T(8,128)(2,1)S(1)} %collective-permute-done.7.refs_4_), channel_id=1, source_target_pairs={{0,1},{1,0},{2,3},{3,2},{4,5},{5,4},{6,7},{7,6},{8,9},{9,8},{10,11... | collective-permute-start | bytes 2064392 | tf_op jit(solution)/shard_map/ppermute | solution.py:395
  106.4 1.3 %collective-permute-start.9 = (bf16[128,128]{1,0:T(8,128)(2,1)S(1)}, bf16[128,128]{1,0:T(8,128)(2,1)S(1)}, u32[]{:S(2)}, u32[]{:S(2)}) collective-permute-start(bf16[128,128]{1,0:T(8,128)(2,1)S(1)} %get-tuple-element.62), channel_id=1, source_target_pairs={{0,1},{1,0},{2,3},{3,2},{4,5},{5,4},{6,7},{7,6},{8,9},{9,8},{10,11... | collective-permute-start | bytes 98312 | tf_op jit(solution)/shard_map/ppermute | solution.py:395
  107.7 5.8 %collective-permute-start.10 = (bf16[2,4,16,128]{3,2,1,0:T(8,128)(2,1)S(1)}, bf16[2,4,16,128]{3,2,1,0:T(8,128)(2,1)S(1)}, u32[]{:S(2)}, u32[]{:S(2)}) collective-permute-start(bf16[2,4,16,128]{3,2,1,0:T(8,128)(2,1)S(1)} %get-tuple-element.67), channel_id=1, source_target_pairs={{0,2},{2,0},{1,3},{3,1},{16,18},{18,16},{17,19},{19,17}} | collective-permute-start | bytes 98312 | tf_op jit(solution)/shard_map/ppermute | solution.py:483
  113.6 3.9 %collective-permute-start.11 = (bf16[4,16,128]{2,1,0:T(8,128)(2,1)S(1)}, bf16[4,16,128]{2,1,0:T(8,128)(2,1)S(1)}, u32[]{:S(2)}, u32[]{:S(2)}) collective-permute-start(bf16[4,16,128]{2,1,0:T(8,128)(2,1)S(1)} %get-tuple-element.63), channel_id=1, source_target_pairs={{0,4},{2,6},{1,5},{3,7},{16,20},{18,22},{17,21},{19,23}} | collective-permute-start | bytes 49160 | tf_op jit(solution)/shard_map/ppermute | solution.py:488
  114.9 2.7 %collective-permute-start.12 = (bf16[4,16,128]{2,1,0:T(8,128)(2,1)S(1)}, bf16[4,16,128]{2,1,0:T(8,128)(2,1)S(1)}, u32[]{:S(2)}, u32[]{:S(2)}) collective-permute-start(bf16[4,16,128]{2,1,0:T(8,128)(2,1)S(1)} %get-tuple-element.65), channel_id=1, source_target_pairs={{0,8},{2,10},{1,9},{3,11},{16,24},{18,26},{17,25},{19,27}} | collective-permute-start | bytes 49160 | tf_op jit(solution)/shard_map/ppermute | solution.py:488
  116.1 2.7 %collective-permute-start.13 = (bf16[4,16,128]{2,1,0:T(8,128)(2,1)S(1)}, bf16[4,16,128]{2,1,0:T(8,128)(2,1)S(1)}, u32[]{:S(2)}, u32[]{:S(2)}) collective-permute-start(bf16[4,16,128]{2,1,0:T(8,128)(2,1)S(1)} %get-tuple-element.64), channel_id=1, source_target_pairs={{0,12},{2,14},{1,13},{3,15},{16,28},{18,30},{17,29},{19,31}} | collective-permute-start | bytes 49160 | tf_op jit(solution)/shard_map/ppermute | solution.py:488
where the time goes:
time: 122 us
  Pallas kernels  78.8 us (65%)
  starting transfers between devices  21.1 us (17%)
  waiting for transfers between devices  13.2 us (11%)
  local copies, waits for them, and re-layouts  7.93 us (6%)
    pallas_call x4, Pallas kernels, shards(): pl.pallas_call(functools.partial(level_kernel, level, level == 0, level =...  43.4 us
    pallas_call x1, Pallas kernels, shards(): pl.pallas_call(second_kernel, grid=(segments,), out_shape=(jax.ShapeDtype...  33.8 us
    ppermute x4, starting transfers between devices, hand_on(): return lax.ppermute(value, ('segment', 'slab'), pairs)  14.6 us
    unnamed x10, local copies, waits for them, and re-layouts  4.88 us
    ppermute x6, waiting for transfers between devices, between_cores(): return lax.ppermute(value, 'slab', swap)  4.41 us
    ppermute x3, starting transfers between devices, shards(): out = out + lax.ppermute(crops[:, level], 'segment', pairs)  3.87 us
    ppermute x1, waiting for transfers between devices, shards(): lax.ppermute(lax.dynamic_index_in_dim(pair, 1 - line, 2, keepdims=False),...  3.78 us
    ppermute x4, waiting for transfers between devices, hand_on(): return lax.ppermute(value, ('segment', 'slab'), pairs)  3.61 us
  transfers between devices with their start and end apart: 14, of which 7 were waited for; matrix products, arithmetic and copies ran while one was open for 1% of the time, Pallas kernels for 27%

commit v1 on v0

--- a/solution.py
+++ b/solution.py
@@ -12,6 +12,7 @@
 LAYERS = 3
 CH = 64
 ROWS = 896
+SLOTS = 16
 VMEM_BYTES = 48 * 1024 * 1024
 
 MOVES = (
@@ -24,9 +25,6 @@
     [list(range(4)), list(range(4, 8))],
     [[2 * r, 2 * r + 1] for r in range(4)],
 )
-
-
-GROUPS = ((0,), (1,), (2,), (3,))
 
 
 def neighbour(layer, tile, step):
@@ -155,44 +153,122 @@
         activate_into(v_ref, at, value, layer)
 
 
-def convolve_pairs(v_ref, w_ref, tiles, layer):
+def stream(accs, unit, steps):
+    def push(at):
+        pltpu.matmul_push_rhs(steps[at][0](), at % 2, unit)
+
+    def take(results):
+        for slot, use in results:
+            use(pltpu.matmul_pop(accs[unit][slot]))
+
+    push(0)
+    waiting = ()
+    for at, (weights, rows, results) in enumerate(steps):
+        for index, (slot, value) in enumerate(rows):
+            pltpu.matmul_acc_lhs(accs[unit][slot], value(), load_staged_rhs=at % 2 if index == 0 else None)
+            if index == 0 and at + 1 < len(steps):
+                push(at + 1)
+        take(waiting)
+        waiting = results
+        yield
+    take(waiting)
+
+
+def convolve_pairs(v_ref, w_ref, layer, accs, finish):
     d = 2**layer
     low = low_lanes((128, 128))
-    sums = []
+    order = [tile for move in MOVES[layer + 1] for tile in move[:2]]
+
+    def push(index):
+        pltpu.matmul_push_rhs(w_ref[index, :, 0:256], index % 2, 0)
+        last = w_ref[index, :, 256:384]
+        pltpu.matmul_push_rhs(jnp.concatenate([last, last], axis=1), index % 2, 1)
+
+    def taken(slot):
+        both = pltpu.matmul_pop(accs[0][slot]).reshape(4, 16, 256)
+        last = pltpu.matmul_pop(accs[1][slot]).reshape(4, 16, 256)
+        before = z_moved(both[:, :, :128], -1, layer)
+        behind = z_moved(last[:, :, :128], 1, layer)
+        here = both[:, :, 128:]
+        return jnp.concatenate([here[:, 8 * i : 8 * i + 8] + before[i] + behind[i] for i in range(2)], axis=1)
+
+    first, second, waiting = {}, {}, []
+
+    def take():
+        index, tile, slots = waiting.pop(0)
+        total = jnp.concatenate([taken(slot) for slot in slots], axis=0)
+        if index == 0:
+            first[tile] = total
+        elif index == 1:
+            first[tile], second[tile] = first[tile] + total, total
+        elif index == 2:
+            first[tile], second[tile] = first[tile] + total, second[tile] - total
+        else:
+            second[tile] = second[tile] - total
+            halves = [half.reshape(8 // d, 1, d, 16, 128) for half in (first.pop(tile), second.pop(tile))]
+            finish(tile, jnp.concatenate(halves, axis=1).reshape(16, 16, 128))
+
+    push(0)
     for index in range(4):
-        rows = []
-        for tile in tiles:
+        for at, tile in enumerate(order):
             after = v_ref[index, neighbour(layer, tile, 1)]
             before = v_ref[index, neighbour(layer, tile, -1)]
-            rows.append(jnp.concatenate([v_ref[index, tile], jnp.where(low, after, before)], axis=1))
-        rows = jnp.concatenate(rows, axis=0)
-        sums.append(z_summed(jnp.dot(rows, w_ref[index], preferred_element_type=jnp.float32), 128, layer))
-    first = sums[0] + sums[1] + sums[2]
-    second = sums[1] - sums[2] - sums[3]
-    results = []
-    for at in range(len(tiles)):
-        halves = [half[at * 8 : (at + 1) * 8].reshape(8 // d, 1, d, 16, 128) for half in (first, second)]
-        results.append(jnp.concatenate(halves, axis=1).reshape(16, 16, 128))
-    return results
-
-
-def convolve_cycles(v_ref, w_ref, units, layer):
-    def rows(*forms):
-        parts = [jnp.concatenate([v_ref[form, 2 * r + m] for form in forms for m in range(2)], axis=1) for r in units]
-        return jnp.concatenate(parts, axis=0)
-
-    def summed(lhs, begin, end):
-        return z_summed(jnp.dot(lhs, w_ref[begin:end, :], preferred_element_type=jnp.float32), 256, layer)
-
-    flat = summed(rows(0), 0, 256)
-    alternate = summed(rows(1), 256, 512)
-    waves = summed(jnp.concatenate([rows(2, 4), rows(3, 2)], axis=0), 512, 1024)
-    count = 4 * len(units)
-    cosine, sine = waves[:count], waves[count:]
-    even, odd = flat + alternate, flat - alternate
-    cells = [value.reshape(len(units), 1, 4, 16, 256) for value in (even + cosine, odd - sine, even - cosine, odd + sine)]
-    cells = jnp.concatenate(cells, axis=1).reshape(len(units), 16, 16, 256)
-    return [cells[at, :, :, m * 128 : m * 128 + 128] for at in range(len(units)) for m in range(2)]
+            rows = jnp.concatenate([v_ref[index, tile], jnp.where(low, after, before)], axis=1)
+            base = 2 * ((8 * index + at) % (SLOTS // 2))
+            for half in range(2):
+                for acc in accs:
+                    staged = index % 2 if at == 0 and half == 0 else None
+                    pltpu.matmul_acc_lhs(acc[base + half], rows[64 * half : 64 * half + 64], load_staged_rhs=staged)
+            waiting.append((index, tile, (base, base + 1)))
+            if at == 2 and index < 3:
+                push(index + 1)
+            if len(waiting) == 3:
+                take()
+    while waiting:
+        take()
+
+
+def convolve_cycles(v_ref, w_ref, layer, accs, finish):
+    sums = {}
+
+    def rows(form, r):
+        return lambda: jnp.concatenate([v_ref[form, 2 * r], v_ref[form, 2 * r + 1]], axis=1)
+
+    def weights(row, tz):
+        return lambda: w_ref[row * 256 : row * 256 + 256, tz * 256 : tz * 256 + 256]
+
+    def adding(name, r, tz):
+        def use(product):
+            product = product.reshape(4, 16, 256)
+            if tz != 1:
+                product = jnp.concatenate(z_moved(product, tz - 1, layer), axis=1)
+            sums[name, r] = sums[name, r] + product if (name, r) in sums else product
+
+        return use
+
+    def plain(form, tz, base):
+        fed = [(base + r, rows(form, r)) for r in range(4)]
+        return [(weights(form, tz), fed, [(base + r, adding(form, r, tz)) for r in range(4)])]
+
+    def paired(tz, base):
+        ends = [(base + r, adding(2, r, tz)) for r in range(4)] + [(base + 4 + r, adding(3, r, tz)) for r in range(4)]
+        real = [(base + r, rows(2, r)) for r in range(4)] + [(base + 4 + r, rows(3, r)) for r in range(4)]
+        other = [(base + r, rows(4, r)) for r in range(4)] + [(base + 4 + r, rows(2, r)) for r in range(4)]
+        return [(weights(2, tz), real, ()), (weights(3, tz), other, ends)]
+
+    ways = (
+        paired(0, 0) + paired(1, 8) + plain(0, 0, 0),
+        paired(2, 0) + plain(0, 1, 8) + plain(0, 2, 0) + plain(1, 0, 8) + plain(1, 1, 0) + plain(1, 2, 8),
+    )
+    streams = [stream(accs, unit, steps) for unit, steps in enumerate(ways)]
+    while streams:
+        streams = [one for one in streams if next(one, True) is None]
+    for r in range(4):
+        even, odd = sums[0, r] + sums[1, r], sums[0, r] - sums[1, r]
+        cosine, sine = sums[2, r], sums[3, r]
+        cells = jnp.stack([even + cosine, odd - sine, even - cosine, odd + sine]).reshape(16, 16, 256)
+        for m in range(2):
+            finish(2 * r + m, cells[:, :, m * 128 : m * 128 + 128])
 
 
 def begin_section(state, v_refs):
@@ -204,22 +280,30 @@
     s_a, *held_in = state
     begin_section(state, v_refs)
     prepare(0)
-    for layer in range(LAYERS):
-        held, following = held_in[layer], held_in[(layer + 1) % LAYERS]
-        if layer + 1 < LAYERS:
-            prepare(layer + 1)
-        bias = bias_refs[layer][0:1][None]
-        if layer == LAYERS - 1:
-            for tile, total in enumerate(convolve_cycles(v_refs[2], w_refs[layer], range(4), layer)):
-                s_a[tile] = (held[tile] + bias + total).astype(jnp.bfloat16).astype(jnp.float32)
-            break
-        for chosen in GROUPS:
-            moves = [MOVES[layer + 1][at] for at in chosen]
-            tiles = [tile for move in moves for tile in move[:2]]
-            sums = convolve_pairs(v_refs[layer], w_refs[layer], tiles, layer)
-            sums = [held[tile] + bias + total for tile, total in zip(tiles, sums)]
-            for at, move in enumerate(moves):
-                spread(move, sums[2 * at], sums[2 * at + 1], following, v_refs[layer + 1], layer + 1)
+
+    def layers(*accs):
+        accs = accs[:SLOTS], accs[SLOTS:]
+        for layer in range(LAYERS):
+            held, following = held_in[layer], held_in[(layer + 1) % LAYERS]
+            if layer + 1 < LAYERS:
+                prepare(layer + 1)
+            bias = bias_refs[layer][0:1][None]
+            done = {}
+
+            def finish(tile, total, layer=layer, held=held, following=following, bias=bias, done=done):
+                total = held[tile] + bias + total
+                if layer == LAYERS - 1:
+                    s_a[tile] = total.astype(jnp.bfloat16).astype(jnp.float32)
+                    return
+                done[tile] = total
+                for move in MOVES[layer + 1]:
+                    if tile == move[1]:
+                        spread(move, done.pop(move[0]), done.pop(tile), following, v_refs[layer + 1], layer + 1)
+
+            convolve = convolve_cycles if layer == LAYERS - 1 else convolve_pairs
+            convolve(v_refs[layer], w_refs[layer], layer, accs, finish)
+
+    pl.run_scoped(layers, *[pltpu.ACC(unit)((64, 256), jnp.float32) for unit in range(2) for slot in range(SLOTS)])
 
 
 def by_parity(x):
@@ -232,35 +316,43 @@
     return jnp.concatenate([moved[at * 16 : (at + 1) * 16] for at in range(16)], axis=1)
 
 
-def lift_into(x, lift_ref, s_a):
+def lifted(x, lift):
     high = x.astype(jnp.bfloat16).astype(jnp.float32)
     columns = jnp.concatenate([high, x - high, high], axis=0).T.astype(jnp.bfloat16)
-    hidden = jnp.dot(columns, lift_ref[...], preferred_element_type=jnp.float32)
-    s_a[...] = hidden.astype(jnp.bfloat16).astype(jnp.float32).reshape(8, 16, 16, 128)
-
-
-def renewed_fields(x, proj_ref, s_a):
-    gain = nt_dot(proj_ref[...], s_a[...].reshape(2048, 128).astype(jnp.bfloat16))
+    hidden = jnp.dot(columns, lift, preferred_element_type=jnp.float32)
+    return hidden.astype(jnp.bfloat16).reshape(8, 16, 16, 128)
+
+
+def renewed_fields(x, proj_ref, hidden_ref):
+    gain = nt_dot(proj_ref[...], hidden_ref[...].reshape(2048, 128))
     return x + gain[:16] + gain[16:32] + gain[32:48]
 
 
-def level_kernel(level, first, last, *refs):
-    (ids_ref, own_0, own_1, far_0, far_1, x_ref, lift_ref, proj_ref) = refs[:8]
-    (w_out, c_out, b_out, leaving, x_out, s_a, s_b, s_c, s_d, v_a, v_b, v_c) = refs[-17:-5]
+def renew_kernel(x_ref, hidden_ref, lift_ref, proj_ref, x_out, hidden_out):
+    x = renewed_fields(x_ref[...], proj_ref, hidden_ref)
+    x_out[...] = x
+    hidden_out[...] = lifted(x, lift_ref[...])
+
+
+def result_kernel(ids_ref, x_ref, hidden_ref, proj_ref, kept, given, x_new):
+    x_new[...] = renewed_fields(x_ref[...], proj_ref, hidden_ref)
+    kept[...] = cells_in_rows((x_ref, x_new), ids_ref[0])
+    given[...] = cells_in_rows((x_ref, x_new), 1 - ids_ref[0])
+
+
+def level_kernel(level, *refs):
+    (ids_ref, own_0, own_1, far_0, far_1, entry) = refs[:6]
+    (w_out, c_out, b_out, leaving, s_a, s_b, s_c, s_d, v_a, v_b, v_c) = refs[-16:-5]
     (packed, w_pair, w_cycle, b_all, sems) = refs[-5:]
     slab, line = ids_ref[0], ids_ref[1]
-    x = by_parity(x_ref[...]) if first else x_ref[...]
-    if first:
-        lift_into(x, lift_ref, s_a)
-    else:
-        s_a[...] = refs[8][...].astype(jnp.float32)
+    s_a[...] = entry[...].astype(jnp.float32)
     state, v_refs = (s_a, s_b, s_c, s_d), (v_a, v_b, v_c)
 
-    def copies(turn):
+    def copy(turn, part):
         at = 2 * level + turn
-        pairs = [pltpu.make_async_copy(w_pair.at[turn, i], w_out.at[at, i], sems.at[turn, i]) for i in range(2)]
-        cycle = pltpu.make_async_copy(w_cycle.at[turn], c_out.at[at], sems.at[turn, 2])
-        return pairs + [cycle, pltpu.make_async_copy(b_all.at[turn], b_out.at[at], sems.at[turn, 3])]
+        source = (w_pair.at[turn, 0], w_pair.at[turn, 1], w_cycle.at[turn], b_all.at[turn])[part]
+        target = (w_out.at[at, 0], w_out.at[at, 1], c_out.at[at], b_out.at[at])[part]
+        return pltpu.make_async_copy(source, target, sems.at[turn, part])
 
     def section(turn, unused):
         for wanted, sources in ((True, (own_0, own_1)), (False, (far_0, far_1))):
@@ -274,21 +366,20 @@
 
         def prepare(layer):
             expand(packed.at[layer], w_refs[layer], b_all.at[turn, layer], layer)
-            copies(turn)[layer].start()
+            copy(turn, layer).start()
 
         run_section(state, v_refs, w_refs, [b_all.at[turn, i] for i in range(LAYERS)], prepare)
-        copies(turn)[LAYERS].start()
+        copy(turn, LAYERS).start()
         return 0
 
     lax.fori_loop(0, 2, section, 0)
     leaving[...] = s_a[...].astype(jnp.bfloat16)
-    x_out[...] = renewed_fields(x, proj_ref, s_a) if last else x
     for turn in range(2):
-        for copy in copies(turn):
-            copy.wait()
-
-
-def feature_kernel(ids_ref, anchor_ref, kept_ref, got_ref, lift_ref, proj_ref, x_ref, lift_out, proj_out):
+        for part in range(LAYERS + 1):
+            copy(turn, part).wait()
+
+
+def feature_kernel(ids_ref, anchor_ref, kept_ref, got_ref, lift_ref, proj_ref, x_ref, lift_out, proj_out, hidden_out):
     slab, slot = ids_ref[0], ids_ref[2]
     kept, got = kept_ref[slot], got_ref[slot]
     halves = (jnp.where(slab == 0, kept, got), jnp.where(slab == 0, got, kept))
@@ -306,7 +397,8 @@
     axis = jnp.where(row >= 9, row - 9, row - 6)
     position = jnp.where(axis == 0, along_x, jnp.where(axis == 1, along_y, along_z)) & (FIELD - 1)
     waves = jnp.sin(2.0 * jnp.pi * position.astype(jnp.float32) / FIELD)
-    x_ref[...] = jnp.where(row < 6, current, jnp.where(row < 12, waves, 0.0))
+    x = by_parity(jnp.where(row < 6, current, jnp.where(row < 12, waves, 0.0)))
+    x_ref[...] = x
 
     def two_halves(part):
         blank = jnp.zeros(part.shape, jnp.float32)
@@ -315,7 +407,9 @@
     lift = 0.5 * lift_ref[...]
     lift = two_halves(lift[0:3]) + two_halves(lift[3:6]) + [jnp.zeros((4, 128), jnp.float32)]
     first, second, unused = [term.astype(jnp.float32) for term in split_terms(jnp.concatenate(lift, axis=0))]
-    lift_out[...] = jnp.concatenate([first, first, second], axis=0).astype(jnp.bfloat16)
+    lift = jnp.concatenate([first, first, second], axis=0).astype(jnp.bfloat16)
+    lift_out[...] = lift
+    hidden_out[...] = lifted(x, lift)
     proj = two_halves(2.0 * proj_ref[...]) + [jnp.zeros((10, 128), jnp.float32)]
     proj = [term.astype(jnp.float32) for term in split_terms(jnp.concatenate(proj, axis=0))]
     proj_out[...] = jnp.concatenate(proj, axis=0).astype(jnp.bfloat16)
@@ -336,23 +430,20 @@
     return nt_dot(turned, jnp.concatenate(blocks, axis=0).astype(jnp.bfloat16)).astype(jnp.bfloat16)
 
 
-def second_kernel(ids_ref, x_ref, lift_ref, proj_ref, w_ref, c_ref, b_ref, kept, given, s_a, s_b, s_c, s_d, v_a, v_b, v_c, x_new):
+def second_kernel(entry, w_ref, c_ref, b_ref, leaving, s_a, s_b, s_c, s_d, v_a, v_b, v_c):
     s = pl.program_id(0)
-
-    state, v_refs = (s_a, s_b, s_c, s_d), (v_a, v_b, v_c)
 
     @pl.when(s == 0)
     def begin():
-        lift_into(x_ref[...], lift_ref, s_a)
+        s_a[...] = entry[...].astype(jnp.float32)
 
     w_refs = [w_ref.at[0, 0], w_ref.at[0, 1], c_ref.at[0]]
-    run_section(state, v_refs, w_refs, [b_ref.at[0, i] for i in range(LAYERS)], lambda layer: None)
+    biases = [b_ref.at[0, i] for i in range(LAYERS)]
+    run_section((s_a, s_b, s_c, s_d), (v_a, v_b, v_c), w_refs, biases, lambda layer: None)
 
     @pl.when(s == pl.num_programs(0) - 1)
     def finish():
-        x_new[...] = renewed_fields(x_ref[...], proj_ref, s_a)
-        kept[...] = cells_in_rows((x_ref, x_new), ids_ref[0])
-        given[...] = cells_in_rows((x_ref, x_new), 1 - ids_ref[0])
+        leaving[...] = s_a[...].astype(jnp.bfloat16)
 
 
 def split_terms(matrix):
@@ -403,23 +494,24 @@
     )(conv_weight[0], conv_bias[0], jnp.eye(192, dtype=jnp.bfloat16))
 
     flat = after(fields, packed).reshape(crop_count, comps, slab_rows, y_cells * z_cells)
-    x, lift, proj = pl.pallas_call(
+    h_shape = jax.ShapeDtypeStruct((8, 16, 16, 128), jnp.bfloat16)
+    x_shape = jax.ShapeDtypeStruct((16, 2048), jnp.float32)
+    x, lift, proj, hidden = pl.pallas_call(
         feature_kernel,
         out_shape=(
-            jax.ShapeDtypeStruct((16, 2048), jnp.float32),
+            x_shape,
             jax.ShapeDtypeStruct((48, 128), jnp.bfloat16),
             jax.ShapeDtypeStruct((48, 128), jnp.bfloat16),
+            h_shape,
         ),
         in_specs=[smem, smem] + [vmem] * 4,
-        out_specs=(vmem, vmem, vmem),
+        out_specs=(vmem, vmem, vmem, vmem),
         compiler_params=params,
     )(ids, anchors, flat, between_cores(flat), lift_weight.T, proj_weight)
 
     w_shape = jax.ShapeDtypeStruct((segments, 2, 4, 256, 384), jnp.bfloat16)
     c_shape = jax.ShapeDtypeStruct((segments, 1024, 768), jnp.bfloat16)
     b_shape = jax.ShapeDtypeStruct((segments, LAYERS, 8, 128), jnp.float32)
-    h_shape = jax.ShapeDtypeStruct((8, 16, 16, 128), jnp.bfloat16)
-    x_shape = jax.ShapeDtypeStruct((16, 2048), jnp.float32)
     layer_flops = 2 * 4 * 1024 * 256 * 512
     def hand_on(value, level):
         pairs = [(s * slabs, (s - lines) * slabs) for s in range(lines, segments - lines * level)]
@@ -430,15 +522,14 @@
     swapped = {0: between_cores(arrived[0])}
     arrived[1] = hand_on(arrived[0], 1)
     kept = ()
-    current = x
     for level in range(levels):
         own = (packed, packed) if level == 0 else (arrived[level - 1], swapped[level - 1])
-        operands = (ids, *own, swapped[level], arrived[level], current, lift, proj, *kept)
-        weights, cycles, rows, hidden, current = pl.pallas_call(
-            functools.partial(level_kernel, level, level == 0, level == levels - 1),
-            out_shape=(w_shape, c_shape, b_shape, h_shape, x_shape),
-            in_specs=[smem] + [vmem] * 7 + ([vmem] + [anyspace] * 3 if kept else []),
-            out_specs=(anyspace, anyspace, anyspace, vmem, vmem),
+        operands = (ids, *own, swapped[level], arrived[level], hidden, *kept)
+        weights, cycles, rows, hidden = pl.pallas_call(
+            functools.partial(level_kernel, level),
+            out_shape=(w_shape, c_shape, b_shape, h_shape),
+            in_specs=[smem] + [vmem] * 5 + ([anyspace] * 3 if kept else []),
+            out_specs=(anyspace, anyspace, anyspace, vmem),
             scratch_shapes=state_scratch()
             + [
                 pltpu.VMEM((LAYERS, ROWS, 128), jnp.bfloat16),
@@ -447,33 +538,46 @@
                 pltpu.VMEM((2, LAYERS, 8, 128), jnp.float32),
                 pltpu.SemaphoreType.DMA((2, LAYERS + 1)),
             ],
-            input_output_aliases={9: 0, 10: 1, 11: 2} if kept else {},
+            input_output_aliases={6: 0, 7: 1, 8: 2} if kept else {},
             compiler_params=params,
             cost_estimate=pl.CostEstimate(flops=2 * LAYERS * layer_flops, bytes_accessed=4 << 20, transcendentals=0),
         )(*operands)
-        kept = (hidden, weights, cycles, rows)
+        kept = (weights, cycles, rows)
         if level + 1 < levels:
             arrived[level + 1] = after(arrived[level + 1], hidden)
             swapped[level + 1] = between_cores(arrived[level + 1])
             if level + 2 < levels:
                 arrived[level + 2] = hand_on(arrived[level + 1], level + 2)
-    first_result = current
-    kept, given = pl.pallas_call(
+    x, hidden = pl.pallas_call(
+        renew_kernel,
+        out_shape=(x_shape, h_shape),
+        in_specs=[vmem] * 4,
+        out_specs=(vmem, vmem),
+        compiler_params=params,
+    )(x, hidden, lift, proj)
+    hidden = pl.pallas_call(
         second_kernel,
         grid=(segments,),
-        out_shape=(jax.ShapeDtypeStruct((128, 128), jnp.bfloat16),) * 2,
-        in_specs=[smem]
-        + [vmem] * 3
-        + [
+        out_shape=h_shape,
+        in_specs=[
+            vmem,
             pl.BlockSpec((1, 2, 4, 256, 384), lambda s: (s, 0, 0, 0, 0)),
             pl.BlockSpec((1, 1024, 768), lambda s: (s, 0, 0)),
             pl.BlockSpec((1, LAYERS, 8, 128), lambda s: (s, 0, 0, 0)),
         ],
-        out_specs=(vmem, vmem),
-        scratch_shapes=state_scratch() + [pltpu.VMEM((16, 2048), jnp.float32)],
+        out_specs=vmem,
+        scratch_shapes=state_scratch(),
         compiler_params=params,
         cost_estimate=pl.CostEstimate(flops=segments * LAYERS * layer_flops, bytes_accessed=16 << 20, transcendentals=0),
-    )(ids, first_result, lift, proj, weights, cycles, rows)
+    )(hidden, weights, cycles, rows)
+    kept, given = pl.pallas_call(
+        result_kernel,
+        out_shape=(jax.ShapeDtypeStruct((128, 128), jnp.bfloat16),) * 2,
+        in_specs=[smem] + [vmem] * 3,
+        out_specs=(vmem, vmem),
+        scratch_shapes=[pltpu.VMEM((16, 2048), jnp.float32)],
+        compiler_params=params,
+    )(ids, x, hidden, proj)
 
     share = z_cells // segments
     got = between_cores(given)

time: 122 us -> 127 us (1.041)
  Pallas kernels: 78.8 us -> 84.7 us
    pallas_call x6 -> x8, Pallas kernels: 78.3 us -> 84.1 us  [the longest x4 43.9 us: shards(): pl.pallas_call(functools.partial(level_kernel, level), out_shape=(w_shape...]
where the time goes in v1:
time: 127 us
  Pallas kernels  84.7 us (67%)
  starting transfers between devices  21.1 us (17%)
  waiting for transfers between devices  12.5 us (10%)
  local copies, waits for them, and re-layouts  7.93 us (6%)
    pallas_call x4, Pallas kernels, shards(): pl.pallas_call(functools.partial(level_kernel, level), out_shape=(w_shape...  43.9 us
    pallas_call x1, Pallas kernels, shards(): pl.pallas_call(second_kernel, grid=(segments,), out_shape=h_shape, in_spe...  36.9 us
    ppermute x4, starting transfers between devices, hand_on(): return lax.ppermute(value, ('segment', 'slab'), pairs)  14.7 us
    unnamed x10, local copies, waits for them, and re-layouts  4.88 us
    ppermute x6, waiting for transfers between devices, between_cores(): return lax.ppermute(value, 'slab', swap)  4.4 us
    ppermute x3, starting transfers between devices, shards(): out = out + lax.ppermute(crops[:, level], 'segment', pairs)  3.87 us
    ppermute x1, waiting for transfers between devices, shards(): lax.ppermute(lax.dynamic_index_in_dim(pair, 1 - line, 2, keepdims=False),...  3.78 us
    ppermute x4, waiting for transfers between devices, hand_on(): return lax.ppermute(value, ('segment', 'slab'), pairs)  2.94 us
  transfers between devices with their start and end apart: 14, of which 7 were waited for; matrix products, arithmetic and copies ran while one was open for 1% of the time, Pallas kernels for 27%

profile of v1, /device:TPU:0, one launch (start us, length us, event | category | flops | bytes accessed | tf_op | source)
XLA Modules:
  0.0 126.8 jit_solution(7031471985207917239)
XLA Ops:
  0.0 0.7 copy.47
  0.7 1.2 copy-done
  1.9 0.5 shard_map.64.refs_1_.refs_2_
  2.4 4.3 %collective-permute-start.1 = (bf16[3,896,128]{2,1,0:T(8,128)(2,1)S(1)}, bf16[3,896,128]{2,1,0:T(8,128)(2,1)S(1)}, u32[]{:S(2)}, u32[]{:S(2)}) collective-permute-start(bf16[3,896,128]{2,1,0:T(8,128)(2,1)S(1)} %shard_map.64.refs_1_.refs_2_), channel_id=1, source_target_pairs={{4,0},{6,2},{8,4},{10,6},{12,8},{14,10},{0,3},{2,1},{20,16},{22,18... | collective-permute-start | bytes 2064392 | tf_op jit(solution)/shard_map/ppermute | solution.py:519
  6.8 1.4 %reshape.24.kept_ref = f32[4,3,8,256]{3,2,1,0:T(8,128)S(1)} reshape(f32[4,3,8,16,16]{4,3,2,1,0:T(8,128)} %param.6) | data formatting | bytes 196608 | tf_op jit(solution)/shard_map/reshape | solution.py:496
  8.4 1.2 collective-permute-done.got_ref
  9.6 0.7 copy-done.1
  10.2 0.7 copy-done.2
  10.9 0.7 copy-done.3
  11.6 1.7 %shard_map.65 = (f32[16,2048]{1,0:T(8,128)S(1)}, bf16[48,128]{1,0:T(8,128)(2,1)S(1)}, bf16[48,128]{1,0:T(8,128)(2,1)S(1)}, bf16[8,16,16,128]{3,2,1,0:T(8,128)(2,1)S(1)}) custom-call(s32[3]{0:T(128)S(1)} %pad_add_fusion.ids_ref.refs_0_, s32[4,3]{1,0:T(4,128)S(1)} %copy-done.2, f32[4,3,8,256]{3,2,1,0:T(8,128)S(1)} %reshape.24.kept_ref, ...), custom_call_target="tpu_custom_call" | custom-call | tf_op jit(solution)/shard_map/pallas_call | solution.py:499
  13.3 2.9 %collective-permute-done.1.refs_4_.refs_1_ = bf16[3,896,128]{2,1,0:T(8,128)(2,1)S(1)} collective-permute-done((bf16[3,896,128]{2,1,0:T(8,128)(2,1)S(1)}, bf16[3,896,128]{2,1,0:T(8,128)(2,1)S(1)}, u32[]{:S(2)}, u32[]{:S(2)}) %collective-permute-start.1) | collective-permute-done | bytes 688160 | tf_op jit(solution)/shard_map/ppermute | solution.py:519
  16.3 3.9 %collective-permute-start.2 = (bf16[3,896,128]{2,1,0:T(8,128)(2,1)S(1)}, bf16[3,896,128]{2,1,0:T(8,128)(2,1)S(1)}, u32[]{:S(2)}, u32[]{:S(2)}) collective-permute-start(bf16[3,896,128]{2,1,0:T(8,128)(2,1)S(1)} %collective-permute-done.1.refs_4_.refs_1_), channel_id=1, source_target_pairs={{4,0},{6,2},{8,4},{10,6},{0,3},{2,1},{20,16},{22,18},{24,20},{26,2... | collective-permute-start | bytes 2064392 | tf_op jit(solution)/shard_map/ppermute | solution.py:519
  20.3 11.0 %shard_map.66 = (bf16[8,2,4,256,384]{4,3,2,1,0:T(8,128)(2,1)}, bf16[8,1024,768]{2,1,0:T(8,128)(2,1)}, f32[8,3,8,128]{3,2,1,0:T(8,128)S(1)}, bf16[8,16,16,128]{3,2,1,0:T(8,128)(2,1)S(1)}) custom-call(s32[3]{0:T(128)S(1)} %pad_add_fusion.ids_ref.refs_0_, bf16[3,896,128]{2,1,0:T(8,128)(2,1)S(1)} %shard_map.64.refs_1_.refs_2_, ...), custom_call_target="tpu_custom_call" | custom-call | flops 6442450944 | bytes 4194304 | tf_op jit(solution)/shard_map/pallas_call | solution.py:528
  31.4 2.3 %collective-permute-start.4 = (bf16[3,896,128]{2,1,0:T(8,128)(2,1)S(1)}, bf16[3,896,128]{2,1,0:T(8,128)(2,1)S(1)}, u32[]{:S(2)}, u32[]{:S(2)}) collective-permute-start(bf16[3,896,128]{2,1,0:T(8,128)(2,1)S(1)} %collective-permute-done.2.refs_4_.refs_1_), channel_id=1, source_target_pairs={{4,0},{6,2},{0,3},{2,1},{20,16},{22,18},{16,19},{18,17}} | collective-permute-start | bytes 2064392 | tf_op jit(solution)/shard_map/ppermute | solution.py:519
  33.7 11.0 %shard_map.67 = (bf16[8,2,4,256,384]{4,3,2,1,0:T(8,128)(2,1)}, bf16[8,1024,768]{2,1,0:T(8,128)(2,1)}, f32[8,3,8,128]{3,2,1,0:T(8,128)S(1)}, bf16[8,16,16,128]{3,2,1,0:T(8,128)(2,1)S(1)}) custom-call(s32[3]{0:T(128)S(1)} %pad_add_fusion.ids_ref.refs_0_, ...), custom_call_target="tpu_custom_call", output_to_operand_aliasing={{0}: (6, {}), {1}: (7, {}), {2}: (8, {})} | custom-call | flops 6442450944 | bytes 4194304 | tf_op jit(solution)/shard_map/pallas_call | solution.py:528
  44.7 4.2 %collective-permute-start.7 = (bf16[3,896,128]{2,1,0:T(8,128)(2,1)S(1)}, bf16[3,896,128]{2,1,0:T(8,128)(2,1)S(1)}, u32[]{:S(2)}, u32[]{:S(2)}) collective-permute-start(bf16[3,896,128]{2,1,0:T(8,128)(2,1)S(1)} %collective-permute-done.4.refs_4_.refs_1_), channel_id=1, source_target_pairs={{0,3},{2,1},{16,19},{18,17}} | collective-permute-start | bytes 2064392 | tf_op jit(solution)/shard_map/ppermute | solution.py:519
  48.9 10.9 %shard_map.68 = (bf16[8,2,4,256,384]{4,3,2,1,0:T(8,128)(2,1)}, bf16[8,1024,768]{2,1,0:T(8,128)(2,1)}, f32[8,3,8,128]{3,2,1,0:T(8,128)S(1)}, bf16[8,16,16,128]{3,2,1,0:T(8,128)(2,1)S(1)}) custom-call(s32[3]{0:T(128)S(1)} %pad_add_fusion.ids_ref.refs_0_, ...), custom_call_target="tpu_custom_call", output_to_operand_aliasing={{0}: (6, {}), {1}: (7, {}), {2}: (8, {})} | custom-call | flops 6442450944 | bytes 4194304 | tf_op jit(solution)/shard_map/pallas_call | solution.py:528
  60.0 2.1 %collective-permute-done.8.refs_3_ = bf16[3,896,128]{2,1,0:T(8,128)(2,1)S(1)} collective-permute-done((bf16[3,896,128]{2,1,0:T(8,128)(2,1)S(1)}, bf16[3,896,128]{2,1,0:T(8,128)(2,1)S(1)}, u32[]{:S(2)}, u32[]{:S(2)}) %collective-permute-start.8) | collective-permute-done | bytes 688160 | tf_op jit(solution)/shard_map/ppermute | solution.py:486
  62.1 11.0 %shard_map.69 = (bf16[8,2,4,256,384]{4,3,2,1,0:T(8,128)(2,1)}, bf16[8,1024,768]{2,1,0:T(8,128)(2,1)}, f32[8,3,8,128]{3,2,1,0:T(8,128)S(1)}, bf16[8,16,16,128]{3,2,1,0:T(8,128)(2,1)S(1)}) custom-call(s32[3]{0:T(128)S(1)} %pad_add_fusion.ids_ref.refs_0_, ...), custom_call_target="tpu_custom_call", output_to_operand_aliasing={{0}: (6, {}), {1}: (7, {}), {2}: (8, {})} | custom-call | flops 6442450944 | bytes 4194304 | tf_op jit(solution)/shard_map/pallas_call | solution.py:528
  73.1 0.6 shard_map.70
  73.7 36.9 %shard_map.71.hidden_ref = bf16[8,16,16,128]{3,2,1,0:T(8,128)(2,1)S(1)} custom-call(bf16[8,16,16,128]{3,2,1,0:T(8,128)(2,1)S(1)} %get-tuple-element.57.entry, bf16[8,2,4,256,384]{4,3,2,1,0:T(8,128)(2,1)} %get-tuple-element.58.w_ref, bf16[8,1024,768]{2,1,0:T(8,128)(2,1)} %get-tuple-element.59.c_ref, f32[8,3,8,128]{3,2,1,0:T(8,128)S(1)} %get-tuple-element.60.b_ref), custom_call_target="tpu_custom_call" | custom-call | flops 25769803776 | bytes 16777216 | tf_op jit(solution)/shard_map/pallas_call | solution.py:558
  110.6 1.0 shard_map.72
  111.8 1.1 collective-permute-done.9
  112.9 2.0 %collective-permute-start.10 = (bf16[2,4,16,128]{3,2,1,0:T(8,128)(2,1)S(1)}, bf16[2,4,16,128]{3,2,1,0:T(8,128)(2,1)S(1)}, u32[]{:S(2)}, u32[]{:S(2)}) collective-permute-start(bf16[2,4,16,128]{3,2,1,0:T(8,128)(2,1)S(1)} %get-tuple-element.67), channel_id=1, source_target_pairs={{0,2},{2,0},{1,3},{3,1},{16,18},{18,16},{17,19},{19,17}} | collective-permute-start | bytes 98312 | tf_op jit(solution)/shard_map/ppermute | solution.py:587
  115.0 3.8 %collective-permute-done.10 = bf16[2,4,16,128]{3,2,1,0:T(8,128)(2,1)S(1)} collective-permute-done((bf16[2,4,16,128]{3,2,1,0:T(8,128)(2,1)S(1)}, bf16[2,4,16,128]{3,2,1,0:T(8,128)(2,1)S(1)}, u32[]{:S(2)}, u32[]{:S(2)}) %collective-permute-start.10) | collective-permute-done | bytes 32800 | tf_op jit(solution)/shard_map/ppermute | solution.py:587
  118.8 1.3 %collective-permute-start.11 = (bf16[4,16,128]{2,1,0:T(8,128)(2,1)S(1)}, bf16[4,16,128]{2,1,0:T(8,128)(2,1)S(1)}, u32[]{:S(2)}, u32[]{:S(2)}) collective-permute-start(bf16[4,16,128]{2,1,0:T(8,128)(2,1)S(1)} %get-tuple-element.63), channel_id=1, source_target_pairs={{0,4},{2,6},{1,5},{3,7},{16,20},{18,22},{17,21},{19,23}} | collective-permute-start | bytes 49160 | tf_op jit(solution)/shard_map/ppermute | solution.py:592
  120.1 1.3 %collective-permute-start.12 = (bf16[4,16,128]{2,1,0:T(8,128)(2,1)S(1)}, bf16[4,16,128]{2,1,0:T(8,128)(2,1)S(1)}, u32[]{:S(2)}, u32[]{:S(2)}) collective-permute-start(bf16[4,16,128]{2,1,0:T(8,128)(2,1)S(1)} %get-tuple-element.65), channel_id=1, source_target_pairs={{0,8},{2,10},{1,9},{3,11},{16,24},{18,26},{17,25},{19,27}} | collective-permute-start | bytes 49160 | tf_op jit(solution)/shard_map/ppermute | solution.py:592
  121.4 1.3 %collective-permute-start.13 = (bf16[4,16,128]{2,1,0:T(8,128)(2,1)S(1)}, bf16[4,16,128]{2,1,0:T(8,128)(2,1)S(1)}, u32[]{:S(2)}, u32[]{:S(2)}) collective-permute-start(bf16[4,16,128]{2,1,0:T(8,128)(2,1)S(1)} %get-tuple-element.64), channel_id=1, source_target_pairs={{0,12},{2,14},{1,13},{3,15},{16,28},{18,30},{17,29},{19,31}} | collective-permute-start | bytes 49160 | tf_op jit(solution)/shard_map/ppermute | solution.py:592
  122.8 1.3 %collective-permute-done.13 = bf16[4,16,128]{2,1,0:T(8,128)(2,1)S(1)} collective-permute-done((bf16[4,16,128]{2,1,0:T(8,128)(2,1)S(1)}, bf16[4,16,128]{2,1,0:T(8,128)(2,1)S(1)}, u32[]{:S(2)}, u32[]{:S(2)}) %collective-permute-start.13) | collective-permute-done | bytes 16416 | tf_op jit(solution)/shard_map/ppermute | solution.py:592
  124.1 0.3 reshape.25
  124.4 1.0 copy.43
  125.8 1.1 reshape.28
  (28 shorter events, 1.2 us)
Async XLA Ops:
  0.7 1.2 copy-start
  2.4 13.8 %collective-permute-start.1 = (bf16[3,896,128]{2,1,0:T(8,128)(2,1)S(1)}, bf16[3,896,128]{2,1,0:T(8,128)(2,1)S(1)}, u32[]{:S(2)}, u32[]{:S(2)}) collective-permute-start(bf16[3,896,128]{2,1,0:T(8,128)(2,1)S(1)} %shard_map.64.refs_1_.refs_2_), channel_id=1, source_target_pairs={{4,0},{6,2},{8,4},{10,6},{12,8},{14,10},{0,3},{2,1},{20,16},{22,18... | collective-permute-start | bytes 2064392 | tf_op jit(solution)/shard_map/ppermute | solution.py:519
  8.2 1.4 %collective-permute-start = (f32[4,3,8,256]{3,2,1,0:T(8,128)S(1)}, f32[4,3,8,256]{3,2,1,0:T(8,128)S(1)}, u32[]{:S(2)}, u32[]{:S(2)}) collective-permute-start(f32[4,3,8,256]{3,2,1,0:T(8,128)S(1)} %reshape.24.kept_ref), channel_id=1, source_target_pairs={{0,1},{1,0},{2,3},{3,2},{4,5},{5,4},{6,7},{7,6},{8,9},{9,8},{10,11... | collective-permute-start | bytes 294920 | tf_op jit(solution)/shard_map/ppermute | solution.py:486
  9.6 0.7 copy-start.1
  10.2 0.7 copy-start.2
  10.9 0.7 copy-start.3
  16.3 4.0 %collective-permute-start.3 = (bf16[3,896,128]{2,1,0:T(8,128)(2,1)S(1)}, bf16[3,896,128]{2,1,0:T(8,128)(2,1)S(1)}, u32[]{:S(2)}, u32[]{:S(2)}) collective-permute-start(bf16[3,896,128]{2,1,0:T(8,128)(2,1)S(1)} %collective-permute-done.1.refs_4_.refs_1_), channel_id=1, source_target_pairs={{0,1},{1,0},{2,3},{3,2},{4,5},{5,4},{6,7},{7,6},{8,9},{9,8},{10,11... | collective-permute-start | bytes 2064392 | tf_op jit(solution)/shard_map/ppermute | solution.py:486
  16.3 14.9 %collective-permute-start.2 = (bf16[3,896,128]{2,1,0:T(8,128)(2,1)S(1)}, bf16[3,896,128]{2,1,0:T(8,128)(2,1)S(1)}, u32[]{:S(2)}, u32[]{:S(2)}) collective-permute-start(bf16[3,896,128]{2,1,0:T(8,128)(2,1)S(1)} %collective-permute-done.1.refs_4_.refs_1_), channel_id=1, source_target_pairs={{4,0},{6,2},{8,4},{10,6},{0,3},{2,1},{20,16},{22,18},{24,20},{26,2... | collective-permute-start | bytes 2064392 | tf_op jit(solution)/shard_map/ppermute | solution.py:519
  31.3 2.4 %collective-permute-start.5 = (bf16[3,896,128]{2,1,0:T(8,128)(2,1)S(1)}, bf16[3,896,128]{2,1,0:T(8,128)(2,1)S(1)}, u32[]{:S(2)}, u32[]{:S(2)}) collective-permute-start(bf16[3,896,128]{2,1,0:T(8,128)(2,1)S(1)} %collective-permute-done.2.refs_4_.refs_1_), channel_id=1, source_target_pairs={{0,1},{1,0},{2,3},{3,2},{4,5},{5,4},{6,7},{7,6},{8,9},{9,8},{10,11... | collective-permute-start | bytes 2064392 | tf_op jit(solution)/shard_map/ppermute | solution.py:486
  31.4 13.3 %collective-permute-start.4 = (bf16[3,896,128]{2,1,0:T(8,128)(2,1)S(1)}, bf16[3,896,128]{2,1,0:T(8,128)(2,1)S(1)}, u32[]{:S(2)}, u32[]{:S(2)}) collective-permute-start(bf16[3,896,128]{2,1,0:T(8,128)(2,1)S(1)} %collective-permute-done.2.refs_4_.refs_1_), channel_id=1, source_target_pairs={{4,0},{6,2},{0,3},{2,1},{20,16},{22,18},{16,19},{18,17}} | collective-permute-start | bytes 2064392 | tf_op jit(solution)/shard_map/ppermute | solution.py:519
  44.6 4.3 %collective-permute-start.6 = (bf16[3,896,128]{2,1,0:T(8,128)(2,1)S(1)}, bf16[3,896,128]{2,1,0:T(8,128)(2,1)S(1)}, u32[]{:S(2)}, u32[]{:S(2)}) collective-permute-start(bf16[3,896,128]{2,1,0:T(8,128)(2,1)S(1)} %collective-permute-done.4.refs_4_.refs_1_), channel_id=1, source_target_pairs={{0,1},{1,0},{2,3},{3,2},{4,5},{5,4},{6,7},{7,6},{8,9},{9,8},{10,11... | collective-permute-start | bytes 2064392 | tf_op jit(solution)/shard_map/ppermute | solution.py:486
  44.7 15.1 %collective-permute-start.7 = (bf16[3,896,128]{2,1,0:T(8,128)(2,1)S(1)}, bf16[3,896,128]{2,1,0:T(8,128)(2,1)S(1)}, u32[]{:S(2)}, u32[]{:S(2)}) collective-permute-start(bf16[3,896,128]{2,1,0:T(8,128)(2,1)S(1)} %collective-permute-done.4.refs_4_.refs_1_), channel_id=1, source_target_pairs={{0,3},{2,1},{16,19},{18,17}} | collective-permute-start | bytes 2064392 | tf_op jit(solution)/shard_map/ppermute | solution.py:519
  59.9 2.2 %collective-permute-start.8 = (bf16[3,896,128]{2,1,0:T(8,128)(2,1)S(1)}, bf16[3,896,128]{2,1,0:T(8,128)(2,1)S(1)}, u32[]{:S(2)}, u32[]{:S(2)}) collective-permute-start(bf16[3,896,128]{2,1,0:T(8,128)(2,1)S(1)} %collective-permute-done.7.refs_4_), channel_id=1, source_target_pairs={{0,1},{1,0},{2,3},{3,2},{4,5},{5,4},{6,7},{7,6},{8,9},{9,8},{10,11... | collective-permute-start | bytes 2064392 | tf_op jit(solution)/shard_map/ppermute | solution.py:486
  111.6 1.3 %collective-permute-start.9 = (bf16[128,128]{1,0:T(8,128)(2,1)S(1)}, bf16[128,128]{1,0:T(8,128)(2,1)S(1)}, u32[]{:S(2)}, u32[]{:S(2)}) collective-permute-start(bf16[128,128]{1,0:T(8,128)(2,1)S(1)} %get-tuple-element.62), channel_id=1, source_target_pairs={{0,1},{1,0},{2,3},{3,2},{4,5},{5,4},{6,7},{7,6},{8,9},{9,8},{10,11... | collective-permute-start | bytes 98312 | tf_op jit(solution)/shard_map/ppermute | solution.py:486
  112.9 5.8 %collective-permute-start.10 = (bf16[2,4,16,128]{3,2,1,0:T(8,128)(2,1)S(1)}, bf16[2,4,16,128]{3,2,1,0:T(8,128)(2,1)S(1)}, u32[]{:S(2)}, u32[]{:S(2)}) collective-permute-start(bf16[2,4,16,128]{3,2,1,0:T(8,128)(2,1)S(1)} %get-tuple-element.67), channel_id=1, source_target_pairs={{0,2},{2,0},{1,3},{3,1},{16,18},{18,16},{17,19},{19,17}} | collective-permute-start | bytes 98312 | tf_op jit(solution)/shard_map/ppermute | solution.py:587
  118.8 3.9 %collective-permute-start.11 = (bf16[4,16,128]{2,1,0:T(8,128)(2,1)S(1)}, bf16[4,16,128]{2,1,0:T(8,128)(2,1)S(1)}, u32[]{:S(2)}, u32[]{:S(2)}) collective-permute-start(bf16[4,16,128]{2,1,0:T(8,128)(2,1)S(1)} %get-tuple-element.63), channel_id=1, source_target_pairs={{0,4},{2,6},{1,5},{3,7},{16,20},{18,22},{17,21},{19,23}} | collective-permute-start | bytes 49160 | tf_op jit(solution)/shard_map/ppermute | solution.py:592
  120.1 2.7 %collective-permute-start.12 = (bf16[4,16,128]{2,1,0:T(8,128)(2,1)S(1)}, bf16[4,16,128]{2,1,0:T(8,128)(2,1)S(1)}, u32[]{:S(2)}, u32[]{:S(2)}) collective-permute-start(bf16[4,16,128]{2,1,0:T(8,128)(2,1)S(1)} %get-tuple-element.65), channel_id=1, source_target_pairs={{0,8},{2,10},{1,9},{3,11},{16,24},{18,26},{17,25},{19,27}} | collective-permute-start | bytes 49160 | tf_op jit(solution)/shard_map/ppermute | solution.py:592
  121.4 2.7 %collective-permute-start.13 = (bf16[4,16,128]{2,1,0:T(8,128)(2,1)S(1)}, bf16[4,16,128]{2,1,0:T(8,128)(2,1)S(1)}, u32[]{:S(2)}, u32[]{:S(2)}) collective-permute-start(bf16[4,16,128]{2,1,0:T(8,128)(2,1)S(1)} %get-tuple-element.64), channel_id=1, source_target_pairs={{0,12},{2,14},{1,13},{3,15},{16,28},{18,30},{17,29},{19,31}} | collective-permute-start | bytes 49160 | tf_op jit(solution)/shard_map/ppermute | solution.py:592

commit v2 on v1

--- a/solution.py
+++ b/solution.py
@@ -222,7 +222,7 @@
             waiting.append((index, tile, (base, base + 1)))
             if at == 2 and index < 3:
                 push(index + 1)
-            if len(waiting) == 3:
+            if len(waiting) == 7:
                 take()
     while waiting:
         take()

time: 127 us -> 127 us (level)
  no operation moved by 1% of the time
where the time goes in v2:
time: 127 us
  Pallas kernels  84.5 us (67%)
  starting transfers between devices  21.1 us (17%)
  waiting for transfers between devices  12.5 us (10%)
  local copies, waits for them, and re-layouts  7.93 us (6%)
    pallas_call x4, Pallas kernels, shards(): pl.pallas_call(functools.partial(level_kernel, level), out_shape=(w_shape...  43.8 us
    pallas_call x1, Pallas kernels, shards(): pl.pallas_call(second_kernel, grid=(segments,), out_shape=h_shape, in_spe...  36.9 us
    ppermute x4, starting transfers between devices, hand_on(): return lax.ppermute(value, ('segment', 'slab'), pairs)  14.7 us
    unnamed x10, local copies, waits for them, and re-layouts  4.88 us
    ppermute x6, waiting for transfers between devices, between_cores(): return lax.ppermute(value, 'slab', swap)  4.4 us
    ppermute x3, starting transfers between devices, shards(): out = out + lax.ppermute(crops[:, level], 'segment', pairs)  3.87 us
    ppermute x1, waiting for transfers between devices, shards(): lax.ppermute(lax.dynamic_index_in_dim(pair, 1 - line, 2, keepdims=False),...  3.75 us
    ppermute x4, waiting for transfers between devices, hand_on(): return lax.ppermute(value, ('segment', 'slab'), pairs)  2.94 us
  transfers between devices with their start and end apart: 14, of which 7 were waited for; matrix products, arithmetic and copies ran while one was open for 1% of the time, Pallas kernels for 27%

profile of v2, /device:TPU:0, one launch (start us, length us, event | category | flops | bytes accessed | tf_op | source)
XLA Modules:
  0.0 126.7 jit_solution(3858813633642659760)
XLA Ops:
  0.0 0.7 copy.47
  0.7 1.2 copy-done
  1.9 0.5 shard_map.64.refs_1_.refs_2_
  2.4 4.3 %collective-permute-start.1 = (bf16[3,896,128]{2,1,0:T(8,128)(2,1)S(1)}, bf16[3,896,128]{2,1,0:T(8,128)(2,1)S(1)}, u32[]{:S(2)}, u32[]{:S(2)}) collective-permute-start(bf16[3,896,128]{2,1,0:T(8,128)(2,1)S(1)} %shard_map.64.refs_1_.refs_2_), channel_id=1, source_target_pairs={{4,0},{6,2},{8,4},{10,6},{12,8},{14,10},{0,3},{2,1},{20,16},{22,18... | collective-permute-start | bytes 2064392 | tf_op jit(solution)/shard_map/ppermute | solution.py:519
  6.8 1.4 %reshape.24.kept_ref = f32[4,3,8,256]{3,2,1,0:T(8,128)S(1)} reshape(f32[4,3,8,16,16]{4,3,2,1,0:T(8,128)} %param.6) | data formatting | bytes 196608 | tf_op jit(solution)/shard_map/reshape | solution.py:496
  8.4 1.2 collective-permute-done.got_ref
  9.6 0.7 copy-done.1
  10.2 0.7 copy-done.2
  10.9 0.7 copy-done.3
  11.6 1.7 %shard_map.65 = (f32[16,2048]{1,0:T(8,128)S(1)}, bf16[48,128]{1,0:T(8,128)(2,1)S(1)}, bf16[48,128]{1,0:T(8,128)(2,1)S(1)}, bf16[8,16,16,128]{3,2,1,0:T(8,128)(2,1)S(1)}) custom-call(s32[3]{0:T(128)S(1)} %pad_add_fusion.ids_ref.refs_0_, s32[4,3]{1,0:T(4,128)S(1)} %copy-done.2, f32[4,3,8,256]{3,2,1,0:T(8,128)S(1)} %reshape.24.kept_ref, ...), custom_call_target="tpu_custom_call" | custom-call | tf_op jit(solution)/shard_map/pallas_call | solution.py:499
  13.3 2.9 %collective-permute-done.1.refs_4_.refs_1_ = bf16[3,896,128]{2,1,0:T(8,128)(2,1)S(1)} collective-permute-done((bf16[3,896,128]{2,1,0:T(8,128)(2,1)S(1)}, bf16[3,896,128]{2,1,0:T(8,128)(2,1)S(1)}, u32[]{:S(2)}, u32[]{:S(2)}) %collective-permute-start.1) | collective-permute-done | bytes 688160 | tf_op jit(solution)/shard_map/ppermute | solution.py:519
  16.3 3.9 %collective-permute-start.2 = (bf16[3,896,128]{2,1,0:T(8,128)(2,1)S(1)}, bf16[3,896,128]{2,1,0:T(8,128)(2,1)S(1)}, u32[]{:S(2)}, u32[]{:S(2)}) collective-permute-start(bf16[3,896,128]{2,1,0:T(8,128)(2,1)S(1)} %collective-permute-done.1.refs_4_.refs_1_), channel_id=1, source_target_pairs={{4,0},{6,2},{8,4},{10,6},{0,3},{2,1},{20,16},{22,18},{24,20},{26,2... | collective-permute-start | bytes 2064392 | tf_op jit(solution)/shard_map/ppermute | solution.py:519
  20.3 11.0 %shard_map.66 = (bf16[8,2,4,256,384]{4,3,2,1,0:T(8,128)(2,1)}, bf16[8,1024,768]{2,1,0:T(8,128)(2,1)}, f32[8,3,8,128]{3,2,1,0:T(8,128)S(1)}, bf16[8,16,16,128]{3,2,1,0:T(8,128)(2,1)S(1)}) custom-call(s32[3]{0:T(128)S(1)} %pad_add_fusion.ids_ref.refs_0_, bf16[3,896,128]{2,1,0:T(8,128)(2,1)S(1)} %shard_map.64.refs_1_.refs_2_, ...), custom_call_target="tpu_custom_call" | custom-call | flops 6442450944 | bytes 4194304 | tf_op jit(solution)/shard_map/pallas_call | solution.py:528
  31.3 2.3 %collective-permute-start.4 = (bf16[3,896,128]{2,1,0:T(8,128)(2,1)S(1)}, bf16[3,896,128]{2,1,0:T(8,128)(2,1)S(1)}, u32[]{:S(2)}, u32[]{:S(2)}) collective-permute-start(bf16[3,896,128]{2,1,0:T(8,128)(2,1)S(1)} %collective-permute-done.2.refs_4_.refs_1_), channel_id=1, source_target_pairs={{4,0},{6,2},{0,3},{2,1},{20,16},{22,18},{16,19},{18,17}} | collective-permute-start | bytes 2064392 | tf_op jit(solution)/shard_map/ppermute | solution.py:519
  33.6 10.9 %shard_map.67 = (bf16[8,2,4,256,384]{4,3,2,1,0:T(8,128)(2,1)}, bf16[8,1024,768]{2,1,0:T(8,128)(2,1)}, f32[8,3,8,128]{3,2,1,0:T(8,128)S(1)}, bf16[8,16,16,128]{3,2,1,0:T(8,128)(2,1)S(1)}) custom-call(s32[3]{0:T(128)S(1)} %pad_add_fusion.ids_ref.refs_0_, ...), custom_call_target="tpu_custom_call", output_to_operand_aliasing={{0}: (6, {}), {1}: (7, {}), {2}: (8, {})} | custom-call | flops 6442450944 | bytes 4194304 | tf_op jit(solution)/shard_map/pallas_call | solution.py:528
  44.7 4.1 %collective-permute-start.7 = (bf16[3,896,128]{2,1,0:T(8,128)(2,1)S(1)}, bf16[3,896,128]{2,1,0:T(8,128)(2,1)S(1)}, u32[]{:S(2)}, u32[]{:S(2)}) collective-permute-start(bf16[3,896,128]{2,1,0:T(8,128)(2,1)S(1)} %collective-permute-done.4.refs_4_.refs_1_), channel_id=1, source_target_pairs={{0,3},{2,1},{16,19},{18,17}} | collective-permute-start | bytes 2064392 | tf_op jit(solution)/shard_map/ppermute | solution.py:519
  48.8 10.9 %shard_map.68 = (bf16[8,2,4,256,384]{4,3,2,1,0:T(8,128)(2,1)}, bf16[8,1024,768]{2,1,0:T(8,128)(2,1)}, f32[8,3,8,128]{3,2,1,0:T(8,128)S(1)}, bf16[8,16,16,128]{3,2,1,0:T(8,128)(2,1)S(1)}) custom-call(s32[3]{0:T(128)S(1)} %pad_add_fusion.ids_ref.refs_0_, ...), custom_call_target="tpu_custom_call", output_to_operand_aliasing={{0}: (6, {}), {1}: (7, {}), {2}: (8, {})} | custom-call | flops 6442450944 | bytes 4194304 | tf_op jit(solution)/shard_map/pallas_call | solution.py:528
  59.8 2.1 %collective-permute-done.8.refs_3_ = bf16[3,896,128]{2,1,0:T(8,128)(2,1)S(1)} collective-permute-done((bf16[3,896,128]{2,1,0:T(8,128)(2,1)S(1)}, bf16[3,896,128]{2,1,0:T(8,128)(2,1)S(1)}, u32[]{:S(2)}, u32[]{:S(2)}) %collective-permute-start.8) | collective-permute-done | bytes 688160 | tf_op jit(solution)/shard_map/ppermute | solution.py:486
  62.0 11.0 %shard_map.69 = (bf16[8,2,4,256,384]{4,3,2,1,0:T(8,128)(2,1)}, bf16[8,1024,768]{2,1,0:T(8,128)(2,1)}, f32[8,3,8,128]{3,2,1,0:T(8,128)S(1)}, bf16[8,16,16,128]{3,2,1,0:T(8,128)(2,1)S(1)}) custom-call(s32[3]{0:T(128)S(1)} %pad_add_fusion.ids_ref.refs_0_, ...), custom_call_target="tpu_custom_call", output_to_operand_aliasing={{0}: (6, {}), {1}: (7, {}), {2}: (8, {})} | custom-call | flops 6442450944 | bytes 4194304 | tf_op jit(solution)/shard_map/pallas_call | solution.py:528
  72.9 0.6 shard_map.70
  73.6 36.9 %shard_map.71.hidden_ref = bf16[8,16,16,128]{3,2,1,0:T(8,128)(2,1)S(1)} custom-call(bf16[8,16,16,128]{3,2,1,0:T(8,128)(2,1)S(1)} %get-tuple-element.57.entry, bf16[8,2,4,256,384]{4,3,2,1,0:T(8,128)(2,1)} %get-tuple-element.58.w_ref, bf16[8,1024,768]{2,1,0:T(8,128)(2,1)} %get-tuple-element.59.c_ref, f32[8,3,8,128]{3,2,1,0:T(8,128)S(1)} %get-tuple-element.60.b_ref), custom_call_target="tpu_custom_call" | custom-call | flops 25769803776 | bytes 16777216 | tf_op jit(solution)/shard_map/pallas_call | solution.py:558
  110.4 1.0 shard_map.72
  111.6 1.1 collective-permute-done.9
  112.8 2.0 %collective-permute-start.10 = (bf16[2,4,16,128]{3,2,1,0:T(8,128)(2,1)S(1)}, bf16[2,4,16,128]{3,2,1,0:T(8,128)(2,1)S(1)}, u32[]{:S(2)}, u32[]{:S(2)}) collective-permute-start(bf16[2,4,16,128]{3,2,1,0:T(8,128)(2,1)S(1)} %get-tuple-element.67), channel_id=1, source_target_pairs={{0,2},{2,0},{1,3},{3,1},{16,18},{18,16},{17,19},{19,17}} | collective-permute-start | bytes 98312 | tf_op jit(solution)/shard_map/ppermute | solution.py:587
  114.8 3.8 %collective-permute-done.10 = bf16[2,4,16,128]{3,2,1,0:T(8,128)(2,1)S(1)} collective-permute-done((bf16[2,4,16,128]{3,2,1,0:T(8,128)(2,1)S(1)}, bf16[2,4,16,128]{3,2,1,0:T(8,128)(2,1)S(1)}, u32[]{:S(2)}, u32[]{:S(2)}) %collective-permute-start.10) | collective-permute-done | bytes 32800 | tf_op jit(solution)/shard_map/ppermute | solution.py:587
  118.6 1.3 %collective-permute-start.11 = (bf16[4,16,128]{2,1,0:T(8,128)(2,1)S(1)}, bf16[4,16,128]{2,1,0:T(8,128)(2,1)S(1)}, u32[]{:S(2)}, u32[]{:S(2)}) collective-permute-start(bf16[4,16,128]{2,1,0:T(8,128)(2,1)S(1)} %get-tuple-element.63), channel_id=1, source_target_pairs={{0,4},{2,6},{1,5},{3,7},{16,20},{18,22},{17,21},{19,23}} | collective-permute-start | bytes 49160 | tf_op jit(solution)/shard_map/ppermute | solution.py:592
  119.9 1.3 %collective-permute-start.12 = (bf16[4,16,128]{2,1,0:T(8,128)(2,1)S(1)}, bf16[4,16,128]{2,1,0:T(8,128)(2,1)S(1)}, u32[]{:S(2)}, u32[]{:S(2)}) collective-permute-start(bf16[4,16,128]{2,1,0:T(8,128)(2,1)S(1)} %get-tuple-element.65), channel_id=1, source_target_pairs={{0,8},{2,10},{1,9},{3,11},{16,24},{18,26},{17,25},{19,27}} | collective-permute-start | bytes 49160 | tf_op jit(solution)/shard_map/ppermute | solution.py:592
  121.2 1.3 %collective-permute-start.13 = (bf16[4,16,128]{2,1,0:T(8,128)(2,1)S(1)}, bf16[4,16,128]{2,1,0:T(8,128)(2,1)S(1)}, u32[]{:S(2)}, u32[]{:S(2)}) collective-permute-start(bf16[4,16,128]{2,1,0:T(8,128)(2,1)S(1)} %get-tuple-element.64), channel_id=1, source_target_pairs={{0,12},{2,14},{1,13},{3,15},{16,28},{18,30},{17,29},{19,31}} | collective-permute-start | bytes 49160 | tf_op jit(solution)/shard_map/ppermute | solution.py:592
  122.6 1.3 %collective-permute-done.13 = bf16[4,16,128]{2,1,0:T(8,128)(2,1)S(1)} collective-permute-done((bf16[4,16,128]{2,1,0:T(8,128)(2,1)S(1)}, bf16[4,16,128]{2,1,0:T(8,128)(2,1)S(1)}, u32[]{:S(2)}, u32[]{:S(2)}) %collective-permute-start.13) | collective-permute-done | bytes 16416 | tf_op jit(solution)/shard_map/ppermute | solution.py:592
  123.9 0.3 reshape.25
  124.3 1.0 copy.43
  125.6 1.1 reshape.28
  (28 shorter events, 1.2 us)
Async XLA Ops:
  0.7 1.2 copy-start
  2.4 13.8 %collective-permute-start.1 = (bf16[3,896,128]{2,1,0:T(8,128)(2,1)S(1)}, bf16[3,896,128]{2,1,0:T(8,128)(2,1)S(1)}, u32[]{:S(2)}, u32[]{:S(2)}) collective-permute-start(bf16[3,896,128]{2,1,0:T(8,128)(2,1)S(1)} %shard_map.64.refs_1_.refs_2_), channel_id=1, source_target_pairs={{4,0},{6,2},{8,4},{10,6},{12,8},{14,10},{0,3},{2,1},{20,16},{22,18... | collective-permute-start | bytes 2064392 | tf_op jit(solution)/shard_map/ppermute | solution.py:519
  8.2 1.4 %collective-permute-start = (f32[4,3,8,256]{3,2,1,0:T(8,128)S(1)}, f32[4,3,8,256]{3,2,1,0:T(8,128)S(1)}, u32[]{:S(2)}, u32[]{:S(2)}) collective-permute-start(f32[4,3,8,256]{3,2,1,0:T(8,128)S(1)} %reshape.24.kept_ref), channel_id=1, source_target_pairs={{0,1},{1,0},{2,3},{3,2},{4,5},{5,4},{6,7},{7,6},{8,9},{9,8},{10,11... | collective-permute-start | bytes 294920 | tf_op jit(solution)/shard_map/ppermute | solution.py:486
  9.6 0.7 copy-start.1
  10.2 0.7 copy-start.2
  10.9 0.7 copy-start.3
  16.3 4.0 %collective-permute-start.3 = (bf16[3,896,128]{2,1,0:T(8,128)(2,1)S(1)}, bf16[3,896,128]{2,1,0:T(8,128)(2,1)S(1)}, u32[]{:S(2)}, u32[]{:S(2)}) collective-permute-start(bf16[3,896,128]{2,1,0:T(8,128)(2,1)S(1)} %collective-permute-done.1.refs_4_.refs_1_), channel_id=1, source_target_pairs={{0,1},{1,0},{2,3},{3,2},{4,5},{5,4},{6,7},{7,6},{8,9},{9,8},{10,11... | collective-permute-start | bytes 2064392 | tf_op jit(solution)/shard_map/ppermute | solution.py:486
  16.3 14.9 %collective-permute-start.2 = (bf16[3,896,128]{2,1,0:T(8,128)(2,1)S(1)}, bf16[3,896,128]{2,1,0:T(8,128)(2,1)S(1)}, u32[]{:S(2)}, u32[]{:S(2)}) collective-permute-start(bf16[3,896,128]{2,1,0:T(8,128)(2,1)S(1)} %collective-permute-done.1.refs_4_.refs_1_), channel_id=1, source_target_pairs={{4,0},{6,2},{8,4},{10,6},{0,3},{2,1},{20,16},{22,18},{24,20},{26,2... | collective-permute-start | bytes 2064392 | tf_op jit(solution)/shard_map/ppermute | solution.py:519
  31.2 2.4 %collective-permute-start.5 = (bf16[3,896,128]{2,1,0:T(8,128)(2,1)S(1)}, bf16[3,896,128]{2,1,0:T(8,128)(2,1)S(1)}, u32[]{:S(2)}, u32[]{:S(2)}) collective-permute-start(bf16[3,896,128]{2,1,0:T(8,128)(2,1)S(1)} %collective-permute-done.2.refs_4_.refs_1_), channel_id=1, source_target_pairs={{0,1},{1,0},{2,3},{3,2},{4,5},{5,4},{6,7},{7,6},{8,9},{9,8},{10,11... | collective-permute-start | bytes 2064392 | tf_op jit(solution)/shard_map/ppermute | solution.py:486
  31.3 13.2 %collective-permute-start.4 = (bf16[3,896,128]{2,1,0:T(8,128)(2,1)S(1)}, bf16[3,896,128]{2,1,0:T(8,128)(2,1)S(1)}, u32[]{:S(2)}, u32[]{:S(2)}) collective-permute-start(bf16[3,896,128]{2,1,0:T(8,128)(2,1)S(1)} %collective-permute-done.2.refs_4_.refs_1_), channel_id=1, source_target_pairs={{4,0},{6,2},{0,3},{2,1},{20,16},{22,18},{16,19},{18,17}} | collective-permute-start | bytes 2064392 | tf_op jit(solution)/shard_map/ppermute | solution.py:519
  44.6 4.2 %collective-permute-start.6 = (bf16[3,896,128]{2,1,0:T(8,128)(2,1)S(1)}, bf16[3,896,128]{2,1,0:T(8,128)(2,1)S(1)}, u32[]{:S(2)}, u32[]{:S(2)}) collective-permute-start(bf16[3,896,128]{2,1,0:T(8,128)(2,1)S(1)} %collective-permute-done.4.refs_4_.refs_1_), channel_id=1, source_target_pairs={{0,1},{1,0},{2,3},{3,2},{4,5},{5,4},{6,7},{7,6},{8,9},{9,8},{10,11... | collective-permute-start | bytes 2064392 | tf_op jit(solution)/shard_map/ppermute | solution.py:486
  44.7 15.1 %collective-permute-start.7 = (bf16[3,896,128]{2,1,0:T(8,128)(2,1)S(1)}, bf16[3,896,128]{2,1,0:T(8,128)(2,1)S(1)}, u32[]{:S(2)}, u32[]{:S(2)}) collective-permute-start(bf16[3,896,128]{2,1,0:T(8,128)(2,1)S(1)} %collective-permute-done.4.refs_4_.refs_1_), channel_id=1, source_target_pairs={{0,3},{2,1},{16,19},{18,17}} | collective-permute-start | bytes 2064392 | tf_op jit(solution)/shard_map/ppermute | solution.py:519
  59.7 2.2 %collective-permute-start.8 = (bf16[3,896,128]{2,1,0:T(8,128)(2,1)S(1)}, bf16[3,896,128]{2,1,0:T(8,128)(2,1)S(1)}, u32[]{:S(2)}, u32[]{:S(2)}) collective-permute-start(bf16[3,896,128]{2,1,0:T(8,128)(2,1)S(1)} %collective-permute-done.7.refs_4_), channel_id=1, source_target_pairs={{0,1},{1,0},{2,3},{3,2},{4,5},{5,4},{6,7},{7,6},{8,9},{9,8},{10,11... | collective-permute-start | bytes 2064392 | tf_op jit(solution)/shard_map/ppermute | solution.py:486
  111.4 1.3 %collective-permute-start.9 = (bf16[128,128]{1,0:T(8,128)(2,1)S(1)}, bf16[128,128]{1,0:T(8,128)(2,1)S(1)}, u32[]{:S(2)}, u32[]{:S(2)}) collective-permute-start(bf16[128,128]{1,0:T(8,128)(2,1)S(1)} %get-tuple-element.62), channel_id=1, source_target_pairs={{0,1},{1,0},{2,3},{3,2},{4,5},{5,4},{6,7},{7,6},{8,9},{9,8},{10,11... | collective-permute-start | bytes 98312 | tf_op jit(solution)/shard_map/ppermute | solution.py:486
  112.8 5.8 %collective-permute-start.10 = (bf16[2,4,16,128]{3,2,1,0:T(8,128)(2,1)S(1)}, bf16[2,4,16,128]{3,2,1,0:T(8,128)(2,1)S(1)}, u32[]{:S(2)}, u32[]{:S(2)}) collective-permute-start(bf16[2,4,16,128]{3,2,1,0:T(8,128)(2,1)S(1)} %get-tuple-element.67), channel_id=1, source_target_pairs={{0,2},{2,0},{1,3},{3,1},{16,18},{18,16},{17,19},{19,17}} | collective-permute-start | bytes 98312 | tf_op jit(solution)/shard_map/ppermute | solution.py:587
  118.6 3.9 %collective-permute-start.11 = (bf16[4,16,128]{2,1,0:T(8,128)(2,1)S(1)}, bf16[4,16,128]{2,1,0:T(8,128)(2,1)S(1)}, u32[]{:S(2)}, u32[]{:S(2)}) collective-permute-start(bf16[4,16,128]{2,1,0:T(8,128)(2,1)S(1)} %get-tuple-element.63), channel_id=1, source_target_pairs={{0,4},{2,6},{1,5},{3,7},{16,20},{18,22},{17,21},{19,23}} | collective-permute-start | bytes 49160 | tf_op jit(solution)/shard_map/ppermute | solution.py:592
  119.9 2.7 %collective-permute-start.12 = (bf16[4,16,128]{2,1,0:T(8,128)(2,1)S(1)}, bf16[4,16,128]{2,1,0:T(8,128)(2,1)S(1)}, u32[]{:S(2)}, u32[]{:S(2)}) collective-permute-start(bf16[4,16,128]{2,1,0:T(8,128)(2,1)S(1)} %get-tuple-element.65), channel_id=1, source_target_pairs={{0,8},{2,10},{1,9},{3,11},{16,24},{18,26},{17,25},{19,27}} | collective-permute-start | bytes 49160 | tf_op jit(solution)/shard_map/ppermute | solution.py:592
  121.2 2.7 %collective-permute-start.13 = (bf16[4,16,128]{2,1,0:T(8,128)(2,1)S(1)}, bf16[4,16,128]{2,1,0:T(8,128)(2,1)S(1)}, u32[]{:S(2)}, u32[]{:S(2)}) collective-permute-start(bf16[4,16,128]{2,1,0:T(8,128)(2,1)S(1)} %get-tuple-element.64), channel_id=1, source_target_pairs={{0,12},{2,14},{1,13},{3,15},{16,28},{18,30},{17,29},{19,31}} | collective-permute-start | bytes 49160 | tf_op jit(solution)/shard_map/ppermute | solution.py:592

commit v3 on v0

--- a/solution.py
+++ b/solution.py
@@ -26,7 +26,7 @@
 )
 
 
-GROUPS = ((0,), (1,), (2,), (3,))
+GROUPS = ((0, 1), (2, 3))
 
 
 def neighbour(layer, tile, step):
@@ -42,10 +42,17 @@
     return lax.dot_general(a, b, (((1,), (1,)), ((), ())), preferred_element_type=jnp.float32)
 
 
-def pack_kernel(raw_ref, bias_ref, eye_ref, packed):
-    eye = eye_ref[...]
+def pack_kernel(raw_hbm, bias_hbm, packed, raw_ref, bias_ref, sems):
+    copies = [pltpu.make_async_copy(raw_hbm.at[0, i], raw_ref.at[i], sems.at[i]) for i in range(LAYERS)]
+    copies.append(pltpu.make_async_copy(bias_hbm, bias_ref, sems.at[LAYERS]))
+    for copy in copies:
+        copy.start()
+    row = lax.broadcasted_iota(jnp.int32, (192, 192), 0)
+    eye = jnp.where(row == lax.broadcasted_iota(jnp.int32, (192, 192), 1), 1.0, 0.0).astype(jnp.bfloat16)
     low = low_lanes((CH, 128))
+    copies[LAYERS].wait()
     for layer in range(LAYERS):
+        copies[layer].wait()
         for ty in range(3):
             pair = jnp.concatenate([raw_ref[layer, 3 + ty], raw_ref[layer, ty]], axis=0)
             packed[layer, ty * 192 : (ty + 1) * 192, :] = nt_dot(eye, pair).astype(jnp.bfloat16)
@@ -54,7 +61,7 @@
         pair = jnp.concatenate([raw_ref[layer, 8], raw_ref[layer, 8]], axis=0)
         twice = nt_dot(eye, pair)
         packed[layer, 768:832, :] = jnp.where(low, twice[0:64], twice[64:128]).astype(jnp.bfloat16)
-        terms = [term.astype(jnp.float32) for term in split_terms(bias_ref[layer : layer + 1, :])]
+        terms = [term.astype(jnp.float32) for term in split_terms(bias_ref[layer])]
         terms = jnp.concatenate(terms + [jnp.zeros((CH - 3, CH), jnp.float32)], axis=0)
         terms = jnp.concatenate([terms, terms], axis=1)
         packed[layer, 832:896, :] = jnp.where(low, twice[128:192], terms).astype(jnp.bfloat16)
@@ -256,11 +263,11 @@
         s_a[...] = refs[8][...].astype(jnp.float32)
     state, v_refs = (s_a, s_b, s_c, s_d), (v_a, v_b, v_c)
 
-    def copies(turn):
+    def copy(turn, part):
         at = 2 * level + turn
-        pairs = [pltpu.make_async_copy(w_pair.at[turn, i], w_out.at[at, i], sems.at[turn, i]) for i in range(2)]
-        cycle = pltpu.make_async_copy(w_cycle.at[turn], c_out.at[at], sems.at[turn, 2])
-        return pairs + [cycle, pltpu.make_async_copy(b_all.at[turn], b_out.at[at], sems.at[turn, 3])]
+        source = (w_pair.at[turn, 0], w_pair.at[turn, 1], w_cycle.at[turn], b_all.at[turn])[part]
+        target = (w_out.at[at, 0], w_out.at[at, 1], c_out.at[at], b_out.at[at])[part]
+        return pltpu.make_async_copy(source, target, sems.at[turn, part])
 
     def section(turn, unused):
         for wanted, sources in ((True, (own_0, own_1)), (False, (far_0, far_1))):
@@ -274,18 +281,18 @@
 
         def prepare(layer):
             expand(packed.at[layer], w_refs[layer], b_all.at[turn, layer], layer)
-            copies(turn)[layer].start()
+            copy(turn, layer).start()
 
         run_section(state, v_refs, w_refs, [b_all.at[turn, i] for i in range(LAYERS)], prepare)
-        copies(turn)[LAYERS].start()
+        copy(turn, LAYERS).start()
         return 0
 
     lax.fori_loop(0, 2, section, 0)
     leaving[...] = s_a[...].astype(jnp.bfloat16)
     x_out[...] = renewed_fields(x, proj_ref, s_a) if last else x
     for turn in range(2):
-        for copy in copies(turn):
-            copy.wait()
+        for part in range(LAYERS + 1):
+            copy(turn, part).wait()
 
 
 def feature_kernel(ids_ref, anchor_ref, kept_ref, got_ref, lift_ref, proj_ref, x_ref, lift_out, proj_out):
@@ -355,6 +362,34 @@
         given[...] = cells_in_rows((x_ref, x_new), 1 - ids_ref[0])
 
 
+def place_kernel(share, *refs):
+    ids_ref, own, *others, out_ref = refs
+    y_cells = out_ref.shape[-1]
+    first = ids_ref[3] == 0
+    got = others[0][...]
+    for other in others[1:]:
+        got = got + other[...]
+    count = 48 * share
+    row = lax.broadcasted_iota(jnp.int32, (count, 128), 0) >> (share.bit_length() - 1)
+    lane = lax.broadcasted_iota(jnp.int32, (count, 128), 1)
+    step = jnp.where(row >= 24, 1, 0)
+    place = step * 64 + (row & 3) * 16 + ((row >> 2) & 1) * 3 + ((row >> 3) - 3 * step)
+    chosen = [jnp.where(lane == place + 8 * upper, 1.0, 0.0).astype(jnp.bfloat16) for upper in range(2)]
+    own_z = lax.broadcasted_iota(jnp.int32, (count, y_cells), 0) & (share - 1)
+    for crop in range(own.shape[0]):
+        piece = jnp.where(first, own[crop].astype(jnp.float32), got[crop].astype(jnp.float32)).astype(jnp.bfloat16)
+        lower, upper = [nt_dot(one, piece) for one in chosen]
+        cells = jnp.zeros((count, y_cells), jnp.float32)
+        for z in range(share):
+            both = jnp.concatenate([lower[:, 8 * z : 8 * z + 8], upper[:, 8 * z : 8 * z + 8]], axis=1)
+            cells = jnp.where(own_z == z, both, cells)
+        for step in range(STEPS):
+            for comp in range(3):
+                for x in range(8):
+                    begin = ((3 * step + comp) * 8 + x) * share
+                    out_ref[step, crop, comp, x] = cells[begin : begin + share]
+
+
 def split_terms(matrix):
     first = matrix.astype(jnp.bfloat16)
     rest = matrix - first.astype(jnp.float32)
@@ -386,7 +421,7 @@
     smem = pl.BlockSpec(memory_space=pltpu.SMEM)
     anyspace = pl.BlockSpec(memory_space=pl.ANY)
     params = pltpu.CompilerParams(vmem_limit_bytes=VMEM_BYTES)
-    ids = jnp.stack([slab_id, line, slot]).astype(jnp.int32)
+    ids = jnp.stack([slab_id, line, slot, segment_id // lines]).astype(jnp.int32)
 
     def after(value, earlier):
         return lax.optimization_barrier((value, earlier))[0]
@@ -397,10 +432,15 @@
     packed = pl.pallas_call(
         pack_kernel,
         out_shape=jax.ShapeDtypeStruct((LAYERS, ROWS, 128), jnp.bfloat16),
-        in_specs=[vmem] * 3,
+        in_specs=[pl.BlockSpec(memory_space=pltpu.HBM)] * 2,
         out_specs=vmem,
+        scratch_shapes=[
+            pltpu.VMEM(conv_weight.shape[1:], jnp.bfloat16),
+            pltpu.VMEM((LAYERS, 1, CH), jnp.float32),
+            pltpu.SemaphoreType.DMA((LAYERS + 1,)),
+        ],
         compiler_params=params,
-    )(conv_weight[0], conv_bias[0], jnp.eye(192, dtype=jnp.bfloat16))
+    )(conv_weight, conv_bias.transpose(1, 0, 2))
 
     flat = after(fields, packed).reshape(crop_count, comps, slab_rows, y_cells * z_cells)
     x, lift, proj = pl.pallas_call(
@@ -482,13 +522,18 @@
     mine = lax.dynamic_index_in_dim(pair, line, 2, keepdims=False)
     got = lax.ppermute(lax.dynamic_index_in_dim(pair, 1 - line, 2, keepdims=False), "segment", swap)
     crops = jnp.where(line == 0, jnp.concatenate([mine, got]), jnp.concatenate([got, mine]))
-    out = jnp.where(segment_id < lines, crops[:, 0], 0)
+    pieces = [crops[:, 0]]
     for level in range(1, levels):
         pairs = [(s, level * lines + s) for s in range(lines)]
-        out = out + lax.ppermute(crops[:, level], "segment", pairs)
-    out = out.reshape(crop_count, share, 8, STEPS, 4, 2, 8)[..., : 2 * comps]
-    out = out.reshape(crop_count, share, 8, STEPS, 4, 2, 2, comps).transpose(3, 0, 7, 6, 4, 5, 2, 1)
-    return out.reshape(STEPS, crop_count, comps, slab_rows, y_cells, share).astype(jnp.float32)
+        pieces.append(lax.ppermute(crops[:, level], "segment", pairs))
+    out = pl.pallas_call(
+        functools.partial(place_kernel, share),
+        out_shape=jax.ShapeDtypeStruct((STEPS, crop_count, comps, slab_rows, share, y_cells), jnp.float32),
+        in_specs=[smem] + [vmem] * levels,
+        out_specs=vmem,
+        compiler_params=params,
+    )(ids, *pieces)
+    return out.transpose(0, 1, 2, 3, 5, 4)
 
 
 def solution(mesh):

time: 122 us -> 124 us (1.016)
  Pallas kernels: 78.8 us -> 83.6 us
  local copies, waits for them, and re-layouts: 7.93 us -> 5.35 us
    pallas_call x1, Pallas kernels: 33.8 us -> 35.8 us  [shards(): pl.pallas_call(second_kernel, grid=(segments,), out_shape=(jax.ShapeDtype...]
    pallas_call x0 -> x1, Pallas kernels: none -> 1.55 us  [shards(): pl.pallas_call(functools.partial(place_kernel, share), out_shape=jax.Shap...]
    convert_element_type x2 -> x0, local copies, waits for them, and re-layouts: 1.26 us -> none  [shards(): out.reshape(STEPS, crop_count, comps, slab_rows, y_cells, share)]
where the time goes in v3:
time: 124 us
  Pallas kernels  83.6 us (67%)
  starting transfers between devices  21.1 us (17%)
  waiting for transfers between devices  13.2 us (11%)
  local copies, waits for them, and re-layouts  5.35 us (4%)
    pallas_call x4, Pallas kernels, shards(): pl.pallas_call(functools.partial(level_kernel, level, level == 0, level =...  44 us
    pallas_call x1, Pallas kernels, shards(): pl.pallas_call(second_kernel, grid=(segments,), out_shape=(jax.ShapeDtype...  35.8 us
    ppermute x4, starting transfers between devices, hand_on(): return lax.ppermute(value, ('segment', 'slab'), pairs)  14.7 us
    ppermute x6, waiting for transfers between devices, between_cores(): return lax.ppermute(value, 'slab', swap)  4.41 us
    unnamed x10, local copies, waits for them, and re-layouts  3.9 us
    ppermute x3, starting transfers between devices, shards(): pieces.append(lax.ppermute(crops[:, level], 'segment', pairs))  3.87 us
    ppermute x1, waiting for transfers between devices, shards(): lax.ppermute(lax.dynamic_index_in_dim(pair, 1 - line, 2, keepdims=False),...  3.78 us
    ppermute x4, waiting for transfers between devices, hand_on(): return lax.ppermute(value, ('segment', 'slab'), pairs)  3.58 us
  transfers between devices with their start and end apart: 14, of which 7 were waited for; matrix products, arithmetic and copies ran while one was open for 1% of the time, Pallas kernels for 27%

profile of v3, /device:TPU:0, one launch (start us, length us, event | category | flops | bytes accessed | tf_op | source)
XLA Modules:
  0.0 123.6 jit_solution(16485749262448178083)
XLA Ops:
  0.0 1.2 copy-done
  1.2 0.7 copy-done.4
  1.8 1.1 shard_map.64.refs_1_.refs_2_
  3.0 4.3 %collective-permute-start = (bf16[3,896,128]{2,1,0:T(8,128)(2,1)S(1)}, bf16[3,896,128]{2,1,0:T(8,128)(2,1)S(1)}, u32[]{:S(2)}, u32[]{:S(2)}) collective-permute-start(bf16[3,896,128]{2,1,0:T(8,128)(2,1)S(1)} %shard_map.64.refs_1_.refs_2_), channel_id=1, source_target_pairs={{4,0},{6,2},{8,4},{10,6},{12,8},{14,10},{0,3},{2,1},{20,16},{22,18... | collective-permute-start | bytes 2064392 | tf_op jit(solution)/shard_map/ppermute | solution.py:467
  7.3 1.4 %reshape.12.kept_ref = f32[4,3,8,256]{3,2,1,0:T(8,128)S(1)} reshape(f32[4,3,8,16,16]{4,3,2,1,0:T(8,128)} %param.6) | data formatting | bytes 196608 | tf_op jit(solution)/shard_map/reshape | solution.py:445
  8.9 0.1 pad_add_fusion.ids_ref.refs_0_
  8.9 1.2 collective-permute-done.1.got_ref
  10.1 0.7 copy-done.1
  10.8 0.7 copy-done.2
  11.5 0.7 copy-done.3
  12.2 1.1 shard_map.65
  13.3 3.6 %collective-permute-done.refs_4_.refs_1_ = bf16[3,896,128]{2,1,0:T(8,128)(2,1)S(1)} collective-permute-done((bf16[3,896,128]{2,1,0:T(8,128)(2,1)S(1)}, bf16[3,896,128]{2,1,0:T(8,128)(2,1)S(1)}, u32[]{:S(2)}, u32[]{:S(2)}) %collective-permute-start) | collective-permute-done | bytes 688160 | tf_op jit(solution)/shard_map/ppermute | solution.py:467
  16.9 3.9 %collective-permute-start.2 = (bf16[3,896,128]{2,1,0:T(8,128)(2,1)S(1)}, bf16[3,896,128]{2,1,0:T(8,128)(2,1)S(1)}, u32[]{:S(2)}, u32[]{:S(2)}) collective-permute-start(bf16[3,896,128]{2,1,0:T(8,128)(2,1)S(1)} %collective-permute-done.refs_4_.refs_1_), channel_id=1, source_target_pairs={{4,0},{6,2},{8,4},{10,6},{0,3},{2,1},{20,16},{22,18},{24,20},{26,2... | collective-permute-start | bytes 2064392 | tf_op jit(solution)/shard_map/ppermute | solution.py:467
  20.8 11.2 %shard_map.66 = (bf16[8,2,4,256,384]{4,3,2,1,0:T(8,128)(2,1)}, bf16[8,1024,768]{2,1,0:T(8,128)(2,1)}, f32[8,3,8,128]{3,2,1,0:T(8,128)S(1)}, bf16[8,16,16,128]{3,2,1,0:T(8,128)(2,1)S(1)}, f32[16,2048]{1,0:T(8,128)S(1)}) custom-call(s32[4]{0:T(128)S(1)} %pad_add_fusion.ids_ref.refs_0_, bf16[3,896,128]{2,1,0:T(8,128)(2,1)S(1)} %shard_map.64.refs_1_.refs_2_, ...), custom_call_target="tpu_custom_call" | custom-call | flops 6442450944 | bytes 4194304 | tf_op jit(solution)/shard_map/pallas_call | solution.py:477
  32.1 0.1 collective-permute-start.5
  32.1 2.3 %collective-permute-start.4 = (bf16[3,896,128]{2,1,0:T(8,128)(2,1)S(1)}, bf16[3,896,128]{2,1,0:T(8,128)(2,1)S(1)}, u32[]{:S(2)}, u32[]{:S(2)}) collective-permute-start(bf16[3,896,128]{2,1,0:T(8,128)(2,1)S(1)} %collective-permute-done.2.refs_4_.refs_1_), channel_id=1, source_target_pairs={{4,0},{6,2},{0,3},{2,1},{20,16},{22,18},{16,19},{18,17}} | collective-permute-start | bytes 2064392 | tf_op jit(solution)/shard_map/ppermute | solution.py:467
  34.5 10.6 %shard_map.67 = (bf16[8,2,4,256,384]{4,3,2,1,0:T(8,128)(2,1)}, bf16[8,1024,768]{2,1,0:T(8,128)(2,1)}, f32[8,3,8,128]{3,2,1,0:T(8,128)S(1)}, bf16[8,16,16,128]{3,2,1,0:T(8,128)(2,1)S(1)}, f32[16,2048]{1,0:T(8,128)S(1)}) custom-call(s32[4]{0:T(128)S(1)} %pad_add_fusion.ids_ref.refs_0_, ...), custom_call_target="tpu_custom_call", output_to_operand_aliasing={{0}: (9, {}), {1}: (10, {}), {2}: (11, {})} | custom-call | flops 6442450944 | bytes 4194304 | tf_op jit(solution)/shard_map/pallas_call | solution.py:477
  45.2 4.2 %collective-permute-start.7 = (bf16[3,896,128]{2,1,0:T(8,128)(2,1)S(1)}, bf16[3,896,128]{2,1,0:T(8,128)(2,1)S(1)}, u32[]{:S(2)}, u32[]{:S(2)}) collective-permute-start(bf16[3,896,128]{2,1,0:T(8,128)(2,1)S(1)} %collective-permute-done.4.refs_4_.refs_1_), channel_id=1, source_target_pairs={{0,3},{2,1},{16,19},{18,17}} | collective-permute-start | bytes 2064392 | tf_op jit(solution)/shard_map/ppermute | solution.py:467
  49.4 10.6 %shard_map.68 = (bf16[8,2,4,256,384]{4,3,2,1,0:T(8,128)(2,1)}, bf16[8,1024,768]{2,1,0:T(8,128)(2,1)}, f32[8,3,8,128]{3,2,1,0:T(8,128)S(1)}, bf16[8,16,16,128]{3,2,1,0:T(8,128)(2,1)S(1)}, f32[16,2048]{1,0:T(8,128)S(1)}) custom-call(s32[4]{0:T(128)S(1)} %pad_add_fusion.ids_ref.refs_0_, ...), custom_call_target="tpu_custom_call", output_to_operand_aliasing={{0}: (9, {}), {1}: (10, {}), {2}: (11, {})} | custom-call | flops 6442450944 | bytes 4194304 | tf_op jit(solution)/shard_map/pallas_call | solution.py:477
  60.1 2.1 %collective-permute-done.8.refs_3_ = bf16[3,896,128]{2,1,0:T(8,128)(2,1)S(1)} collective-permute-done((bf16[3,896,128]{2,1,0:T(8,128)(2,1)S(1)}, bf16[3,896,128]{2,1,0:T(8,128)(2,1)S(1)}, u32[]{:S(2)}, u32[]{:S(2)}) %collective-permute-start.8) | collective-permute-done | bytes 688160 | tf_op jit(solution)/shard_map/ppermute | solution.py:430
  62.2 11.5 %shard_map.69 = (bf16[8,2,4,256,384]{4,3,2,1,0:T(8,128)(2,1)}, bf16[8,1024,768]{2,1,0:T(8,128)(2,1)}, f32[8,3,8,128]{3,2,1,0:T(8,128)S(1)}, bf16[8,16,16,128]{3,2,1,0:T(8,128)(2,1)}, f32[16,2048]{1,0:T(8,128)S(1)}) custom-call(s32[4]{0:T(128)S(1)} %pad_add_fusion.ids_ref.refs_0_, ...), custom_call_target="tpu_custom_call", output_to_operand_aliasing={{0}: (9, {}), {1}: (10, {}), {2}: (11, {})} | custom-call | flops 6442450944 | bytes 4194304 | tf_op jit(solution)/shard_map/pallas_call | solution.py:477
  73.7 35.8 %shard_map.70 = (bf16[128,128]{1,0:T(8,128)(2,1)S(1)}, bf16[128,128]{1,0:T(8,128)(2,1)S(1)}) custom-call(s32[4]{0:T(128)S(1)} %pad_add_fusion.ids_ref.refs_0_, f32[16,2048]{1,0:T(8,128)S(1)} %get-tuple-element.57.x_ref, bf16[48,128]{1,0:T(8,128)(2,1)S(1)} %get-tuple-element.37.refs_6_.lift_ref, bf16[48,128]{1,0:T(8,128)(2,1)S(1)} %get-tuple-element.38.refs_7_.proj_ref, ...), custom_call_target="tpu_custom_call" | custom-call | flops 25769803776 | bytes 16777216 | tf_op jit(solution)/shard_map/pallas_call | solution.py:501
  109.5 0.2 collective-permute-start.9
  109.7 1.1 collective-permute-done.9
  110.9 2.0 %collective-permute-start.10 = (bf16[2,4,16,128]{3,2,0,1:T(8,128)(2,1)S(1)}, bf16[2,4,16,128]{3,2,0,1:T(8,128)(2,1)S(1)}, u32[]{:S(2)}, u32[]{:S(2)}) collective-permute-start(bf16[2,4,16,128]{3,2,0,1:T(8,128)(2,1)S(1)} %get-tuple-element.68), channel_id=1, source_target_pairs={{0,2},{2,0},{1,3},{3,1},{16,18},{18,16},{17,19},{19,17}} | collective-permute-start | bytes 98312 | tf_op jit(solution)/shard_map/ppermute | solution.py:523
  112.9 3.8 %collective-permute-done.10 = bf16[2,4,16,128]{3,2,0,1:T(8,128)(2,1)S(1)} collective-permute-done((bf16[2,4,16,128]{3,2,0,1:T(8,128)(2,1)S(1)}, bf16[2,4,16,128]{3,2,0,1:T(8,128)(2,1)S(1)}, u32[]{:S(2)}, u32[]{:S(2)}) %collective-permute-start.10) | collective-permute-done | bytes 32800 | tf_op jit(solution)/shard_map/ppermute | solution.py:523
  116.7 1.3 %collective-permute-start.11 = (bf16[4,16,128]{2,1,0:T(8,128)(2,1)S(1)}, bf16[4,16,128]{2,1,0:T(8,128)(2,1)S(1)}, u32[]{:S(2)}, u32[]{:S(2)}) collective-permute-start(bf16[4,16,128]{2,1,0:T(8,128)(2,1)S(1)} %get-tuple-element.65), channel_id=1, source_target_pairs={{0,4},{2,6},{1,5},{3,7},{16,20},{18,22},{17,21},{19,23}} | collective-permute-start | bytes 49160 | tf_op jit(solution)/shard_map/ppermute | solution.py:528
  118.0 1.3 %collective-permute-start.12 = (bf16[4,16,128]{2,1,0:T(8,128)(2,1)S(1)}, bf16[4,16,128]{2,1,0:T(8,128)(2,1)S(1)}, u32[]{:S(2)}, u32[]{:S(2)}) collective-permute-start(bf16[4,16,128]{2,1,0:T(8,128)(2,1)S(1)} %get-tuple-element.64), channel_id=1, source_target_pairs={{0,8},{2,10},{1,9},{3,11},{16,24},{18,26},{17,25},{19,27}} | collective-permute-start | bytes 49160 | tf_op jit(solution)/shard_map/ppermute | solution.py:528
  119.3 1.3 %collective-permute-start.13 = (bf16[4,16,128]{2,1,0:T(8,128)(2,1)S(1)}, bf16[4,16,128]{2,1,0:T(8,128)(2,1)S(1)}, u32[]{:S(2)}, u32[]{:S(2)}) collective-permute-start(bf16[4,16,128]{2,1,0:T(8,128)(2,1)S(1)} %get-tuple-element.63), channel_id=1, source_target_pairs={{0,12},{2,14},{1,13},{3,15},{16,28},{18,30},{17,29},{19,31}} | collective-permute-start | bytes 49160 | tf_op jit(solution)/shard_map/ppermute | solution.py:528
  120.6 0.1 collective-permute-done.12.refs_3_
  120.7 1.3 %collective-permute-done.13.refs_4_ = bf16[4,16,128]{2,1,0:T(8,128)(2,1)S(1)} collective-permute-done((bf16[4,16,128]{2,1,0:T(8,128)(2,1)S(1)}, bf16[4,16,128]{2,1,0:T(8,128)(2,1)S(1)}, u32[]{:S(2)}, u32[]{:S(2)}) %collective-permute-start.13) | collective-permute-done | bytes 16416 | tf_op jit(solution)/shard_map/ppermute | solution.py:528
  122.0 1.5 %shard_map.71 = f32[2,4,3,8,2,16]{5,4,3,2,1,0:T(2,128)} custom-call(s32[4]{0:T(128)S(1)} %pad_add_fusion.ids_ref.refs_0_, bf16[4,16,128]{2,1,0:T(8,128)(2,1)S(1)} %get-tuple-element.66.refs_1_, bf16[4,16,128]{2,1,0:T(8,128)(2,1)S(1)} %collective-permute-done.11.refs_2_, bf16[4,16,128]{2,1,0:T(8,128)(2,1)S(1)} %collective-permute-done.12.refs_3_, ...), custom_call_target="tpu_custom_call" | custom-call | tf_op jit(solution)/shard_map/pallas_call | solution.py:529
  (21 shorter events, 0.3 us)
Async XLA Ops:
  0.0 1.2 copy-start
  1.2 0.7 copy-start.4
  3.0 13.8 %collective-permute-start = (bf16[3,896,128]{2,1,0:T(8,128)(2,1)S(1)}, bf16[3,896,128]{2,1,0:T(8,128)(2,1)S(1)}, u32[]{:S(2)}, u32[]{:S(2)}) collective-permute-start(bf16[3,896,128]{2,1,0:T(8,128)(2,1)S(1)} %shard_map.64.refs_1_.refs_2_), channel_id=1, source_target_pairs={{4,0},{6,2},{8,4},{10,6},{12,8},{14,10},{0,3},{2,1},{20,16},{22,18... | collective-permute-start | bytes 2064392 | tf_op jit(solution)/shard_map/ppermute | solution.py:467
  8.8 1.4 %collective-permute-start.1 = (f32[4,3,8,256]{3,2,1,0:T(8,128)S(1)}, f32[4,3,8,256]{3,2,1,0:T(8,128)S(1)}, u32[]{:S(2)}, u32[]{:S(2)}) collective-permute-start(f32[4,3,8,256]{3,2,1,0:T(8,128)S(1)} %reshape.12.kept_ref), channel_id=1, source_target_pairs={{0,1},{1,0},{2,3},{3,2},{4,5},{5,4},{6,7},{7,6},{8,9},{9,8},{10,11... | collective-permute-start | bytes 294920 | tf_op jit(solution)/shard_map/ppermute | solution.py:430
  10.1 0.7 copy-start.1
  10.8 0.7 copy-start.2
  11.5 0.7 copy-start.3
  16.8 4.0 %collective-permute-start.3 = (bf16[3,896,128]{2,1,0:T(8,128)(2,1)S(1)}, bf16[3,896,128]{2,1,0:T(8,128)(2,1)S(1)}, u32[]{:S(2)}, u32[]{:S(2)}) collective-permute-start(bf16[3,896,128]{2,1,0:T(8,128)(2,1)S(1)} %collective-permute-done.refs_4_.refs_1_), channel_id=1, source_target_pairs={{0,1},{1,0},{2,3},{3,2},{4,5},{5,4},{6,7},{7,6},{8,9},{9,8},{10,11... | collective-permute-start | bytes 2064392 | tf_op jit(solution)/shard_map/ppermute | solution.py:430
  16.9 15.2 %collective-permute-start.2 = (bf16[3,896,128]{2,1,0:T(8,128)(2,1)S(1)}, bf16[3,896,128]{2,1,0:T(8,128)(2,1)S(1)}, u32[]{:S(2)}, u32[]{:S(2)}) collective-permute-start(bf16[3,896,128]{2,1,0:T(8,128)(2,1)S(1)} %collective-permute-done.refs_4_.refs_1_), channel_id=1, source_target_pairs={{4,0},{6,2},{8,4},{10,6},{0,3},{2,1},{20,16},{22,18},{24,20},{26,2... | collective-permute-start | bytes 2064392 | tf_op jit(solution)/shard_map/ppermute | solution.py:467
  32.1 2.4 %collective-permute-start.5 = (bf16[3,896,128]{2,1,0:T(8,128)(2,1)S(1)}, bf16[3,896,128]{2,1,0:T(8,128)(2,1)S(1)}, u32[]{:S(2)}, u32[]{:S(2)}) collective-permute-start(bf16[3,896,128]{2,1,0:T(8,128)(2,1)S(1)} %collective-permute-done.2.refs_4_.refs_1_), channel_id=1, source_target_pairs={{0,1},{1,0},{2,3},{3,2},{4,5},{5,4},{6,7},{7,6},{8,9},{9,8},{10,11... | collective-permute-start | bytes 2064392 | tf_op jit(solution)/shard_map/ppermute | solution.py:430
  32.1 12.9 %collective-permute-start.4 = (bf16[3,896,128]{2,1,0:T(8,128)(2,1)S(1)}, bf16[3,896,128]{2,1,0:T(8,128)(2,1)S(1)}, u32[]{:S(2)}, u32[]{:S(2)}) collective-permute-start(bf16[3,896,128]{2,1,0:T(8,128)(2,1)S(1)} %collective-permute-done.2.refs_4_.refs_1_), channel_id=1, source_target_pairs={{4,0},{6,2},{0,3},{2,1},{20,16},{22,18},{16,19},{18,17}} | collective-permute-start | bytes 2064392 | tf_op jit(solution)/shard_map/ppermute | solution.py:467
  45.1 4.3 %collective-permute-start.6 = (bf16[3,896,128]{2,1,0:T(8,128)(2,1)S(1)}, bf16[3,896,128]{2,1,0:T(8,128)(2,1)S(1)}, u32[]{:S(2)}, u32[]{:S(2)}) collective-permute-start(bf16[3,896,128]{2,1,0:T(8,128)(2,1)S(1)} %collective-permute-done.4.refs_4_.refs_1_), channel_id=1, source_target_pairs={{0,1},{1,0},{2,3},{3,2},{4,5},{5,4},{6,7},{7,6},{8,9},{9,8},{10,11... | collective-permute-start | bytes 2064392 | tf_op jit(solution)/shard_map/ppermute | solution.py:430
  45.2 14.8 %collective-permute-start.7 = (bf16[3,896,128]{2,1,0:T(8,128)(2,1)S(1)}, bf16[3,896,128]{2,1,0:T(8,128)(2,1)S(1)}, u32[]{:S(2)}, u32[]{:S(2)}) collective-permute-start(bf16[3,896,128]{2,1,0:T(8,128)(2,1)S(1)} %collective-permute-done.4.refs_4_.refs_1_), channel_id=1, source_target_pairs={{0,3},{2,1},{16,19},{18,17}} | collective-permute-start | bytes 2064392 | tf_op jit(solution)/shard_map/ppermute | solution.py:467
  60.0 2.2 %collective-permute-start.8 = (bf16[3,896,128]{2,1,0:T(8,128)(2,1)S(1)}, bf16[3,896,128]{2,1,0:T(8,128)(2,1)S(1)}, u32[]{:S(2)}, u32[]{:S(2)}) collective-permute-start(bf16[3,896,128]{2,1,0:T(8,128)(2,1)S(1)} %collective-permute-done.7.refs_4_), channel_id=1, source_target_pairs={{0,1},{1,0},{2,3},{3,2},{4,5},{5,4},{6,7},{7,6},{8,9},{9,8},{10,11... | collective-permute-start | bytes 2064392 | tf_op jit(solution)/shard_map/ppermute | solution.py:430
  109.5 1.3 %collective-permute-start.9 = (bf16[128,128]{1,0:T(8,128)(2,1)S(1)}, bf16[128,128]{1,0:T(8,128)(2,1)S(1)}, u32[]{:S(2)}, u32[]{:S(2)}) collective-permute-start(bf16[128,128]{1,0:T(8,128)(2,1)S(1)} %get-tuple-element.62), channel_id=1, source_target_pairs={{0,1},{1,0},{2,3},{3,2},{4,5},{5,4},{6,7},{7,6},{8,9},{9,8},{10,11... | collective-permute-start | bytes 98312 | tf_op jit(solution)/shard_map/ppermute | solution.py:430
  110.9 5.8 %collective-permute-start.10 = (bf16[2,4,16,128]{3,2,0,1:T(8,128)(2,1)S(1)}, bf16[2,4,16,128]{3,2,0,1:T(8,128)(2,1)S(1)}, u32[]{:S(2)}, u32[]{:S(2)}) collective-permute-start(bf16[2,4,16,128]{3,2,0,1:T(8,128)(2,1)S(1)} %get-tuple-element.68), channel_id=1, source_target_pairs={{0,2},{2,0},{1,3},{3,1},{16,18},{18,16},{17,19},{19,17}} | collective-permute-start | bytes 98312 | tf_op jit(solution)/shard_map/ppermute | solution.py:523
  116.7 3.9 %collective-permute-start.11 = (bf16[4,16,128]{2,1,0:T(8,128)(2,1)S(1)}, bf16[4,16,128]{2,1,0:T(8,128)(2,1)S(1)}, u32[]{:S(2)}, u32[]{:S(2)}) collective-permute-start(bf16[4,16,128]{2,1,0:T(8,128)(2,1)S(1)} %get-tuple-element.65), channel_id=1, source_target_pairs={{0,4},{2,6},{1,5},{3,7},{16,20},{18,22},{17,21},{19,23}} | collective-permute-start | bytes 49160 | tf_op jit(solution)/shard_map/ppermute | solution.py:528
  118.0 2.7 %collective-permute-start.12 = (bf16[4,16,128]{2,1,0:T(8,128)(2,1)S(1)}, bf16[4,16,128]{2,1,0:T(8,128)(2,1)S(1)}, u32[]{:S(2)}, u32[]{:S(2)}) collective-permute-start(bf16[4,16,128]{2,1,0:T(8,128)(2,1)S(1)} %get-tuple-element.64), channel_id=1, source_target_pairs={{0,8},{2,10},{1,9},{3,11},{16,24},{18,26},{17,25},{19,27}} | collective-permute-start | bytes 49160 | tf_op jit(solution)/shard_map/ppermute | solution.py:528
  119.3 2.7 %collective-permute-start.13 = (bf16[4,16,128]{2,1,0:T(8,128)(2,1)S(1)}, bf16[4,16,128]{2,1,0:T(8,128)(2,1)S(1)}, u32[]{:S(2)}, u32[]{:S(2)}) collective-permute-start(bf16[4,16,128]{2,1,0:T(8,128)(2,1)S(1)} %get-tuple-element.63), channel_id=1, source_target_pairs={{0,12},{2,14},{1,13},{3,15},{16,28},{18,30},{17,29},{19,31}} | collective-permute-start | bytes 49160 | tf_op jit(solution)/shard_map/ppermute | solution.py:528

commit v4 on v3

--- a/solution.py
+++ b/solution.py
@@ -26,7 +26,7 @@
 )
 
 
-GROUPS = ((0, 1), (2, 3))
+GROUPS = ((0,), (1,), (2,), (3,))
 
 
 def neighbour(layer, tile, step):
@@ -42,17 +42,10 @@
     return lax.dot_general(a, b, (((1,), (1,)), ((), ())), preferred_element_type=jnp.float32)
 
 
-def pack_kernel(raw_hbm, bias_hbm, packed, raw_ref, bias_ref, sems):
-    copies = [pltpu.make_async_copy(raw_hbm.at[0, i], raw_ref.at[i], sems.at[i]) for i in range(LAYERS)]
-    copies.append(pltpu.make_async_copy(bias_hbm, bias_ref, sems.at[LAYERS]))
-    for copy in copies:
-        copy.start()
-    row = lax.broadcasted_iota(jnp.int32, (192, 192), 0)
-    eye = jnp.where(row == lax.broadcasted_iota(jnp.int32, (192, 192), 1), 1.0, 0.0).astype(jnp.bfloat16)
+def pack_kernel(raw_ref, bias_ref, eye_ref, packed):
+    eye = eye_ref[...]
     low = low_lanes((CH, 128))
-    copies[LAYERS].wait()
     for layer in range(LAYERS):
-        copies[layer].wait()
         for ty in range(3):
             pair = jnp.concatenate([raw_ref[layer, 3 + ty], raw_ref[layer, ty]], axis=0)
             packed[layer, ty * 192 : (ty + 1) * 192, :] = nt_dot(eye, pair).astype(jnp.bfloat16)
@@ -193,9 +186,8 @@
 
     flat = summed(rows(0), 0, 256)
     alternate = summed(rows(1), 256, 512)
-    waves = summed(jnp.concatenate([rows(2, 4), rows(3, 2)], axis=0), 512, 1024)
-    count = 4 * len(units)
-    cosine, sine = waves[:count], waves[count:]
+    cosine = summed(rows(2, 4), 512, 1024)
+    sine = summed(rows(3, 2), 512, 1024)
     even, odd = flat + alternate, flat - alternate
     cells = [value.reshape(len(units), 1, 4, 16, 256) for value in (even + cosine, odd - sine, even - cosine, odd + sine)]
     cells = jnp.concatenate(cells, axis=1).reshape(len(units), 16, 16, 256)
@@ -432,15 +424,10 @@
     packed = pl.pallas_call(
         pack_kernel,
         out_shape=jax.ShapeDtypeStruct((LAYERS, ROWS, 128), jnp.bfloat16),
-        in_specs=[pl.BlockSpec(memory_space=pltpu.HBM)] * 2,
+        in_specs=[vmem] * 3,
         out_specs=vmem,
-        scratch_shapes=[
-            pltpu.VMEM(conv_weight.shape[1:], jnp.bfloat16),
-            pltpu.VMEM((LAYERS, 1, CH), jnp.float32),
-            pltpu.SemaphoreType.DMA((LAYERS + 1,)),
-        ],
         compiler_params=params,
-    )(conv_weight, conv_bias.transpose(1, 0, 2))
+    )(conv_weight[0], conv_bias.transpose(1, 0, 2), jnp.eye(192, dtype=jnp.bfloat16))
 
     flat = after(fields, packed).reshape(crop_count, comps, slab_rows, y_cells * z_cells)
     x, lift, proj = pl.pallas_call(

time: 124 us -> 120 us (0.968)
  Pallas kernels: 83.6 us -> 79.5 us
    pallas_call x1, Pallas kernels: 35.8 us -> 33.4 us  [shards(): pl.pallas_call(second_kernel, grid=(segments,), out_shape=(jax.ShapeDtype...]
  transfers between devices with their start and end apart: 14 -> 14, of which waited for: 7 -> 8; matrix products, arithmetic and copies ran while one was open for 1% -> 1% of each run, Pallas kernels for 27% -> 27%
where the time goes in v4:
time: 120 us
  Pallas kernels  79.5 us (66%)
  starting transfers between devices  21.1 us (18%)
  waiting for transfers between devices  13.2 us (11%)
  local copies, waits for them, and re-layouts  5.35 us (4%)
    pallas_call x4, Pallas kernels, shards(): pl.pallas_call(functools.partial(level_kernel, level, level == 0, level =...  42.9 us
    pallas_call x1, Pallas kernels, shards(): pl.pallas_call(second_kernel, grid=(segments,), out_shape=(jax.ShapeDtype...  33.4 us
    ppermute x4, starting transfers between devices, hand_on(): return lax.ppermute(value, ('segment', 'slab'), pairs)  14.5 us
    ppermute x6, waiting for transfers between devices, between_cores(): return lax.ppermute(value, 'slab', swap)  4.38 us
    unnamed x10, local copies, waits for them, and re-layouts  3.89 us
    ppermute x3, starting transfers between devices, shards(): pieces.append(lax.ppermute(crops[:, level], 'segment', pairs))  3.87 us
    ppermute x4, waiting for transfers between devices, hand_on(): return lax.ppermute(value, ('segment', 'slab'), pairs)  3.74 us
    ppermute x1, waiting for transfers between devices, shards(): lax.ppermute(lax.dynamic_index_in_dim(pair, 1 - line, 2, keepdims=False),...  3.68 us
  transfers between devices with their start and end apart: 14, of which 8 were waited for; matrix products, arithmetic and copies ran while one was open for 1% of the time, Pallas kernels for 27%

profile of v4, /device:TPU:0, one launch (start us, length us, event | category | flops | bytes accessed | tf_op | source)
XLA Modules:
  0.0 119.5 jit_solution(7529936066443677909)
XLA Ops:
  0.0 1.2 copy-done
  1.2 0.7 copy-done.4
  1.9 0.5 shard_map.64.refs_1_.refs_2_
  2.4 4.3 %collective-permute-start = (bf16[3,896,128]{2,1,0:T(8,128)(2,1)S(1)}, bf16[3,896,128]{2,1,0:T(8,128)(2,1)S(1)}, u32[]{:S(2)}, u32[]{:S(2)}) collective-permute-start(bf16[3,896,128]{2,1,0:T(8,128)(2,1)S(1)} %shard_map.64.refs_1_.refs_2_), channel_id=1, source_target_pairs={{4,0},{6,2},{8,4},{10,6},{12,8},{14,10},{0,3},{2,1},{20,16},{22,18... | collective-permute-start | bytes 2064392 | tf_op jit(solution)/shard_map/ppermute | solution.py:454
  6.8 1.4 %reshape.12.kept_ref = f32[4,3,8,256]{3,2,1,0:T(8,128)S(1)} reshape(f32[4,3,8,16,16]{4,3,2,1,0:T(8,128)} %param.6) | data formatting | bytes 196608 | tf_op jit(solution)/shard_map/reshape | solution.py:432
  8.4 1.2 collective-permute-done.1.got_ref
  9.6 0.7 copy-done.1
  10.2 0.7 copy-done.2
  10.9 0.7 copy-done.3
  11.6 1.1 shard_map.65
  12.7 3.6 %collective-permute-done.refs_4_.refs_1_ = bf16[3,896,128]{2,1,0:T(8,128)(2,1)S(1)} collective-permute-done((bf16[3,896,128]{2,1,0:T(8,128)(2,1)S(1)}, bf16[3,896,128]{2,1,0:T(8,128)(2,1)S(1)}, u32[]{:S(2)}, u32[]{:S(2)}) %collective-permute-start) | collective-permute-done | bytes 688160 | tf_op jit(solution)/shard_map/ppermute | solution.py:454
  16.3 3.9 %collective-permute-start.2 = (bf16[3,896,128]{2,1,0:T(8,128)(2,1)S(1)}, bf16[3,896,128]{2,1,0:T(8,128)(2,1)S(1)}, u32[]{:S(2)}, u32[]{:S(2)}) collective-permute-start(bf16[3,896,128]{2,1,0:T(8,128)(2,1)S(1)} %collective-permute-done.refs_4_.refs_1_), channel_id=1, source_target_pairs={{4,0},{6,2},{8,4},{10,6},{0,3},{2,1},{20,16},{22,18},{24,20},{26,2... | collective-permute-start | bytes 2064392 | tf_op jit(solution)/shard_map/ppermute | solution.py:454
  20.3 10.9 %shard_map.66 = (bf16[8,2,4,256,384]{4,3,2,1,0:T(8,128)(2,1)}, bf16[8,1024,768]{2,1,0:T(8,128)(2,1)}, f32[8,3,8,128]{3,2,1,0:T(8,128)S(1)}, bf16[8,16,16,128]{3,2,1,0:T(8,128)(2,1)S(1)}, f32[16,2048]{1,0:T(8,128)S(1)}) custom-call(s32[4]{0:T(128)S(1)} %pad_add_fusion.ids_ref.refs_0_, bf16[3,896,128]{2,1,0:T(8,128)(2,1)S(1)} %shard_map.64.refs_1_.refs_2_, ...), custom_call_target="tpu_custom_call" | custom-call | flops 6442450944 | bytes 4194304 | tf_op jit(solution)/shard_map/pallas_call | solution.py:464
  31.3 2.3 %collective-permute-start.4 = (bf16[3,896,128]{2,1,0:T(8,128)(2,1)S(1)}, bf16[3,896,128]{2,1,0:T(8,128)(2,1)S(1)}, u32[]{:S(2)}, u32[]{:S(2)}) collective-permute-start(bf16[3,896,128]{2,1,0:T(8,128)(2,1)S(1)} %collective-permute-done.2.refs_4_.refs_1_), channel_id=1, source_target_pairs={{4,0},{6,2},{0,3},{2,1},{20,16},{22,18},{16,19},{18,17}} | collective-permute-start | bytes 2064392 | tf_op jit(solution)/shard_map/ppermute | solution.py:454
  33.6 10.3 %shard_map.67 = (bf16[8,2,4,256,384]{4,3,2,1,0:T(8,128)(2,1)}, bf16[8,1024,768]{2,1,0:T(8,128)(2,1)}, f32[8,3,8,128]{3,2,1,0:T(8,128)S(1)}, bf16[8,16,16,128]{3,2,1,0:T(8,128)(2,1)S(1)}, f32[16,2048]{1,0:T(8,128)S(1)}) custom-call(s32[4]{0:T(128)S(1)} %pad_add_fusion.ids_ref.refs_0_, ...), custom_call_target="tpu_custom_call", output_to_operand_aliasing={{0}: (9, {}), {1}: (10, {}), {2}: (11, {})} | custom-call | flops 6442450944 | bytes 4194304 | tf_op jit(solution)/shard_map/pallas_call | solution.py:464
  44.0 0.2 collective-permute-done.4.refs_4_.refs_1_
  44.1 0.1 collective-permute-start.6
  44.2 4.0 %collective-permute-start.7 = (bf16[3,896,128]{2,1,0:T(8,128)(2,1)S(1)}, bf16[3,896,128]{2,1,0:T(8,128)(2,1)S(1)}, u32[]{:S(2)}, u32[]{:S(2)}) collective-permute-start(bf16[3,896,128]{2,1,0:T(8,128)(2,1)S(1)} %collective-permute-done.4.refs_4_.refs_1_), channel_id=1, source_target_pairs={{0,3},{2,1},{16,19},{18,17}} | collective-permute-start | bytes 2064392 | tf_op jit(solution)/shard_map/ppermute | solution.py:454
  48.2 10.3 %shard_map.68 = (bf16[8,2,4,256,384]{4,3,2,1,0:T(8,128)(2,1)}, bf16[8,1024,768]{2,1,0:T(8,128)(2,1)}, f32[8,3,8,128]{3,2,1,0:T(8,128)S(1)}, bf16[8,16,16,128]{3,2,1,0:T(8,128)(2,1)S(1)}, f32[16,2048]{1,0:T(8,128)S(1)}) custom-call(s32[4]{0:T(128)S(1)} %pad_add_fusion.ids_ref.refs_0_, ...), custom_call_target="tpu_custom_call", output_to_operand_aliasing={{0}: (9, {}), {1}: (10, {}), {2}: (11, {})} | custom-call | flops 6442450944 | bytes 4194304 | tf_op jit(solution)/shard_map/pallas_call | solution.py:464
  58.7 2.1 %collective-permute-done.8.refs_3_ = bf16[3,896,128]{2,1,0:T(8,128)(2,1)S(1)} collective-permute-done((bf16[3,896,128]{2,1,0:T(8,128)(2,1)S(1)}, bf16[3,896,128]{2,1,0:T(8,128)(2,1)S(1)}, u32[]{:S(2)}, u32[]{:S(2)}) %collective-permute-start.8) | collective-permute-done | bytes 688160 | tf_op jit(solution)/shard_map/ppermute | solution.py:422
  60.8 11.3 %shard_map.69 = (bf16[8,2,4,256,384]{4,3,2,1,0:T(8,128)(2,1)}, bf16[8,1024,768]{2,1,0:T(8,128)(2,1)}, f32[8,3,8,128]{3,2,1,0:T(8,128)S(1)}, bf16[8,16,16,128]{3,2,1,0:T(8,128)(2,1)}, f32[16,2048]{1,0:T(8,128)S(1)}) custom-call(s32[4]{0:T(128)S(1)} %pad_add_fusion.ids_ref.refs_0_, ...), custom_call_target="tpu_custom_call", output_to_operand_aliasing={{0}: (9, {}), {1}: (10, {}), {2}: (11, {})} | custom-call | flops 6442450944 | bytes 4194304 | tf_op jit(solution)/shard_map/pallas_call | solution.py:464
  72.1 33.4 %shard_map.70 = (bf16[128,128]{1,0:T(8,128)(2,1)S(1)}, bf16[128,128]{1,0:T(8,128)(2,1)S(1)}) custom-call(s32[4]{0:T(128)S(1)} %pad_add_fusion.ids_ref.refs_0_, f32[16,2048]{1,0:T(8,128)S(1)} %get-tuple-element.57.x_ref, bf16[48,128]{1,0:T(8,128)(2,1)S(1)} %get-tuple-element.37.refs_6_.lift_ref, bf16[48,128]{1,0:T(8,128)(2,1)S(1)} %get-tuple-element.38.refs_7_.proj_ref, ...), custom_call_target="tpu_custom_call" | custom-call | flops 25769803776 | bytes 16777216 | tf_op jit(solution)/shard_map/pallas_call | solution.py:488
  105.5 0.2 collective-permute-start.9
  105.7 1.1 collective-permute-done.9
  106.8 2.1 %collective-permute-start.10 = (bf16[2,4,16,128]{3,2,0,1:T(8,128)(2,1)S(1)}, bf16[2,4,16,128]{3,2,0,1:T(8,128)(2,1)S(1)}, u32[]{:S(2)}, u32[]{:S(2)}) collective-permute-start(bf16[2,4,16,128]{3,2,0,1:T(8,128)(2,1)S(1)} %get-tuple-element.68), channel_id=1, source_target_pairs={{0,2},{2,0},{1,3},{3,1},{16,18},{18,16},{17,19},{19,17}} | collective-permute-start | bytes 98312 | tf_op jit(solution)/shard_map/ppermute | solution.py:510
  109.0 3.7 %collective-permute-done.10 = bf16[2,4,16,128]{3,2,0,1:T(8,128)(2,1)S(1)} collective-permute-done((bf16[2,4,16,128]{3,2,0,1:T(8,128)(2,1)S(1)}, bf16[2,4,16,128]{3,2,0,1:T(8,128)(2,1)S(1)}, u32[]{:S(2)}, u32[]{:S(2)}) %collective-permute-start.10) | collective-permute-done | bytes 32800 | tf_op jit(solution)/shard_map/ppermute | solution.py:510
  112.7 1.3 %collective-permute-start.11 = (bf16[4,16,128]{2,1,0:T(8,128)(2,1)S(1)}, bf16[4,16,128]{2,1,0:T(8,128)(2,1)S(1)}, u32[]{:S(2)}, u32[]{:S(2)}) collective-permute-start(bf16[4,16,128]{2,1,0:T(8,128)(2,1)S(1)} %get-tuple-element.65), channel_id=1, source_target_pairs={{0,4},{2,6},{1,5},{3,7},{16,20},{18,22},{17,21},{19,23}} | collective-permute-start | bytes 49160 | tf_op jit(solution)/shard_map/ppermute | solution.py:515
  114.0 1.3 %collective-permute-start.12 = (bf16[4,16,128]{2,1,0:T(8,128)(2,1)S(1)}, bf16[4,16,128]{2,1,0:T(8,128)(2,1)S(1)}, u32[]{:S(2)}, u32[]{:S(2)}) collective-permute-start(bf16[4,16,128]{2,1,0:T(8,128)(2,1)S(1)} %get-tuple-element.64), channel_id=1, source_target_pairs={{0,8},{2,10},{1,9},{3,11},{16,24},{18,26},{17,25},{19,27}} | collective-permute-start | bytes 49160 | tf_op jit(solution)/shard_map/ppermute | solution.py:515
  115.3 1.3 %collective-permute-start.13 = (bf16[4,16,128]{2,1,0:T(8,128)(2,1)S(1)}, bf16[4,16,128]{2,1,0:T(8,128)(2,1)S(1)}, u32[]{:S(2)}, u32[]{:S(2)}) collective-permute-start(bf16[4,16,128]{2,1,0:T(8,128)(2,1)S(1)} %get-tuple-element.63), channel_id=1, source_target_pairs={{0,12},{2,14},{1,13},{3,15},{16,28},{18,30},{17,29},{19,31}} | collective-permute-start | bytes 49160 | tf_op jit(solution)/shard_map/ppermute | solution.py:515
  116.6 0.1 collective-permute-done.12.refs_3_
  116.7 1.3 %collective-permute-done.13.refs_4_ = bf16[4,16,128]{2,1,0:T(8,128)(2,1)S(1)} collective-permute-done((bf16[4,16,128]{2,1,0:T(8,128)(2,1)S(1)}, bf16[4,16,128]{2,1,0:T(8,128)(2,1)S(1)}, u32[]{:S(2)}, u32[]{:S(2)}) %collective-permute-start.13) | collective-permute-done | bytes 16416 | tf_op jit(solution)/shard_map/ppermute | solution.py:515
  118.0 1.5 %shard_map.71 = f32[2,4,3,8,2,16]{5,4,3,2,1,0:T(2,128)} custom-call(s32[4]{0:T(128)S(1)} %pad_add_fusion.ids_ref.refs_0_, bf16[4,16,128]{2,1,0:T(8,128)(2,1)S(1)} %get-tuple-element.66.refs_1_, bf16[4,16,128]{2,1,0:T(8,128)(2,1)S(1)} %collective-permute-done.11.refs_2_, bf16[4,16,128]{2,1,0:T(8,128)(2,1)S(1)} %collective-permute-done.12.refs_3_, ...), custom_call_target="tpu_custom_call" | custom-call | tf_op jit(solution)/shard_map/pallas_call | solution.py:516
  (22 shorter events, 0.4 us)
Async XLA Ops:
  0.0 1.2 copy-start
  1.2 0.7 copy-start.4
  2.4 13.8 %collective-permute-start = (bf16[3,896,128]{2,1,0:T(8,128)(2,1)S(1)}, bf16[3,896,128]{2,1,0:T(8,128)(2,1)S(1)}, u32[]{:S(2)}, u32[]{:S(2)}) collective-permute-start(bf16[3,896,128]{2,1,0:T(8,128)(2,1)S(1)} %shard_map.64.refs_1_.refs_2_), channel_id=1, source_target_pairs={{4,0},{6,2},{8,4},{10,6},{12,8},{14,10},{0,3},{2,1},{20,16},{22,18... | collective-permute-start | bytes 2064392 | tf_op jit(solution)/shard_map/ppermute | solution.py:454
  8.2 1.4 %collective-permute-start.1 = (f32[4,3,8,256]{3,2,1,0:T(8,128)S(1)}, f32[4,3,8,256]{3,2,1,0:T(8,128)S(1)}, u32[]{:S(2)}, u32[]{:S(2)}) collective-permute-start(f32[4,3,8,256]{3,2,1,0:T(8,128)S(1)} %reshape.12.kept_ref), channel_id=1, source_target_pairs={{0,1},{1,0},{2,3},{3,2},{4,5},{5,4},{6,7},{7,6},{8,9},{9,8},{10,11... | collective-permute-start | bytes 294920 | tf_op jit(solution)/shard_map/ppermute | solution.py:422
  9.6 0.7 copy-start.1
  10.2 0.7 copy-start.2
  10.9 0.7 copy-start.3
  16.3 4.0 %collective-permute-start.3 = (bf16[3,896,128]{2,1,0:T(8,128)(2,1)S(1)}, bf16[3,896,128]{2,1,0:T(8,128)(2,1)S(1)}, u32[]{:S(2)}, u32[]{:S(2)}) collective-permute-start(bf16[3,896,128]{2,1,0:T(8,128)(2,1)S(1)} %collective-permute-done.refs_4_.refs_1_), channel_id=1, source_target_pairs={{0,1},{1,0},{2,3},{3,2},{4,5},{5,4},{6,7},{7,6},{8,9},{9,8},{10,11... | collective-permute-start | bytes 2064392 | tf_op jit(solution)/shard_map/ppermute | solution.py:422
  16.3 14.9 %collective-permute-start.2 = (bf16[3,896,128]{2,1,0:T(8,128)(2,1)S(1)}, bf16[3,896,128]{2,1,0:T(8,128)(2,1)S(1)}, u32[]{:S(2)}, u32[]{:S(2)}) collective-permute-start(bf16[3,896,128]{2,1,0:T(8,128)(2,1)S(1)} %collective-permute-done.refs_4_.refs_1_), channel_id=1, source_target_pairs={{4,0},{6,2},{8,4},{10,6},{0,3},{2,1},{20,16},{22,18},{24,20},{26,2... | collective-permute-start | bytes 2064392 | tf_op jit(solution)/shard_map/ppermute | solution.py:454
  31.2 2.4 %collective-permute-start.5 = (bf16[3,896,128]{2,1,0:T(8,128)(2,1)S(1)}, bf16[3,896,128]{2,1,0:T(8,128)(2,1)S(1)}, u32[]{:S(2)}, u32[]{:S(2)}) collective-permute-start(bf16[3,896,128]{2,1,0:T(8,128)(2,1)S(1)} %collective-permute-done.2.refs_4_.refs_1_), channel_id=1, source_target_pairs={{0,1},{1,0},{2,3},{3,2},{4,5},{5,4},{6,7},{7,6},{8,9},{9,8},{10,11... | collective-permute-start | bytes 2064392 | tf_op jit(solution)/shard_map/ppermute | solution.py:422
  31.3 12.8 %collective-permute-start.4 = (bf16[3,896,128]{2,1,0:T(8,128)(2,1)S(1)}, bf16[3,896,128]{2,1,0:T(8,128)(2,1)S(1)}, u32[]{:S(2)}, u32[]{:S(2)}) collective-permute-start(bf16[3,896,128]{2,1,0:T(8,128)(2,1)S(1)} %collective-permute-done.2.refs_4_.refs_1_), channel_id=1, source_target_pairs={{4,0},{6,2},{0,3},{2,1},{20,16},{22,18},{16,19},{18,17}} | collective-permute-start | bytes 2064392 | tf_op jit(solution)/shard_map/ppermute | solution.py:454
  44.1 4.1 %collective-permute-start.6 = (bf16[3,896,128]{2,1,0:T(8,128)(2,1)S(1)}, bf16[3,896,128]{2,1,0:T(8,128)(2,1)S(1)}, u32[]{:S(2)}, u32[]{:S(2)}) collective-permute-start(bf16[3,896,128]{2,1,0:T(8,128)(2,1)S(1)} %collective-permute-done.4.refs_4_.refs_1_), channel_id=1, source_target_pairs={{0,1},{1,0},{2,3},{3,2},{4,5},{5,4},{6,7},{7,6},{8,9},{9,8},{10,11... | collective-permute-start | bytes 2064392 | tf_op jit(solution)/shard_map/ppermute | solution.py:422
  44.2 14.4 %collective-permute-start.7 = (bf16[3,896,128]{2,1,0:T(8,128)(2,1)S(1)}, bf16[3,896,128]{2,1,0:T(8,128)(2,1)S(1)}, u32[]{:S(2)}, u32[]{:S(2)}) collective-permute-start(bf16[3,896,128]{2,1,0:T(8,128)(2,1)S(1)} %collective-permute-done.4.refs_4_.refs_1_), channel_id=1, source_target_pairs={{0,3},{2,1},{16,19},{18,17}} | collective-permute-start | bytes 2064392 | tf_op jit(solution)/shard_map/ppermute | solution.py:454
  58.6 2.2 %collective-permute-start.8 = (bf16[3,896,128]{2,1,0:T(8,128)(2,1)S(1)}, bf16[3,896,128]{2,1,0:T(8,128)(2,1)S(1)}, u32[]{:S(2)}, u32[]{:S(2)}) collective-permute-start(bf16[3,896,128]{2,1,0:T(8,128)(2,1)S(1)} %collective-permute-done.7.refs_4_), channel_id=1, source_target_pairs={{0,1},{1,0},{2,3},{3,2},{4,5},{5,4},{6,7},{7,6},{8,9},{9,8},{10,11... | collective-permute-start | bytes 2064392 | tf_op jit(solution)/shard_map/ppermute | solution.py:422
  105.5 1.3 %collective-permute-start.9 = (bf16[128,128]{1,0:T(8,128)(2,1)S(1)}, bf16[128,128]{1,0:T(8,128)(2,1)S(1)}, u32[]{:S(2)}, u32[]{:S(2)}) collective-permute-start(bf16[128,128]{1,0:T(8,128)(2,1)S(1)} %get-tuple-element.62), channel_id=1, source_target_pairs={{0,1},{1,0},{2,3},{3,2},{4,5},{5,4},{6,7},{7,6},{8,9},{9,8},{10,11... | collective-permute-start | bytes 98312 | tf_op jit(solution)/shard_map/ppermute | solution.py:422
  106.8 5.8 %collective-permute-start.10 = (bf16[2,4,16,128]{3,2,0,1:T(8,128)(2,1)S(1)}, bf16[2,4,16,128]{3,2,0,1:T(8,128)(2,1)S(1)}, u32[]{:S(2)}, u32[]{:S(2)}) collective-permute-start(bf16[2,4,16,128]{3,2,0,1:T(8,128)(2,1)S(1)} %get-tuple-element.68), channel_id=1, source_target_pairs={{0,2},{2,0},{1,3},{3,1},{16,18},{18,16},{17,19},{19,17}} | collective-permute-start | bytes 98312 | tf_op jit(solution)/shard_map/ppermute | solution.py:510
  112.7 3.9 %collective-permute-start.11 = (bf16[4,16,128]{2,1,0:T(8,128)(2,1)S(1)}, bf16[4,16,128]{2,1,0:T(8,128)(2,1)S(1)}, u32[]{:S(2)}, u32[]{:S(2)}) collective-permute-start(bf16[4,16,128]{2,1,0:T(8,128)(2,1)S(1)} %get-tuple-element.65), channel_id=1, source_target_pairs={{0,4},{2,6},{1,5},{3,7},{16,20},{18,22},{17,21},{19,23}} | collective-permute-start | bytes 49160 | tf_op jit(solution)/shard_map/ppermute | solution.py:515
  114.0 2.7 %collective-permute-start.12 = (bf16[4,16,128]{2,1,0:T(8,128)(2,1)S(1)}, bf16[4,16,128]{2,1,0:T(8,128)(2,1)S(1)}, u32[]{:S(2)}, u32[]{:S(2)}) collective-permute-start(bf16[4,16,128]{2,1,0:T(8,128)(2,1)S(1)} %get-tuple-element.64), channel_id=1, source_target_pairs={{0,8},{2,10},{1,9},{3,11},{16,24},{18,26},{17,25},{19,27}} | collective-permute-start | bytes 49160 | tf_op jit(solution)/shard_map/ppermute | solution.py:515
  115.3 2.7 %collective-permute-start.13 = (bf16[4,16,128]{2,1,0:T(8,128)(2,1)S(1)}, bf16[4,16,128]{2,1,0:T(8,128)(2,1)S(1)}, u32[]{:S(2)}, u32[]{:S(2)}) collective-permute-start(bf16[4,16,128]{2,1,0:T(8,128)(2,1)S(1)} %get-tuple-element.63), channel_id=1, source_target_pairs={{0,12},{2,14},{1,13},{3,15},{16,28},{18,30},{17,29},{19,31}} | collective-permute-start | bytes 49160 | tf_op jit(solution)/shard_map/ppermute | solution.py:515

commit v5 on v4

--- a/solution.py
+++ b/solution.py
@@ -215,7 +215,7 @@
         for chosen in GROUPS:
             moves = [MOVES[layer + 1][at] for at in chosen]
             tiles = [tile for move in moves for tile in move[:2]]
-            sums = convolve_pairs(v_refs[layer], w_refs[layer], tiles, layer)
+            sums = [convolve_pairs(v_refs[layer], w_refs[layer], [tile], layer)[0] for tile in tiles]
             sums = [held[tile] + bias + total for tile, total in zip(tiles, sums)]
             for at, move in enumerate(moves):
                 spread(move, sums[2 * at], sums[2 * at + 1], following, v_refs[layer + 1], layer + 1)
@@ -354,13 +354,8 @@
         given[...] = cells_in_rows((x_ref, x_new), 1 - ids_ref[0])
 
 
-def place_kernel(share, *refs):
-    ids_ref, own, *others, out_ref = refs
+def place_kernel(share, pieces, out_ref):
     y_cells = out_ref.shape[-1]
-    first = ids_ref[3] == 0
-    got = others[0][...]
-    for other in others[1:]:
-        got = got + other[...]
     count = 48 * share
     row = lax.broadcasted_iota(jnp.int32, (count, 128), 0) >> (share.bit_length() - 1)
     lane = lax.broadcasted_iota(jnp.int32, (count, 128), 1)
@@ -368,9 +363,8 @@
     place = step * 64 + (row & 3) * 16 + ((row >> 2) & 1) * 3 + ((row >> 3) - 3 * step)
     chosen = [jnp.where(lane == place + 8 * upper, 1.0, 0.0).astype(jnp.bfloat16) for upper in range(2)]
     own_z = lax.broadcasted_iota(jnp.int32, (count, y_cells), 0) & (share - 1)
-    for crop in range(own.shape[0]):
-        piece = jnp.where(first, own[crop].astype(jnp.float32), got[crop].astype(jnp.float32)).astype(jnp.bfloat16)
-        lower, upper = [nt_dot(one, piece) for one in chosen]
+    for crop in range(pieces.shape[0]):
+        lower, upper = [nt_dot(one, pieces[crop]) for one in chosen]
         cells = jnp.zeros((count, y_cells), jnp.float32)
         for z in range(share):
             both = jnp.concatenate([lower[:, 8 * z : 8 * z + 8], upper[:, 8 * z : 8 * z + 8]], axis=1)
@@ -505,21 +499,16 @@
     share = z_cells // segments
     got = between_cores(given)
     pair = jnp.where(slab_id == 0, jnp.stack([kept, got]), jnp.stack([got, kept]))
-    pair = pair.reshape(slabs, levels, lines, share * 8, 128)
-    mine = lax.dynamic_index_in_dim(pair, line, 2, keepdims=False)
-    got = lax.ppermute(lax.dynamic_index_in_dim(pair, 1 - line, 2, keepdims=False), "segment", swap)
-    crops = jnp.where(line == 0, jnp.concatenate([mine, got]), jnp.concatenate([got, mine]))
-    pieces = [crops[:, 0]]
-    for level in range(1, levels):
-        pairs = [(s, level * lines + s) for s in range(lines)]
-        pieces.append(lax.ppermute(crops[:, level], "segment", pairs))
+    pieces = pair.reshape(slabs, segments, share * 8, 128).transpose(1, 0, 2, 3)
+    pieces = lax.all_to_all(pieces, "segment", 0, 0, tiled=True)
+    pieces = pieces[:lines].reshape(crop_count, share * 8, 128)
     out = pl.pallas_call(
         functools.partial(place_kernel, share),
         out_shape=jax.ShapeDtypeStruct((STEPS, crop_count, comps, slab_rows, share, y_cells), jnp.float32),
-        in_specs=[smem] + [vmem] * levels,
+        in_specs=[vmem],
         out_specs=vmem,
         compiler_params=params,
-    )(ids, *pieces)
+    )(pieces)
     return out.transpose(0, 1, 2, 3, 5, 4)
 
 

time: 120 us -> 119 us (level)
  blocking collectives: 0 us -> 9.29 us
  starting transfers between devices: 21.1 us -> 15.2 us
  waiting for transfers between devices: 13.2 us -> 8.02 us
    all_to_all x0 -> x1, blocking collectives: none -> 9.29 us  [shards(): pieces = lax.all_to_all(pieces, 'segment', 0, 0, tiled=True)]
    ppermute x4 -> x0, starting transfers between devices: 5.98 us -> none  [the longest x3 3.87 us: shards(): pieces.append(lax.ppermute(crops[:, level], 'segment', pairs))]
    ppermute x4 -> x0, waiting for transfers between devices: 5.1 us -> none  [the longest x1 3.68 us: shards(): lax.ppermute(lax.dynamic_index_in_dim(pair, 1 - line, 2, keepdims=False),...]
  transfers between devices with their start and end apart: 14 -> 10, of which waited for: 8 -> 4; matrix products, arithmetic and copies ran while one was open for 1% -> 1% of each run, Pallas kernels for 27% -> 28%
where the time goes in v5:
time: 119 us; the launch traced here: 118 us
  Pallas kernels  80.2 us (67%)
  starting transfers between devices  15.2 us (13%)
  blocking collectives  9.29 us (8%)
  waiting for transfers between devices  8.02 us (7%)
  local copies, waits for them, and re-layouts  5.33 us (4%)
    pallas_call x4, Pallas kernels, shards(): pl.pallas_call(functools.partial(level_kernel, level, level == 0, level =...  43.3 us
    pallas_call x1, Pallas kernels, shards(): pl.pallas_call(second_kernel, grid=(segments,), out_shape=(jax.ShapeDtype...  34.3 us
    ppermute x4, starting transfers between devices, hand_on(): return lax.ppermute(value, ('segment', 'slab'), pairs)  14.6 us
    all_to_all x1, blocking collectives, shards(): pieces = lax.all_to_all(pieces, 'segment', 0, 0, tiled=True)  9.29 us
    ppermute x6, waiting for transfers between devices, between_cores(): return lax.ppermute(value, 'slab', swap)  4.4 us
    unnamed x10, local copies, waits for them, and re-layouts  3.89 us
    ppermute x4, waiting for transfers between devices, hand_on(): return lax.ppermute(value, ('segment', 'slab'), pairs)  3.62 us
  transfers between devices with their start and end apart: 10, of which 4 were waited for; matrix products, arithmetic and copies ran while one was open for 1% of the time, Pallas kernels for 28%

profile of v5, /device:TPU:0, one launch (start us, length us, event | category | flops | bytes accessed | tf_op | source)
XLA Modules:
  0.0 118.3 jit_solution(1019191196675021384)
XLA Ops:
  0.0 0.0 copy-start
  0.0 1.2 copy-done
  1.2 0.7 copy-done.4
  1.9 0.5 shard_map.64.refs_1_.refs_2_
  2.4 4.3 %collective-permute-start = (bf16[3,896,128]{2,1,0:T(8,128)(2,1)S(1)}, bf16[3,896,128]{2,1,0:T(8,128)(2,1)S(1)}, u32[]{:S(2)}, u32[]{:S(2)}) collective-permute-start(bf16[3,896,128]{2,1,0:T(8,128)(2,1)S(1)} %shard_map.64.refs_1_.refs_2_), channel_id=1, source_target_pairs={{4,0},{6,2},{8,4},{10,6},{12,8},{14,10},{0,3},{2,1},{20,16},{22,18... | collective-permute-start | bytes 2064392 | tf_op jit(solution)/shard_map/ppermute | solution.py:448
  6.8 1.4 %reshape.15.kept_ref = f32[4,3,8,256]{3,2,1,0:T(8,128)S(1)} reshape(f32[4,3,8,16,16]{4,3,2,1,0:T(8,128)} %param.6) | data formatting | bytes 196608 | tf_op jit(solution)/shard_map/reshape | solution.py:426
  8.2 0.1 collective-permute-start.1
  8.3 0.1 pad_add_fusion.ids_ref.refs_0_
  8.4 1.2 %collective-permute-done.1.got_ref = f32[4,3,8,256]{3,2,1,0:T(8,128)S(1)} collective-permute-done((f32[4,3,8,256]{3,2,1,0:T(8,128)S(1)}, f32[4,3,8,256]{3,2,1,0:T(8,128)S(1)}, u32[]{:S(2)}, u32[]{:S(2)}) %collective-permute-start.1) | collective-permute-done | bytes 98336 | tf_op jit(solution)/shard_map/ppermute | solution.py:416
  9.6 0.7 copy-done.1
  10.2 0.7 copy-done.2
  10.9 0.7 copy-done.3
  11.6 1.1 shard_map.65
  12.7 3.6 %collective-permute-done.refs_4_.refs_1_ = bf16[3,896,128]{2,1,0:T(8,128)(2,1)S(1)} collective-permute-done((bf16[3,896,128]{2,1,0:T(8,128)(2,1)S(1)}, bf16[3,896,128]{2,1,0:T(8,128)(2,1)S(1)}, u32[]{:S(2)}, u32[]{:S(2)}) %collective-permute-start) | collective-permute-done | bytes 688160 | tf_op jit(solution)/shard_map/ppermute | solution.py:448
  16.3 0.1 collective-permute-start.3
  16.3 3.9 %collective-permute-start.2 = (bf16[3,896,128]{2,1,0:T(8,128)(2,1)S(1)}, bf16[3,896,128]{2,1,0:T(8,128)(2,1)S(1)}, u32[]{:S(2)}, u32[]{:S(2)}) collective-permute-start(bf16[3,896,128]{2,1,0:T(8,128)(2,1)S(1)} %collective-permute-done.refs_4_.refs_1_), channel_id=1, source_target_pairs={{4,0},{6,2},{8,4},{10,6},{0,3},{2,1},{20,16},{22,18},{24,20},{26,2... | collective-permute-start | bytes 2064392 | tf_op jit(solution)/shard_map/ppermute | solution.py:448
  20.3 11.0 %shard_map.66 = (bf16[8,2,4,256,384]{4,3,2,1,0:T(8,128)(2,1)}, bf16[8,1024,768]{2,1,0:T(8,128)(2,1)}, f32[8,3,8,128]{3,2,1,0:T(8,128)S(1)}, bf16[8,16,16,128]{3,2,1,0:T(8,128)(2,1)S(1)}, f32[16,2048]{1,0:T(8,128)S(1)}) custom-call(s32[4]{0:T(128)S(1)} %pad_add_fusion.ids_ref.refs_0_, bf16[3,896,128]{2,1,0:T(8,128)(2,1)S(1)} %shard_map.64.refs_1_.refs_2_, ...), custom_call_target="tpu_custom_call" | custom-call | flops 6442450944 | bytes 4194304 | tf_op jit(solution)/shard_map/pallas_call | solution.py:458
  31.3 0.1 collective-permute-start.5
  31.4 2.3 %collective-permute-start.4 = (bf16[3,896,128]{2,1,0:T(8,128)(2,1)S(1)}, bf16[3,896,128]{2,1,0:T(8,128)(2,1)S(1)}, u32[]{:S(2)}, u32[]{:S(2)}) collective-permute-start(bf16[3,896,128]{2,1,0:T(8,128)(2,1)S(1)} %collective-permute-done.2.refs_4_.refs_1_), channel_id=1, source_target_pairs={{4,0},{6,2},{0,3},{2,1},{20,16},{22,18},{16,19},{18,17}} | collective-permute-start | bytes 2064392 | tf_op jit(solution)/shard_map/ppermute | solution.py:448
  33.7 10.5 %shard_map.67 = (bf16[8,2,4,256,384]{4,3,2,1,0:T(8,128)(2,1)}, bf16[8,1024,768]{2,1,0:T(8,128)(2,1)}, f32[8,3,8,128]{3,2,1,0:T(8,128)S(1)}, bf16[8,16,16,128]{3,2,1,0:T(8,128)(2,1)S(1)}, f32[16,2048]{1,0:T(8,128)S(1)}) custom-call(s32[4]{0:T(128)S(1)} %pad_add_fusion.ids_ref.refs_0_, ...), custom_call_target="tpu_custom_call", output_to_operand_aliasing={{0}: (9, {}), {1}: (10, {}), {2}: (11, {})} | custom-call | flops 6442450944 | bytes 4194304 | tf_op jit(solution)/shard_map/pallas_call | solution.py:458
  44.1 0.0 collective-permute-done.4.refs_4_.refs_1_
  44.2 0.1 collective-permute-start.6
  44.3 4.1 %collective-permute-start.7 = (bf16[3,896,128]{2,1,0:T(8,128)(2,1)S(1)}, bf16[3,896,128]{2,1,0:T(8,128)(2,1)S(1)}, u32[]{:S(2)}, u32[]{:S(2)}) collective-permute-start(bf16[3,896,128]{2,1,0:T(8,128)(2,1)S(1)} %collective-permute-done.4.refs_4_.refs_1_), channel_id=1, source_target_pairs={{0,3},{2,1},{16,19},{18,17}} | collective-permute-start | bytes 2064392 | tf_op jit(solution)/shard_map/ppermute | solution.py:448
  48.4 10.4 %shard_map.68 = (bf16[8,2,4,256,384]{4,3,2,1,0:T(8,128)(2,1)}, bf16[8,1024,768]{2,1,0:T(8,128)(2,1)}, f32[8,3,8,128]{3,2,1,0:T(8,128)S(1)}, bf16[8,16,16,128]{3,2,1,0:T(8,128)(2,1)S(1)}, f32[16,2048]{1,0:T(8,128)S(1)}) custom-call(s32[4]{0:T(128)S(1)} %pad_add_fusion.ids_ref.refs_0_, ...), custom_call_target="tpu_custom_call", output_to_operand_aliasing={{0}: (9, {}), {1}: (10, {}), {2}: (11, {})} | custom-call | flops 6442450944 | bytes 4194304 | tf_op jit(solution)/shard_map/pallas_call | solution.py:458
  58.9 0.1 collective-permute-start.8
  59.0 2.1 %collective-permute-done.8.refs_3_ = bf16[3,896,128]{2,1,0:T(8,128)(2,1)S(1)} collective-permute-done((bf16[3,896,128]{2,1,0:T(8,128)(2,1)S(1)}, bf16[3,896,128]{2,1,0:T(8,128)(2,1)S(1)}, u32[]{:S(2)}, u32[]{:S(2)}) %collective-permute-start.8) | collective-permute-done | bytes 688160 | tf_op jit(solution)/shard_map/ppermute | solution.py:416
  61.1 11.3 %shard_map.69 = (bf16[8,2,4,256,384]{4,3,2,1,0:T(8,128)(2,1)}, bf16[8,1024,768]{2,1,0:T(8,128)(2,1)}, f32[8,3,8,128]{3,2,1,0:T(8,128)S(1)}, bf16[8,16,16,128]{3,2,1,0:T(8,128)(2,1)}, f32[16,2048]{1,0:T(8,128)S(1)}) custom-call(s32[4]{0:T(128)S(1)} %pad_add_fusion.ids_ref.refs_0_, ...), custom_call_target="tpu_custom_call", output_to_operand_aliasing={{0}: (9, {}), {1}: (10, {}), {2}: (11, {})} | custom-call | flops 6442450944 | bytes 4194304 | tf_op jit(solution)/shard_map/pallas_call | solution.py:458
  72.5 34.3 %shard_map.70 = (bf16[128,128]{1,0:T(8,128)(2,1)S(1)}, bf16[128,128]{1,0:T(8,128)(2,1)S(1)}) custom-call(s32[4]{0:T(128)S(1)} %pad_add_fusion.ids_ref.refs_0_, f32[16,2048]{1,0:T(8,128)S(1)} %get-tuple-element.57.x_ref, bf16[48,128]{1,0:T(8,128)(2,1)S(1)} %get-tuple-element.37.refs_6_.lift_ref, bf16[48,128]{1,0:T(8,128)(2,1)S(1)} %get-tuple-element.38.refs_7_.proj_ref, ...), custom_call_target="tpu_custom_call" | custom-call | flops 25769803776 | bytes 16777216 | tf_op jit(solution)/shard_map/pallas_call | solution.py:482
  106.7 0.2 collective-permute-start.9
  106.9 1.1 collective-permute-done.9
  108.0 9.3 %all_to_all.5 = bf16[8,2,16,128]{3,2,1,0:T(8,128)(2,1)S(1)} all-to-all(bf16[8,2,16,128]{3,2,1,0:T(8,128)(2,1)S(1)} %fusion.1), channel_id=1, replica_groups=mesh['groups'=2,'segment'=8,'slab'=2] {'segment'}, dimensions={0} | all-to-all | bytes 131072 | tf_op jit(solution)/shard_map/all_to_all | solution.py:503
  117.3 1.0 shard_map.71
  (12 shorter events, 0.0 us)
Async XLA Ops:
  0.0 1.2 copy-start
  1.2 0.7 copy-start.4
  2.4 13.8 %collective-permute-start = (bf16[3,896,128]{2,1,0:T(8,128)(2,1)S(1)}, bf16[3,896,128]{2,1,0:T(8,128)(2,1)S(1)}, u32[]{:S(2)}, u32[]{:S(2)}) collective-permute-start(bf16[3,896,128]{2,1,0:T(8,128)(2,1)S(1)} %shard_map.64.refs_1_.refs_2_), channel_id=1, source_target_pairs={{4,0},{6,2},{8,4},{10,6},{12,8},{14,10},{0,3},{2,1},{20,16},{22,18... | collective-permute-start | bytes 2064392 | tf_op jit(solution)/shard_map/ppermute | solution.py:448
  8.2 1.4 %collective-permute-start.1 = (f32[4,3,8,256]{3,2,1,0:T(8,128)S(1)}, f32[4,3,8,256]{3,2,1,0:T(8,128)S(1)}, u32[]{:S(2)}, u32[]{:S(2)}) collective-permute-start(f32[4,3,8,256]{3,2,1,0:T(8,128)S(1)} %reshape.15.kept_ref), channel_id=1, source_target_pairs={{0,1},{1,0},{2,3},{3,2},{4,5},{5,4},{6,7},{7,6},{8,9},{9,8},{10,11... | collective-permute-start | bytes 294920 | tf_op jit(solution)/shard_map/ppermute | solution.py:416
  9.6 0.7 copy-start.1
  10.2 0.7 copy-start.2
  10.9 0.7 copy-start.3
  16.3 4.0 %collective-permute-start.3 = (bf16[3,896,128]{2,1,0:T(8,128)(2,1)S(1)}, bf16[3,896,128]{2,1,0:T(8,128)(2,1)S(1)}, u32[]{:S(2)}, u32[]{:S(2)}) collective-permute-start(bf16[3,896,128]{2,1,0:T(8,128)(2,1)S(1)} %collective-permute-done.refs_4_.refs_1_), channel_id=1, source_target_pairs={{0,1},{1,0},{2,3},{3,2},{4,5},{5,4},{6,7},{7,6},{8,9},{9,8},{10,11... | collective-permute-start | bytes 2064392 | tf_op jit(solution)/shard_map/ppermute | solution.py:416
  16.3 14.9 %collective-permute-start.2 = (bf16[3,896,128]{2,1,0:T(8,128)(2,1)S(1)}, bf16[3,896,128]{2,1,0:T(8,128)(2,1)S(1)}, u32[]{:S(2)}, u32[]{:S(2)}) collective-permute-start(bf16[3,896,128]{2,1,0:T(8,128)(2,1)S(1)} %collective-permute-done.refs_4_.refs_1_), channel_id=1, source_target_pairs={{4,0},{6,2},{8,4},{10,6},{0,3},{2,1},{20,16},{22,18},{24,20},{26,2... | collective-permute-start | bytes 2064392 | tf_op jit(solution)/shard_map/ppermute | solution.py:448
  31.3 2.4 %collective-permute-start.5 = (bf16[3,896,128]{2,1,0:T(8,128)(2,1)S(1)}, bf16[3,896,128]{2,1,0:T(8,128)(2,1)S(1)}, u32[]{:S(2)}, u32[]{:S(2)}) collective-permute-start(bf16[3,896,128]{2,1,0:T(8,128)(2,1)S(1)} %collective-permute-done.2.refs_4_.refs_1_), channel_id=1, source_target_pairs={{0,1},{1,0},{2,3},{3,2},{4,5},{5,4},{6,7},{7,6},{8,9},{9,8},{10,11... | collective-permute-start | bytes 2064392 | tf_op jit(solution)/shard_map/ppermute | solution.py:416
  31.4 12.8 %collective-permute-start.4 = (bf16[3,896,128]{2,1,0:T(8,128)(2,1)S(1)}, bf16[3,896,128]{2,1,0:T(8,128)(2,1)S(1)}, u32[]{:S(2)}, u32[]{:S(2)}) collective-permute-start(bf16[3,896,128]{2,1,0:T(8,128)(2,1)S(1)} %collective-permute-done.2.refs_4_.refs_1_), channel_id=1, source_target_pairs={{4,0},{6,2},{0,3},{2,1},{20,16},{22,18},{16,19},{18,17}} | collective-permute-start | bytes 2064392 | tf_op jit(solution)/shard_map/ppermute | solution.py:448
  44.2 4.2 %collective-permute-start.6 = (bf16[3,896,128]{2,1,0:T(8,128)(2,1)S(1)}, bf16[3,896,128]{2,1,0:T(8,128)(2,1)S(1)}, u32[]{:S(2)}, u32[]{:S(2)}) collective-permute-start(bf16[3,896,128]{2,1,0:T(8,128)(2,1)S(1)} %collective-permute-done.4.refs_4_.refs_1_), channel_id=1, source_target_pairs={{0,1},{1,0},{2,3},{3,2},{4,5},{5,4},{6,7},{7,6},{8,9},{9,8},{10,11... | collective-permute-start | bytes 2064392 | tf_op jit(solution)/shard_map/ppermute | solution.py:416
  44.3 14.6 %collective-permute-start.7 = (bf16[3,896,128]{2,1,0:T(8,128)(2,1)S(1)}, bf16[3,896,128]{2,1,0:T(8,128)(2,1)S(1)}, u32[]{:S(2)}, u32[]{:S(2)}) collective-permute-start(bf16[3,896,128]{2,1,0:T(8,128)(2,1)S(1)} %collective-permute-done.4.refs_4_.refs_1_), channel_id=1, source_target_pairs={{0,3},{2,1},{16,19},{18,17}} | collective-permute-start | bytes 2064392 | tf_op jit(solution)/shard_map/ppermute | solution.py:448
  58.9 2.2 %collective-permute-start.8 = (bf16[3,896,128]{2,1,0:T(8,128)(2,1)S(1)}, bf16[3,896,128]{2,1,0:T(8,128)(2,1)S(1)}, u32[]{:S(2)}, u32[]{:S(2)}) collective-permute-start(bf16[3,896,128]{2,1,0:T(8,128)(2,1)S(1)} %collective-permute-done.7.refs_4_), channel_id=1, source_target_pairs={{0,1},{1,0},{2,3},{3,2},{4,5},{5,4},{6,7},{7,6},{8,9},{9,8},{10,11... | collective-permute-start | bytes 2064392 | tf_op jit(solution)/shard_map/ppermute | solution.py:416
  106.7 1.3 %collective-permute-start.9 = (bf16[128,128]{1,0:T(8,128)(2,1)S(1)}, bf16[128,128]{1,0:T(8,128)(2,1)S(1)}, u32[]{:S(2)}, u32[]{:S(2)}) collective-permute-start(bf16[128,128]{1,0:T(8,128)(2,1)S(1)} %get-tuple-element.62), channel_id=1, source_target_pairs={{0,1},{1,0},{2,3},{3,2},{4,5},{5,4},{6,7},{7,6},{8,9},{9,8},{10,11... | collective-permute-start | bytes 98312 | tf_op jit(solution)/shard_map/ppermute | solution.py:416

commit v6 on v5

--- a/solution.py
+++ b/solution.py
@@ -215,7 +215,7 @@
         for chosen in GROUPS:
             moves = [MOVES[layer + 1][at] for at in chosen]
             tiles = [tile for move in moves for tile in move[:2]]
-            sums = [convolve_pairs(v_refs[layer], w_refs[layer], [tile], layer)[0] for tile in tiles]
+            sums = convolve_pairs(v_refs[layer], w_refs[layer], tiles, layer)
             sums = [held[tile] + bias + total for tile, total in zip(tiles, sums)]
             for at, move in enumerate(moves):
                 spread(move, sums[2 * at], sums[2 * at + 1], following, v_refs[layer + 1], layer + 1)
@@ -231,11 +231,11 @@
     return jnp.concatenate([moved[at * 16 : (at + 1) * 16] for at in range(16)], axis=1)
 
 
-def lift_into(x, lift_ref, s_a):
+def lifted(x, lift):
     high = x.astype(jnp.bfloat16).astype(jnp.float32)
     columns = jnp.concatenate([high, x - high, high], axis=0).T.astype(jnp.bfloat16)
-    hidden = jnp.dot(columns, lift_ref[...], preferred_element_type=jnp.float32)
-    s_a[...] = hidden.astype(jnp.bfloat16).astype(jnp.float32).reshape(8, 16, 16, 128)
+    hidden = jnp.dot(columns, lift, preferred_element_type=jnp.float32)
+    return hidden.astype(jnp.bfloat16).reshape(8, 16, 16, 128)
 
 
 def renewed_fields(x, proj_ref, s_a):
@@ -243,16 +243,13 @@
     return x + gain[:16] + gain[16:32] + gain[32:48]
 
 
-def level_kernel(level, first, last, *refs):
+def level_kernel(level, last, *refs):
     (ids_ref, own_0, own_1, far_0, far_1, x_ref, lift_ref, proj_ref) = refs[:8]
     (w_out, c_out, b_out, leaving, x_out, s_a, s_b, s_c, s_d, v_a, v_b, v_c) = refs[-17:-5]
     (packed, w_pair, w_cycle, b_all, sems) = refs[-5:]
     slab, line = ids_ref[0], ids_ref[1]
-    x = by_parity(x_ref[...]) if first else x_ref[...]
-    if first:
-        lift_into(x, lift_ref, s_a)
-    else:
-        s_a[...] = refs[8][...].astype(jnp.float32)
+    x = x_ref[...]
+    s_a[...] = refs[8][...].astype(jnp.float32)
     state, v_refs = (s_a, s_b, s_c, s_d), (v_a, v_b, v_c)
 
     def copy(turn, part):
@@ -287,7 +284,7 @@
             copy(turn, part).wait()
 
 
-def feature_kernel(ids_ref, anchor_ref, kept_ref, got_ref, lift_ref, proj_ref, x_ref, lift_out, proj_out):
+def feature_kernel(ids_ref, anchor_ref, kept_ref, got_ref, lift_ref, proj_ref, x_ref, lift_out, proj_out, hidden_out):
     slab, slot = ids_ref[0], ids_ref[2]
     kept, got = kept_ref[slot], got_ref[slot]
     halves = (jnp.where(slab == 0, kept, got), jnp.where(slab == 0, got, kept))
@@ -305,7 +302,8 @@
     axis = jnp.where(row >= 9, row - 9, row - 6)
     position = jnp.where(axis == 0, along_x, jnp.where(axis == 1, along_y, along_z)) & (FIELD - 1)
     waves = jnp.sin(2.0 * jnp.pi * position.astype(jnp.float32) / FIELD)
-    x_ref[...] = jnp.where(row < 6, current, jnp.where(row < 12, waves, 0.0))
+    x = by_parity(jnp.where(row < 6, current, jnp.where(row < 12, waves, 0.0)))
+    x_ref[...] = x
 
     def two_halves(part):
         blank = jnp.zeros(part.shape, jnp.float32)
@@ -314,7 +312,9 @@
     lift = 0.5 * lift_ref[...]
     lift = two_halves(lift[0:3]) + two_halves(lift[3:6]) + [jnp.zeros((4, 128), jnp.float32)]
     first, second, unused = [term.astype(jnp.float32) for term in split_terms(jnp.concatenate(lift, axis=0))]
-    lift_out[...] = jnp.concatenate([first, first, second], axis=0).astype(jnp.bfloat16)
+    lift = jnp.concatenate([first, first, second], axis=0).astype(jnp.bfloat16)
+    lift_out[...] = lift
+    hidden_out[...] = lifted(x, lift)
     proj = two_halves(2.0 * proj_ref[...]) + [jnp.zeros((10, 128), jnp.float32)]
     proj = [term.astype(jnp.float32) for term in split_terms(jnp.concatenate(proj, axis=0))]
     proj_out[...] = jnp.concatenate(proj, axis=0).astype(jnp.bfloat16)
@@ -342,7 +342,7 @@
 
     @pl.when(s == 0)
     def begin():
-        lift_into(x_ref[...], lift_ref, s_a)
+        s_a[...] = lifted(x_ref[...], lift_ref[...]).astype(jnp.float32)
 
     w_refs = [w_ref.at[0, 0], w_ref.at[0, 1], c_ref.at[0]]
     run_section(state, v_refs, w_refs, [b_ref.at[0, i] for i in range(LAYERS)], lambda layer: None)
@@ -424,22 +424,23 @@
     )(conv_weight[0], conv_bias.transpose(1, 0, 2), jnp.eye(192, dtype=jnp.bfloat16))
 
     flat = after(fields, packed).reshape(crop_count, comps, slab_rows, y_cells * z_cells)
-    x, lift, proj = pl.pallas_call(
+    h_shape = jax.ShapeDtypeStruct((8, 16, 16, 128), jnp.bfloat16)
+    x, lift, proj, hidden = pl.pallas_call(
         feature_kernel,
         out_shape=(
             jax.ShapeDtypeStruct((16, 2048), jnp.float32),
             jax.ShapeDtypeStruct((48, 128), jnp.bfloat16),
             jax.ShapeDtypeStruct((48, 128), jnp.bfloat16),
+            h_shape,
         ),
         in_specs=[smem, smem] + [vmem] * 4,
-        out_specs=(vmem, vmem, vmem),
+        out_specs=(vmem, vmem, vmem, vmem),
         compiler_params=params,
     )(ids, anchors, flat, between_cores(flat), lift_weight.T, proj_weight)
 
     w_shape = jax.ShapeDtypeStruct((segments, 2, 4, 256, 384), jnp.bfloat16)
     c_shape = jax.ShapeDtypeStruct((segments, 1024, 768), jnp.bfloat16)
     b_shape = jax.ShapeDtypeStruct((segments, LAYERS, 8, 128), jnp.float32)
-    h_shape = jax.ShapeDtypeStruct((8, 16, 16, 128), jnp.bfloat16)
     x_shape = jax.ShapeDtypeStruct((16, 2048), jnp.float32)
     layer_flops = 2 * 4 * 1024 * 256 * 512
     def hand_on(value, level):
@@ -454,11 +455,11 @@
     current = x
     for level in range(levels):
         own = (packed, packed) if level == 0 else (arrived[level - 1], swapped[level - 1])
-        operands = (ids, *own, swapped[level], arrived[level], current, lift, proj, *kept)
+        operands = (ids, *own, swapped[level], arrived[level], current, lift, proj, hidden, *kept)
         weights, cycles, rows, hidden, current = pl.pallas_call(
-            functools.partial(level_kernel, level, level == 0, level == levels - 1),
+            functools.partial(level_kernel, level, level == levels - 1),
             out_shape=(w_shape, c_shape, b_shape, h_shape, x_shape),
-            in_specs=[smem] + [vmem] * 7 + ([vmem] + [anyspace] * 3 if kept else []),
+            in_specs=[smem] + [vmem] * 8 + ([anyspace] * 3 if kept else []),
             out_specs=(anyspace, anyspace, anyspace, vmem, vmem),
             scratch_shapes=state_scratch()
             + [
@@ -472,7 +473,7 @@
             compiler_params=params,
             cost_estimate=pl.CostEstimate(flops=2 * LAYERS * layer_flops, bytes_accessed=4 << 20, transcendentals=0),
         )(*operands)
-        kept = (hidden, weights, cycles, rows)
+        kept = (weights, cycles, rows)
         if level + 1 < levels:
             arrived[level + 1] = after(arrived[level + 1], hidden)
             swapped[level + 1] = between_cores(arrived[level + 1])

time: 119 us -> 117 us (0.983)
  Pallas kernels: 80.2 us -> 78.9 us
where the time goes in v6:
time: 117 us; the launch traced here: 116 us
  Pallas kernels  78.9 us (67%)
  starting transfers between devices  15.2 us (13%)
  blocking collectives  9.29 us (8%)
  waiting for transfers between devices  7.35 us (6%)
  local copies, waits for them, and re-layouts  5.33 us (5%)
    pallas_call x4, Pallas kernels, shards(): pl.pallas_call(functools.partial(level_kernel, level, level == levels - 1...  42.2 us
    pallas_call x1, Pallas kernels, shards(): pl.pallas_call(second_kernel, grid=(segments,), out_shape=(jax.ShapeDtype...  33.4 us
    ppermute x4, starting transfers between devices, hand_on(): return lax.ppermute(value, ('segment', 'slab'), pairs)  14.7 us
    all_to_all x1, blocking collectives, shards(): pieces = lax.all_to_all(pieces, 'segment', 0, 0, tiled=True)  9.29 us
    ppermute x6, waiting for transfers between devices, between_cores(): return lax.ppermute(value, 'slab', swap)  4.4 us
    unnamed x10, local copies, waits for them, and re-layouts  3.89 us
    ppermute x4, waiting for transfers between devices, hand_on(): return lax.ppermute(value, ('segment', 'slab'), pairs)  2.94 us
  transfers between devices with their start and end apart: 10, of which 4 were waited for; matrix products, arithmetic and copies ran while one was open for 1% of the time, Pallas kernels for 28%

profile of v6, /device:TPU:0, one launch (start us, length us, event | category | flops | bytes accessed | tf_op | source)
XLA Modules:
  0.0 116.4 jit_solution(1041976344869864711)
XLA Ops:
  0.0 0.0 copy-start
  0.0 1.2 copy-done
  1.2 0.7 copy-done.4
  1.9 0.5 shard_map.64.refs_1_.refs_2_
  2.4 4.3 %collective-permute-start = (bf16[3,896,128]{2,1,0:T(8,128)(2,1)S(1)}, bf16[3,896,128]{2,1,0:T(8,128)(2,1)S(1)}, u32[]{:S(2)}, u32[]{:S(2)}) collective-permute-start(bf16[3,896,128]{2,1,0:T(8,128)(2,1)S(1)} %shard_map.64.refs_1_.refs_2_), channel_id=1, source_target_pairs={{4,0},{6,2},{8,4},{10,6},{12,8},{14,10},{0,3},{2,1},{20,16},{22,18... | collective-permute-start | bytes 2064392 | tf_op jit(solution)/shard_map/ppermute | solution.py:449
  6.8 1.4 %reshape.15.kept_ref = f32[4,3,8,256]{3,2,1,0:T(8,128)S(1)} reshape(f32[4,3,8,16,16]{4,3,2,1,0:T(8,128)} %param.6) | data formatting | bytes 196608 | tf_op jit(solution)/shard_map/reshape | solution.py:426
  8.2 0.1 collective-permute-start.1
  8.3 0.1 pad_add_fusion.ids_ref.refs_0_
  8.4 1.2 %collective-permute-done.1.got_ref = f32[4,3,8,256]{3,2,1,0:T(8,128)S(1)} collective-permute-done((f32[4,3,8,256]{3,2,1,0:T(8,128)S(1)}, f32[4,3,8,256]{3,2,1,0:T(8,128)S(1)}, u32[]{:S(2)}, u32[]{:S(2)}) %collective-permute-start.1) | collective-permute-done | bytes 98336 | tf_op jit(solution)/shard_map/ppermute | solution.py:416
  9.6 0.7 copy-done.1
  10.2 0.7 copy-done.2
  10.9 0.7 copy-done.3
  11.6 1.7 %shard_map.65 = (f32[16,2048]{1,0:T(8,128)S(1)}, bf16[48,128]{1,0:T(8,128)(2,1)S(1)}, bf16[48,128]{1,0:T(8,128)(2,1)S(1)}, bf16[8,16,16,128]{3,2,1,0:T(8,128)(2,1)S(1)}) custom-call(s32[4]{0:T(128)S(1)} %pad_add_fusion.ids_ref.refs_0_, s32[4,3]{1,0:T(4,128)S(1)} %copy-done.2, f32[4,3,8,256]{3,2,1,0:T(8,128)S(1)} %reshape.15.kept_ref, ...), custom_call_target="tpu_custom_call" | custom-call | tf_op jit(solution)/shard_map/pallas_call | solution.py:428
  13.3 2.9 %collective-permute-done.refs_4_.refs_1_ = bf16[3,896,128]{2,1,0:T(8,128)(2,1)S(1)} collective-permute-done((bf16[3,896,128]{2,1,0:T(8,128)(2,1)S(1)}, bf16[3,896,128]{2,1,0:T(8,128)(2,1)S(1)}, u32[]{:S(2)}, u32[]{:S(2)}) %collective-permute-start) | collective-permute-done | bytes 688160 | tf_op jit(solution)/shard_map/ppermute | solution.py:449
  16.3 0.1 collective-permute-start.3
  16.3 3.9 %collective-permute-start.2 = (bf16[3,896,128]{2,1,0:T(8,128)(2,1)S(1)}, bf16[3,896,128]{2,1,0:T(8,128)(2,1)S(1)}, u32[]{:S(2)}, u32[]{:S(2)}) collective-permute-start(bf16[3,896,128]{2,1,0:T(8,128)(2,1)S(1)} %collective-permute-done.refs_4_.refs_1_), channel_id=1, source_target_pairs={{4,0},{6,2},{8,4},{10,6},{0,3},{2,1},{20,16},{22,18},{24,20},{26,2... | collective-permute-start | bytes 2064392 | tf_op jit(solution)/shard_map/ppermute | solution.py:449
  20.3 10.3 %shard_map.66 = (bf16[8,2,4,256,384]{4,3,2,1,0:T(8,128)(2,1)}, bf16[8,1024,768]{2,1,0:T(8,128)(2,1)}, f32[8,3,8,128]{3,2,1,0:T(8,128)S(1)}, bf16[8,16,16,128]{3,2,1,0:T(8,128)(2,1)S(1)}, f32[16,2048]{1,0:T(8,128)S(1)}) custom-call(s32[4]{0:T(128)S(1)} %pad_add_fusion.ids_ref.refs_0_, bf16[3,896,128]{2,1,0:T(8,128)(2,1)S(1)} %shard_map.64.refs_1_.refs_2_, ...), custom_call_target="tpu_custom_call" | custom-call | flops 6442450944 | bytes 4194304 | tf_op jit(solution)/shard_map/pallas_call | solution.py:459
  30.6 0.0 collective-permute-done.2.refs_4_.refs_1_
  30.6 0.1 collective-permute-start.5
  30.7 2.6 %collective-permute-start.4 = (bf16[3,896,128]{2,1,0:T(8,128)(2,1)S(1)}, bf16[3,896,128]{2,1,0:T(8,128)(2,1)S(1)}, u32[]{:S(2)}, u32[]{:S(2)}) collective-permute-start(bf16[3,896,128]{2,1,0:T(8,128)(2,1)S(1)} %collective-permute-done.2.refs_4_.refs_1_), channel_id=1, source_target_pairs={{4,0},{6,2},{0,3},{2,1},{20,16},{22,18},{16,19},{18,17}} | collective-permute-start | bytes 2064392 | tf_op jit(solution)/shard_map/ppermute | solution.py:449
  33.3 10.3 %shard_map.67 = (bf16[8,2,4,256,384]{4,3,2,1,0:T(8,128)(2,1)}, bf16[8,1024,768]{2,1,0:T(8,128)(2,1)}, f32[8,3,8,128]{3,2,1,0:T(8,128)S(1)}, bf16[8,16,16,128]{3,2,1,0:T(8,128)(2,1)S(1)}, f32[16,2048]{1,0:T(8,128)S(1)}) custom-call(s32[4]{0:T(128)S(1)} %pad_add_fusion.ids_ref.refs_0_, ...), custom_call_target="tpu_custom_call", output_to_operand_aliasing={{0}: (9, {}), {1}: (10, {}), {2}: (11, {})} | custom-call | flops 6442450944 | bytes 4194304 | tf_op jit(solution)/shard_map/pallas_call | solution.py:459
  43.6 0.1 collective-permute-start.6
  43.7 3.9 %collective-permute-start.7 = (bf16[3,896,128]{2,1,0:T(8,128)(2,1)S(1)}, bf16[3,896,128]{2,1,0:T(8,128)(2,1)S(1)}, u32[]{:S(2)}, u32[]{:S(2)}) collective-permute-start(bf16[3,896,128]{2,1,0:T(8,128)(2,1)S(1)} %collective-permute-done.4.refs_4_.refs_1_), channel_id=1, source_target_pairs={{0,3},{2,1},{16,19},{18,17}} | collective-permute-start | bytes 2064392 | tf_op jit(solution)/shard_map/ppermute | solution.py:449
  47.6 10.3 %shard_map.68 = (bf16[8,2,4,256,384]{4,3,2,1,0:T(8,128)(2,1)}, bf16[8,1024,768]{2,1,0:T(8,128)(2,1)}, f32[8,3,8,128]{3,2,1,0:T(8,128)S(1)}, bf16[8,16,16,128]{3,2,1,0:T(8,128)(2,1)S(1)}, f32[16,2048]{1,0:T(8,128)S(1)}) custom-call(s32[4]{0:T(128)S(1)} %pad_add_fusion.ids_ref.refs_0_, ...), custom_call_target="tpu_custom_call", output_to_operand_aliasing={{0}: (9, {}), {1}: (10, {}), {2}: (11, {})} | custom-call | flops 6442450944 | bytes 4194304 | tf_op jit(solution)/shard_map/pallas_call | solution.py:459
  58.0 0.1 collective-permute-start.8
  58.1 2.1 %collective-permute-done.8.refs_3_ = bf16[3,896,128]{2,1,0:T(8,128)(2,1)S(1)} collective-permute-done((bf16[3,896,128]{2,1,0:T(8,128)(2,1)S(1)}, bf16[3,896,128]{2,1,0:T(8,128)(2,1)S(1)}, u32[]{:S(2)}, u32[]{:S(2)}) %collective-permute-start.8) | collective-permute-done | bytes 688160 | tf_op jit(solution)/shard_map/ppermute | solution.py:416
  60.2 11.2 %shard_map.69 = (bf16[8,2,4,256,384]{4,3,2,1,0:T(8,128)(2,1)}, bf16[8,1024,768]{2,1,0:T(8,128)(2,1)}, f32[8,3,8,128]{3,2,1,0:T(8,128)S(1)}, bf16[8,16,16,128]{3,2,1,0:T(8,128)(2,1)}, f32[16,2048]{1,0:T(8,128)S(1)}) custom-call(s32[4]{0:T(128)S(1)} %pad_add_fusion.ids_ref.refs_0_, ...), custom_call_target="tpu_custom_call", output_to_operand_aliasing={{0}: (9, {}), {1}: (10, {}), {2}: (11, {})} | custom-call | flops 6442450944 | bytes 4194304 | tf_op jit(solution)/shard_map/pallas_call | solution.py:459
  71.4 33.4 %shard_map.70 = (bf16[128,128]{1,0:T(8,128)(2,1)S(1)}, bf16[128,128]{1,0:T(8,128)(2,1)S(1)}) custom-call(s32[4]{0:T(128)S(1)} %pad_add_fusion.ids_ref.refs_0_, f32[16,2048]{1,0:T(8,128)S(1)} %get-tuple-element.59.x_ref, bf16[48,128]{1,0:T(8,128)(2,1)S(1)} %get-tuple-element.38.refs_6_.lift_ref, bf16[48,128]{1,0:T(8,128)(2,1)S(1)} %get-tuple-element.39.refs_7_.proj_ref, ...), custom_call_target="tpu_custom_call" | custom-call | flops 25769803776 | bytes 16777216 | tf_op jit(solution)/shard_map/pallas_call | solution.py:483
  104.9 0.2 collective-permute-start.9
  105.1 1.1 collective-permute-done.9
  106.2 9.3 %all_to_all.5 = bf16[8,2,16,128]{3,2,1,0:T(8,128)(2,1)S(1)} all-to-all(bf16[8,2,16,128]{3,2,1,0:T(8,128)(2,1)S(1)} %fusion.1), channel_id=1, replica_groups=mesh['groups'=2,'segment'=8,'slab'=2] {'segment'}, dimensions={0} | all-to-all | bytes 131072 | tf_op jit(solution)/shard_map/all_to_all | solution.py:504
  115.4 1.0 shard_map.71
  (12 shorter events, 0.0 us)
Async XLA Ops:
  0.0 1.2 %copy-start = (bf16[1,3,9,64,192]{4,3,2,1,0:T(8,128)(2,1)S(1)}, bf16[1,3,9,64,192]{4,3,2,1,0:T(8,128)(2,1)}, u32[]{:S(2)}) copy-start(bf16[1,3,9,64,192]{4,3,2,1,0:T(8,128)(2,1)} %param.9) | copy-start | bytes 1990660
  1.2 0.7 copy-start.4
  2.4 13.8 %collective-permute-start = (bf16[3,896,128]{2,1,0:T(8,128)(2,1)S(1)}, bf16[3,896,128]{2,1,0:T(8,128)(2,1)S(1)}, u32[]{:S(2)}, u32[]{:S(2)}) collective-permute-start(bf16[3,896,128]{2,1,0:T(8,128)(2,1)S(1)} %shard_map.64.refs_1_.refs_2_), channel_id=1, source_target_pairs={{4,0},{6,2},{8,4},{10,6},{12,8},{14,10},{0,3},{2,1},{20,16},{22,18... | collective-permute-start | bytes 2064392 | tf_op jit(solution)/shard_map/ppermute | solution.py:449
  8.2 1.4 %collective-permute-start.1 = (f32[4,3,8,256]{3,2,1,0:T(8,128)S(1)}, f32[4,3,8,256]{3,2,1,0:T(8,128)S(1)}, u32[]{:S(2)}, u32[]{:S(2)}) collective-permute-start(f32[4,3,8,256]{3,2,1,0:T(8,128)S(1)} %reshape.15.kept_ref), channel_id=1, source_target_pairs={{0,1},{1,0},{2,3},{3,2},{4,5},{5,4},{6,7},{7,6},{8,9},{9,8},{10,11... | collective-permute-start | bytes 294920 | tf_op jit(solution)/shard_map/ppermute | solution.py:416
  9.6 0.7 copy-start.1
  10.2 0.7 copy-start.2
  10.9 0.7 copy-start.3
  16.3 4.0 %collective-permute-start.3 = (bf16[3,896,128]{2,1,0:T(8,128)(2,1)S(1)}, bf16[3,896,128]{2,1,0:T(8,128)(2,1)S(1)}, u32[]{:S(2)}, u32[]{:S(2)}) collective-permute-start(bf16[3,896,128]{2,1,0:T(8,128)(2,1)S(1)} %collective-permute-done.refs_4_.refs_1_), channel_id=1, source_target_pairs={{0,1},{1,0},{2,3},{3,2},{4,5},{5,4},{6,7},{7,6},{8,9},{9,8},{10,11... | collective-permute-start | bytes 2064392 | tf_op jit(solution)/shard_map/ppermute | solution.py:416
  16.3 14.2 %collective-permute-start.2 = (bf16[3,896,128]{2,1,0:T(8,128)(2,1)S(1)}, bf16[3,896,128]{2,1,0:T(8,128)(2,1)S(1)}, u32[]{:S(2)}, u32[]{:S(2)}) collective-permute-start(bf16[3,896,128]{2,1,0:T(8,128)(2,1)S(1)} %collective-permute-done.refs_4_.refs_1_), channel_id=1, source_target_pairs={{4,0},{6,2},{8,4},{10,6},{0,3},{2,1},{20,16},{22,18},{24,20},{26,2... | collective-permute-start | bytes 2064392 | tf_op jit(solution)/shard_map/ppermute | solution.py:449
  30.6 2.7 %collective-permute-start.5 = (bf16[3,896,128]{2,1,0:T(8,128)(2,1)S(1)}, bf16[3,896,128]{2,1,0:T(8,128)(2,1)S(1)}, u32[]{:S(2)}, u32[]{:S(2)}) collective-permute-start(bf16[3,896,128]{2,1,0:T(8,128)(2,1)S(1)} %collective-permute-done.2.refs_4_.refs_1_), channel_id=1, source_target_pairs={{0,1},{1,0},{2,3},{3,2},{4,5},{5,4},{6,7},{7,6},{8,9},{9,8},{10,11... | collective-permute-start | bytes 2064392 | tf_op jit(solution)/shard_map/ppermute | solution.py:416
  30.7 13.0 %collective-permute-start.4 = (bf16[3,896,128]{2,1,0:T(8,128)(2,1)S(1)}, bf16[3,896,128]{2,1,0:T(8,128)(2,1)S(1)}, u32[]{:S(2)}, u32[]{:S(2)}) collective-permute-start(bf16[3,896,128]{2,1,0:T(8,128)(2,1)S(1)} %collective-permute-done.2.refs_4_.refs_1_), channel_id=1, source_target_pairs={{4,0},{6,2},{0,3},{2,1},{20,16},{22,18},{16,19},{18,17}} | collective-permute-start | bytes 2064392 | tf_op jit(solution)/shard_map/ppermute | solution.py:449
  43.6 4.0 %collective-permute-start.6 = (bf16[3,896,128]{2,1,0:T(8,128)(2,1)S(1)}, bf16[3,896,128]{2,1,0:T(8,128)(2,1)S(1)}, u32[]{:S(2)}, u32[]{:S(2)}) collective-permute-start(bf16[3,896,128]{2,1,0:T(8,128)(2,1)S(1)} %collective-permute-done.4.refs_4_.refs_1_), channel_id=1, source_target_pairs={{0,1},{1,0},{2,3},{3,2},{4,5},{5,4},{6,7},{7,6},{8,9},{9,8},{10,11... | collective-permute-start | bytes 2064392 | tf_op jit(solution)/shard_map/ppermute | solution.py:416
  43.7 14.3 %collective-permute-start.7 = (bf16[3,896,128]{2,1,0:T(8,128)(2,1)S(1)}, bf16[3,896,128]{2,1,0:T(8,128)(2,1)S(1)}, u32[]{:S(2)}, u32[]{:S(2)}) collective-permute-start(bf16[3,896,128]{2,1,0:T(8,128)(2,1)S(1)} %collective-permute-done.4.refs_4_.refs_1_), channel_id=1, source_target_pairs={{0,3},{2,1},{16,19},{18,17}} | collective-permute-start | bytes 2064392 | tf_op jit(solution)/shard_map/ppermute | solution.py:449
  58.0 2.2 %collective-permute-start.8 = (bf16[3,896,128]{2,1,0:T(8,128)(2,1)S(1)}, bf16[3,896,128]{2,1,0:T(8,128)(2,1)S(1)}, u32[]{:S(2)}, u32[]{:S(2)}) collective-permute-start(bf16[3,896,128]{2,1,0:T(8,128)(2,1)S(1)} %collective-permute-done.7.refs_4_), channel_id=1, source_target_pairs={{0,1},{1,0},{2,3},{3,2},{4,5},{5,4},{6,7},{7,6},{8,9},{9,8},{10,11... | collective-permute-start | bytes 2064392 | tf_op jit(solution)/shard_map/ppermute | solution.py:416
  104.9 1.3 %collective-permute-start.9 = (bf16[128,128]{1,0:T(8,128)(2,1)S(1)}, bf16[128,128]{1,0:T(8,128)(2,1)S(1)}, u32[]{:S(2)}, u32[]{:S(2)}) collective-permute-start(bf16[128,128]{1,0:T(8,128)(2,1)S(1)} %get-tuple-element.64), channel_id=1, source_target_pairs={{0,1},{1,0},{2,3},{3,2},{4,5},{5,4},{6,7},{7,6},{8,9},{9,8},{10,11... | collective-permute-start | bytes 98312 | tf_op jit(solution)/shard_map/ppermute | solution.py:416

commit v7 on v6

--- a/solution.py
+++ b/solution.py
@@ -335,23 +335,37 @@
     return nt_dot(turned, jnp.concatenate(blocks, axis=0).astype(jnp.bfloat16)).astype(jnp.bfloat16)
 
 
-def second_kernel(ids_ref, x_ref, lift_ref, proj_ref, w_ref, c_ref, b_ref, kept, given, s_a, s_b, s_c, s_d, v_a, v_b, v_c, x_new):
-    s = pl.program_id(0)
-
-    state, v_refs = (s_a, s_b, s_c, s_d), (v_a, v_b, v_c)
-
-    @pl.when(s == 0)
-    def begin():
-        s_a[...] = lifted(x_ref[...], lift_ref[...]).astype(jnp.float32)
-
-    w_refs = [w_ref.at[0, 0], w_ref.at[0, 1], c_ref.at[0]]
-    run_section(state, v_refs, w_refs, [b_ref.at[0, i] for i in range(LAYERS)], lambda layer: None)
-
-    @pl.when(s == pl.num_programs(0) - 1)
-    def finish():
-        x_new[...] = renewed_fields(x_ref[...], proj_ref, s_a)
-        kept[...] = cells_in_rows((x_ref, x_new), ids_ref[0])
-        given[...] = cells_in_rows((x_ref, x_new), 1 - ids_ref[0])
+def second_kernel(ids_ref, x_ref, lift_ref, proj_ref, w_hbm, c_hbm, b_hbm, kept, given, *scratch):
+    s_a, s_b, s_c, s_d, v_a, v_b, v_c, x_new, w_all, c_all, b_all, sems = scratch
+    sections = w_hbm.shape[0]
+
+    def copy(s, slot, part):
+        source, target = ((w_hbm, w_all), (c_hbm, c_all), (b_hbm, b_all))[part]
+        return pltpu.make_async_copy(source.at[s], target.at[slot], sems.at[slot, part])
+
+    for part in range(3):
+        copy(0, 0, part).start()
+    s_a[...] = lifted(x_ref[...], lift_ref[...]).astype(jnp.float32)
+
+    def section(s, unused):
+        slot = lax.rem(s, 2)
+        for part in range(3):
+            copy(s, slot, part).wait()
+
+        @pl.when(s + 1 < sections)
+        def fetch():
+            for part in range(3):
+                copy(s + 1, 1 - slot, part).start()
+
+        w_refs = [w_all.at[slot, 0], w_all.at[slot, 1], c_all.at[slot]]
+        biases = [b_all.at[slot, i] for i in range(LAYERS)]
+        run_section((s_a, s_b, s_c, s_d), (v_a, v_b, v_c), w_refs, biases, lambda layer: None)
+        return 0
+
+    lax.fori_loop(0, sections, section, 0)
+    x_new[...] = renewed_fields(x_ref[...], proj_ref, s_a)
+    kept[...] = cells_in_rows((x_ref, x_new), ids_ref[0])
+    given[...] = cells_in_rows((x_ref, x_new), 1 - ids_ref[0])
 
 
 def place_kernel(share, pieces, out_ref):
@@ -482,17 +496,17 @@
     first_result = current
     kept, given = pl.pallas_call(
         second_kernel,
-        grid=(segments,),
         out_shape=(jax.ShapeDtypeStruct((128, 128), jnp.bfloat16),) * 2,
-        in_specs=[smem]
-        + [vmem] * 3
+        in_specs=[smem] + [vmem] * 3 + [anyspace] * 3,
+        out_specs=(vmem, vmem),
+        scratch_shapes=state_scratch()
         + [
-            pl.BlockSpec((1, 2, 4, 256, 384), lambda s: (s, 0, 0, 0, 0)),
-            pl.BlockSpec((1, 1024, 768), lambda s: (s, 0, 0)),
-            pl.BlockSpec((1, LAYERS, 8, 128), lambda s: (s, 0, 0, 0)),
+            pltpu.VMEM((16, 2048), jnp.float32),
+            pltpu.VMEM((2, 2, 4, 256, 384), jnp.bfloat16),
+            pltpu.VMEM((2, 1024, 768), jnp.bfloat16),
+            pltpu.VMEM((2, LAYERS, 8, 128), jnp.float32),
+            pltpu.SemaphoreType.DMA((2, 3)),
         ],
-        out_specs=(vmem, vmem),
-        scratch_shapes=state_scratch() + [pltpu.VMEM((16, 2048), jnp.float32)],
         compiler_params=params,
         cost_estimate=pl.CostEstimate(flops=segments * LAYERS * layer_flops, bytes_accessed=16 << 20, transcendentals=0),
     )(ids, first_result, lift, proj, weights, cycles, rows)

time: 117 us -> 117 us (level)
  no operation moved by 1% of the time
where the time goes in v7:
time: 117 us; the launch traced here: 116 us
  Pallas kernels  78.8 us (67%)
  starting transfers between devices  15.2 us (13%)
  blocking collectives  9.29 us (8%)
  waiting for transfers between devices  7.35 us (6%)
  local copies, waits for them, and re-layouts  5.33 us (5%)
    pallas_call x4, Pallas kernels, shards(): pl.pallas_call(functools.partial(level_kernel, level, level == levels - 1...  42.2 us
    pallas_call x1, Pallas kernels, shards(): pl.pallas_call(second_kernel, out_shape=(jax.ShapeDtypeStruct((128, 128),...  33.4 us
    ppermute x4, starting transfers between devices, hand_on(): return lax.ppermute(value, ('segment', 'slab'), pairs)  14.7 us
    all_to_all x1, blocking collectives, shards(): pieces = lax.all_to_all(pieces, 'segment', 0, 0, tiled=True)  9.29 us
    ppermute x6, waiting for transfers between devices, between_cores(): return lax.ppermute(value, 'slab', swap)  4.4 us
    unnamed x10, local copies, waits for them, and re-layouts  3.89 us
    ppermute x4, waiting for transfers between devices, hand_on(): return lax.ppermute(value, ('segment', 'slab'), pairs)  2.94 us
  transfers between devices with their start and end apart: 10, of which 4 were waited for; matrix products, arithmetic and copies ran while one was open for 1% of the time, Pallas kernels for 28%

profile of v7, /device:TPU:0, one launch (start us, length us, event | category | flops | bytes accessed | tf_op | source)
XLA Modules:
  0.0 116.4 jit_solution(9745328558643371653)
XLA Ops:
  0.0 0.0 copy-start
  0.0 1.2 copy-done
  1.2 0.7 copy-done.4
  1.9 0.5 shard_map.64.refs_1_.refs_2_
  2.4 4.3 %collective-permute-start = (bf16[3,896,128]{2,1,0:T(8,128)(2,1)S(1)}, bf16[3,896,128]{2,1,0:T(8,128)(2,1)S(1)}, u32[]{:S(2)}, u32[]{:S(2)}) collective-permute-start(bf16[3,896,128]{2,1,0:T(8,128)(2,1)S(1)} %shard_map.64.refs_1_.refs_2_), channel_id=1, source_target_pairs={{4,0},{6,2},{8,4},{10,6},{12,8},{14,10},{0,3},{2,1},{20,16},{22,18... | collective-permute-start | bytes 2064392 | tf_op jit(solution)/shard_map/ppermute | solution.py:463
  6.8 1.4 %reshape.15.kept_ref = f32[4,3,8,256]{3,2,1,0:T(8,128)S(1)} reshape(f32[4,3,8,16,16]{4,3,2,1,0:T(8,128)} %param.6) | data formatting | bytes 196608 | tf_op jit(solution)/shard_map/reshape | solution.py:440
  8.2 0.1 collective-permute-start.1
  8.3 0.1 pad_add_fusion.ids_ref.refs_0_
  8.4 1.2 %collective-permute-done.1.got_ref = f32[4,3,8,256]{3,2,1,0:T(8,128)S(1)} collective-permute-done((f32[4,3,8,256]{3,2,1,0:T(8,128)S(1)}, f32[4,3,8,256]{3,2,1,0:T(8,128)S(1)}, u32[]{:S(2)}, u32[]{:S(2)}) %collective-permute-start.1) | collective-permute-done | bytes 98336 | tf_op jit(solution)/shard_map/ppermute | solution.py:430
  9.6 0.7 copy-done.1
  10.2 0.7 copy-done.2
  10.9 0.7 copy-done.3
  11.6 1.7 %shard_map.65 = (f32[16,2048]{1,0:T(8,128)S(1)}, bf16[48,128]{1,0:T(8,128)(2,1)S(1)}, bf16[48,128]{1,0:T(8,128)(2,1)S(1)}, bf16[8,16,16,128]{3,2,1,0:T(8,128)(2,1)S(1)}) custom-call(s32[4]{0:T(128)S(1)} %pad_add_fusion.ids_ref.refs_0_, s32[4,3]{1,0:T(4,128)S(1)} %copy-done.2, f32[4,3,8,256]{3,2,1,0:T(8,128)S(1)} %reshape.15.kept_ref, ...), custom_call_target="tpu_custom_call" | custom-call | tf_op jit(solution)/shard_map/pallas_call | solution.py:442
  13.3 2.9 %collective-permute-done.refs_4_.refs_1_ = bf16[3,896,128]{2,1,0:T(8,128)(2,1)S(1)} collective-permute-done((bf16[3,896,128]{2,1,0:T(8,128)(2,1)S(1)}, bf16[3,896,128]{2,1,0:T(8,128)(2,1)S(1)}, u32[]{:S(2)}, u32[]{:S(2)}) %collective-permute-start) | collective-permute-done | bytes 688160 | tf_op jit(solution)/shard_map/ppermute | solution.py:463
  16.3 0.1 collective-permute-start.3
  16.3 3.9 %collective-permute-start.2 = (bf16[3,896,128]{2,1,0:T(8,128)(2,1)S(1)}, bf16[3,896,128]{2,1,0:T(8,128)(2,1)S(1)}, u32[]{:S(2)}, u32[]{:S(2)}) collective-permute-start(bf16[3,896,128]{2,1,0:T(8,128)(2,1)S(1)} %collective-permute-done.refs_4_.refs_1_), channel_id=1, source_target_pairs={{4,0},{6,2},{8,4},{10,6},{0,3},{2,1},{20,16},{22,18},{24,20},{26,2... | collective-permute-start | bytes 2064392 | tf_op jit(solution)/shard_map/ppermute | solution.py:463
  20.3 10.3 %shard_map.66 = (bf16[8,2,4,256,384]{4,3,2,1,0:T(8,128)(2,1)}, bf16[8,1024,768]{2,1,0:T(8,128)(2,1)}, f32[8,3,8,128]{3,2,1,0:T(8,128)S(1)}, bf16[8,16,16,128]{3,2,1,0:T(8,128)(2,1)S(1)}, f32[16,2048]{1,0:T(8,128)S(1)}) custom-call(s32[4]{0:T(128)S(1)} %pad_add_fusion.ids_ref.refs_0_, bf16[3,896,128]{2,1,0:T(8,128)(2,1)S(1)} %shard_map.64.refs_1_.refs_2_, ...), custom_call_target="tpu_custom_call" | custom-call | flops 6442450944 | bytes 4194304 | tf_op jit(solution)/shard_map/pallas_call | solution.py:473
  30.6 0.0 collective-permute-done.2.refs_4_.refs_1_
  30.6 0.1 collective-permute-start.5
  30.7 2.6 %collective-permute-start.4 = (bf16[3,896,128]{2,1,0:T(8,128)(2,1)S(1)}, bf16[3,896,128]{2,1,0:T(8,128)(2,1)S(1)}, u32[]{:S(2)}, u32[]{:S(2)}) collective-permute-start(bf16[3,896,128]{2,1,0:T(8,128)(2,1)S(1)} %collective-permute-done.2.refs_4_.refs_1_), channel_id=1, source_target_pairs={{4,0},{6,2},{0,3},{2,1},{20,16},{22,18},{16,19},{18,17}} | collective-permute-start | bytes 2064392 | tf_op jit(solution)/shard_map/ppermute | solution.py:463
  33.3 10.3 %shard_map.67 = (bf16[8,2,4,256,384]{4,3,2,1,0:T(8,128)(2,1)}, bf16[8,1024,768]{2,1,0:T(8,128)(2,1)}, f32[8,3,8,128]{3,2,1,0:T(8,128)S(1)}, bf16[8,16,16,128]{3,2,1,0:T(8,128)(2,1)S(1)}, f32[16,2048]{1,0:T(8,128)S(1)}) custom-call(s32[4]{0:T(128)S(1)} %pad_add_fusion.ids_ref.refs_0_, ...), custom_call_target="tpu_custom_call", output_to_operand_aliasing={{0}: (9, {}), {1}: (10, {}), {2}: (11, {})} | custom-call | flops 6442450944 | bytes 4194304 | tf_op jit(solution)/shard_map/pallas_call | solution.py:473
  43.6 0.1 collective-permute-start.6
  43.7 3.9 %collective-permute-start.7 = (bf16[3,896,128]{2,1,0:T(8,128)(2,1)S(1)}, bf16[3,896,128]{2,1,0:T(8,128)(2,1)S(1)}, u32[]{:S(2)}, u32[]{:S(2)}) collective-permute-start(bf16[3,896,128]{2,1,0:T(8,128)(2,1)S(1)} %collective-permute-done.4.refs_4_.refs_1_), channel_id=1, source_target_pairs={{0,3},{2,1},{16,19},{18,17}} | collective-permute-start | bytes 2064392 | tf_op jit(solution)/shard_map/ppermute | solution.py:463
  47.6 10.3 %shard_map.68 = (bf16[8,2,4,256,384]{4,3,2,1,0:T(8,128)(2,1)}, bf16[8,1024,768]{2,1,0:T(8,128)(2,1)}, f32[8,3,8,128]{3,2,1,0:T(8,128)S(1)}, bf16[8,16,16,128]{3,2,1,0:T(8,128)(2,1)S(1)}, f32[16,2048]{1,0:T(8,128)S(1)}) custom-call(s32[4]{0:T(128)S(1)} %pad_add_fusion.ids_ref.refs_0_, ...), custom_call_target="tpu_custom_call", output_to_operand_aliasing={{0}: (9, {}), {1}: (10, {}), {2}: (11, {})} | custom-call | flops 6442450944 | bytes 4194304 | tf_op jit(solution)/shard_map/pallas_call | solution.py:473
  58.0 0.1 collective-permute-start.8
  58.1 2.1 %collective-permute-done.8.refs_3_ = bf16[3,896,128]{2,1,0:T(8,128)(2,1)S(1)} collective-permute-done((bf16[3,896,128]{2,1,0:T(8,128)(2,1)S(1)}, bf16[3,896,128]{2,1,0:T(8,128)(2,1)S(1)}, u32[]{:S(2)}, u32[]{:S(2)}) %collective-permute-start.8) | collective-permute-done | bytes 688160 | tf_op jit(solution)/shard_map/ppermute | solution.py:430
  60.2 11.2 %shard_map.69 = (bf16[8,2,4,256,384]{4,3,2,1,0:T(8,128)(2,1)}, bf16[8,1024,768]{2,1,0:T(8,128)(2,1)}, f32[8,3,8,128]{3,2,1,0:T(8,128)S(1)}, bf16[8,16,16,128]{3,2,1,0:T(8,128)(2,1)}, f32[16,2048]{1,0:T(8,128)S(1)}) custom-call(s32[4]{0:T(128)S(1)} %pad_add_fusion.ids_ref.refs_0_, ...), custom_call_target="tpu_custom_call", output_to_operand_aliasing={{0}: (9, {}), {1}: (10, {}), {2}: (11, {})} | custom-call | flops 6442450944 | bytes 4194304 | tf_op jit(solution)/shard_map/pallas_call | solution.py:473
  71.4 33.4 %shard_map.70 = (bf16[128,128]{1,0:T(8,128)(2,1)S(1)}, bf16[128,128]{1,0:T(8,128)(2,1)S(1)}) custom-call(s32[4]{0:T(128)S(1)} %pad_add_fusion.ids_ref.refs_0_, f32[16,2048]{1,0:T(8,128)S(1)} %get-tuple-element.59.x_ref, bf16[48,128]{1,0:T(8,128)(2,1)S(1)} %get-tuple-element.38.refs_6_.lift_ref, bf16[48,128]{1,0:T(8,128)(2,1)S(1)} %get-tuple-element.39.refs_7_.proj_ref, ...), custom_call_target="tpu_custom_call" | custom-call | flops 25769803776 | bytes 16777216 | tf_op jit(solution)/shard_map/pallas_call | solution.py:497
  104.8 0.2 collective-permute-start.9
  105.0 1.1 collective-permute-done.9
  106.1 9.3 %all_to_all.5 = bf16[8,2,16,128]{3,2,1,0:T(8,128)(2,1)S(1)} all-to-all(bf16[8,2,16,128]{3,2,1,0:T(8,128)(2,1)S(1)} %fusion.1), channel_id=1, replica_groups=mesh['groups'=2,'segment'=8,'slab'=2] {'segment'}, dimensions={0} | all-to-all | bytes 131072 | tf_op jit(solution)/shard_map/all_to_all | solution.py:518
  115.4 1.0 shard_map.71
  (12 shorter events, 0.0 us)
Async XLA Ops:
  0.0 1.2 %copy-start = (bf16[1,3,9,64,192]{4,3,2,1,0:T(8,128)(2,1)S(1)}, bf16[1,3,9,64,192]{4,3,2,1,0:T(8,128)(2,1)}, u32[]{:S(2)}) copy-start(bf16[1,3,9,64,192]{4,3,2,1,0:T(8,128)(2,1)} %param.9) | copy-start | bytes 1990660
  1.2 0.7 copy-start.4
  2.4 13.8 %collective-permute-start = (bf16[3,896,128]{2,1,0:T(8,128)(2,1)S(1)}, bf16[3,896,128]{2,1,0:T(8,128)(2,1)S(1)}, u32[]{:S(2)}, u32[]{:S(2)}) collective-permute-start(bf16[3,896,128]{2,1,0:T(8,128)(2,1)S(1)} %shard_map.64.refs_1_.refs_2_), channel_id=1, source_target_pairs={{4,0},{6,2},{8,4},{10,6},{12,8},{14,10},{0,3},{2,1},{20,16},{22,18... | collective-permute-start | bytes 2064392 | tf_op jit(solution)/shard_map/ppermute | solution.py:463
  8.2 1.4 %collective-permute-start.1 = (f32[4,3,8,256]{3,2,1,0:T(8,128)S(1)}, f32[4,3,8,256]{3,2,1,0:T(8,128)S(1)}, u32[]{:S(2)}, u32[]{:S(2)}) collective-permute-start(f32[4,3,8,256]{3,2,1,0:T(8,128)S(1)} %reshape.15.kept_ref), channel_id=1, source_target_pairs={{0,1},{1,0},{2,3},{3,2},{4,5},{5,4},{6,7},{7,6},{8,9},{9,8},{10,11... | collective-permute-start | bytes 294920 | tf_op jit(solution)/shard_map/ppermute | solution.py:430
  9.6 0.7 copy-start.1
  10.2 0.7 copy-start.2
  10.9 0.7 copy-start.3
  16.3 4.0 %collective-permute-start.3 = (bf16[3,896,128]{2,1,0:T(8,128)(2,1)S(1)}, bf16[3,896,128]{2,1,0:T(8,128)(2,1)S(1)}, u32[]{:S(2)}, u32[]{:S(2)}) collective-permute-start(bf16[3,896,128]{2,1,0:T(8,128)(2,1)S(1)} %collective-permute-done.refs_4_.refs_1_), channel_id=1, source_target_pairs={{0,1},{1,0},{2,3},{3,2},{4,5},{5,4},{6,7},{7,6},{8,9},{9,8},{10,11... | collective-permute-start | bytes 2064392 | tf_op jit(solution)/shard_map/ppermute | solution.py:430
  16.3 14.2 %collective-permute-start.2 = (bf16[3,896,128]{2,1,0:T(8,128)(2,1)S(1)}, bf16[3,896,128]{2,1,0:T(8,128)(2,1)S(1)}, u32[]{:S(2)}, u32[]{:S(2)}) collective-permute-start(bf16[3,896,128]{2,1,0:T(8,128)(2,1)S(1)} %collective-permute-done.refs_4_.refs_1_), channel_id=1, source_target_pairs={{4,0},{6,2},{8,4},{10,6},{0,3},{2,1},{20,16},{22,18},{24,20},{26,2... | collective-permute-start | bytes 2064392 | tf_op jit(solution)/shard_map/ppermute | solution.py:463
  30.6 2.7 %collective-permute-start.5 = (bf16[3,896,128]{2,1,0:T(8,128)(2,1)S(1)}, bf16[3,896,128]{2,1,0:T(8,128)(2,1)S(1)}, u32[]{:S(2)}, u32[]{:S(2)}) collective-permute-start(bf16[3,896,128]{2,1,0:T(8,128)(2,1)S(1)} %collective-permute-done.2.refs_4_.refs_1_), channel_id=1, source_target_pairs={{0,1},{1,0},{2,3},{3,2},{4,5},{5,4},{6,7},{7,6},{8,9},{9,8},{10,11... | collective-permute-start | bytes 2064392 | tf_op jit(solution)/shard_map/ppermute | solution.py:430
  30.7 13.0 %collective-permute-start.4 = (bf16[3,896,128]{2,1,0:T(8,128)(2,1)S(1)}, bf16[3,896,128]{2,1,0:T(8,128)(2,1)S(1)}, u32[]{:S(2)}, u32[]{:S(2)}) collective-permute-start(bf16[3,896,128]{2,1,0:T(8,128)(2,1)S(1)} %collective-permute-done.2.refs_4_.refs_1_), channel_id=1, source_target_pairs={{4,0},{6,2},{0,3},{2,1},{20,16},{22,18},{16,19},{18,17}} | collective-permute-start | bytes 2064392 | tf_op jit(solution)/shard_map/ppermute | solution.py:463
  43.6 4.0 %collective-permute-start.6 = (bf16[3,896,128]{2,1,0:T(8,128)(2,1)S(1)}, bf16[3,896,128]{2,1,0:T(8,128)(2,1)S(1)}, u32[]{:S(2)}, u32[]{:S(2)}) collective-permute-start(bf16[3,896,128]{2,1,0:T(8,128)(2,1)S(1)} %collective-permute-done.4.refs_4_.refs_1_), channel_id=1, source_target_pairs={{0,1},{1,0},{2,3},{3,2},{4,5},{5,4},{6,7},{7,6},{8,9},{9,8},{10,11... | collective-permute-start | bytes 2064392 | tf_op jit(solution)/shard_map/ppermute | solution.py:430
  43.7 14.3 %collective-permute-start.7 = (bf16[3,896,128]{2,1,0:T(8,128)(2,1)S(1)}, bf16[3,896,128]{2,1,0:T(8,128)(2,1)S(1)}, u32[]{:S(2)}, u32[]{:S(2)}) collective-permute-start(bf16[3,896,128]{2,1,0:T(8,128)(2,1)S(1)} %collective-permute-done.4.refs_4_.refs_1_), channel_id=1, source_target_pairs={{0,3},{2,1},{16,19},{18,17}} | collective-permute-start | bytes 2064392 | tf_op jit(solution)/shard_map/ppermute | solution.py:463
  58.0 2.2 %collective-permute-start.8 = (bf16[3,896,128]{2,1,0:T(8,128)(2,1)S(1)}, bf16[3,896,128]{2,1,0:T(8,128)(2,1)S(1)}, u32[]{:S(2)}, u32[]{:S(2)}) collective-permute-start(bf16[3,896,128]{2,1,0:T(8,128)(2,1)S(1)} %collective-permute-done.7.refs_4_), channel_id=1, source_target_pairs={{0,1},{1,0},{2,3},{3,2},{4,5},{5,4},{6,7},{7,6},{8,9},{9,8},{10,11... | collective-permute-start | bytes 2064392 | tf_op jit(solution)/shard_map/ppermute | solution.py:430
  104.8 1.3 %collective-permute-start.9 = (bf16[128,128]{1,0:T(8,128)(2,1)S(1)}, bf16[128,128]{1,0:T(8,128)(2,1)S(1)}, u32[]{:S(2)}, u32[]{:S(2)}) collective-permute-start(bf16[128,128]{1,0:T(8,128)(2,1)S(1)} %get-tuple-element.64), channel_id=1, source_target_pairs={{0,1},{1,0},{2,3},{3,2},{4,5},{5,4},{6,7},{7,6},{8,9},{9,8},{10,11... | collective-permute-start | bytes 98312 | tf_op jit(solution)/shard_map/ppermute | solution.py:430
